TPU v7x, 32 devices: a whole 2x2x4 slice. The times are simulated.
32 devices in a mesh: row: 8 (over z, x), col: 4 (over y, core).
Axes of the slice: x: 2, y: 2, z: 4, core: 2. Of those that a mesh axis runs over, the one named last changes fastest.
Arguments:
- edge_vec: float32 [3, 256], P(None, ('row', 'col')), may hold values from -8 to 8
- edge_atoms: int32 [2, 256], P(None, ('row', 'col')), may hold values from 0 to 47
- block_weight: bfloat16 [144, 16384], replicated, may hold values from -0.5 to 0.5
- base_hamiltonian: bfloat16 [6144, 6144], P('row', 'col'), as said below
- lower_bound: float32 [1], replicated, may hold values from -50 to -40
- upper_bound: float32 [1], replicated, may hold values from 40 to 50
Outputs:
- purified: float32 [6144, 6144], P('row', 'col')
Inputs may be any that keep to these rules, and one draw needn't show every extreme that they name: `base_hamiltonian`: symmetric.
All inputs are finite; a program needn't handle non-finite values.
Results may differ from a plain program's by a relative error of at most 0.0031.
Values may be sent and summed in bfloat16 or wider, within the bound.
No kernel may reach another device: no remote copies, remote signals or barrier semaphores. Data moves between devices by JAX's collectives and lax.ppermute only.
A program may use at most 192 MiB of HBM per device.

v0:
```python
import jax
import jax.numpy as jnp
from jax import lax
from jax.sharding import PartitionSpec as P

ORB = 128
NR = 16
RB = 6


def features(edge_vec):
    squared = jnp.sum(edge_vec * edge_vec, axis=0)
    radius = jnp.sqrt(squared + 0.25)
    unit_x = edge_vec[0] / radius
    unit_y = edge_vec[1] / radius
    unit_z = edge_vec[2] / radius
    harmonics = jnp.stack(
        [
            jnp.ones_like(unit_x),
            unit_x,
            unit_y,
            unit_z,
            unit_x * unit_y,
            unit_y * unit_z,
            unit_z * unit_x,
            unit_x * unit_x - unit_y * unit_y,
            3.0 * unit_z * unit_z - 1.0,
        ]
    )
    centers = 1.0 + 0.3 * jnp.arange(NR, dtype=jnp.float32)
    radial = jnp.exp(-jnp.square((radius[None, :] - centers[:, None]) / 0.5))
    return (radial[:, None, :] * harmonics[None, :, :]).reshape(NR * 9, edge_vec.shape[1])


def shards(edge_vec, edge_atoms, block_weight, base_hamiltonian, lower_bound, upper_bound):
    atoms_float = edge_atoms.astype(jnp.float32)
    packed = jnp.concatenate([features(edge_vec), atoms_float], axis=0)
    gathered = lax.all_gather(packed, ("row", "col"), axis=1, tiled=True)
    embedding = gathered[:-2]
    atom_pairs = gathered[-2:].astype(jnp.int32)
    first_atom = atom_pairs[0]
    second_atom = atom_pairs[1]
    atoms_total = RB * lax.axis_size("row")
    col_blocks = atoms_total // lax.axis_size("col")
    row_index = lax.axis_index("row")
    col_index = lax.axis_index("col")
    row_atoms = row_index * RB + jnp.arange(RB, dtype=jnp.int32)
    col_atoms = col_index * col_blocks + jnp.arange(col_blocks, dtype=jnp.int32)
    direct = (
        (
            (first_atom[None, None, :] == row_atoms[:, None, None])
            & (second_atom[None, None, :] == col_atoms[None, :, None])
        )
        .astype(jnp.float32)
        .reshape(RB * col_blocks, -1)
    )
    mirror = (
        (
            (first_atom[None, None, :] == col_atoms[None, :, None])
            & (second_atom[None, None, :] == row_atoms[:, None, None])
        )
        .astype(jnp.float32)
        .reshape(RB * col_blocks, -1)
    )
    contract = (((1,), (1,)), ((), ()))
    coefficient = lax.dot_general(
        direct, embedding, contract, precision=lax.Precision.HIGHEST
    ).astype(jnp.bfloat16)
    coefficient_back = lax.dot_general(
        mirror, embedding, contract, precision=lax.Precision.HIGHEST
    ).astype(jnp.bfloat16)
    blocks = jnp.dot(coefficient, block_weight, preferred_element_type=jnp.float32).reshape(
        RB, col_blocks, ORB, ORB
    )
    blocks_back = jnp.dot(
        coefficient_back, block_weight, preferred_element_type=jnp.float32
    ).reshape(RB, col_blocks, ORB, ORB)
    tile_rows = RB * ORB
    tile_cols = col_blocks * ORB
    hamiltonian = (
        (blocks + blocks_back.transpose(0, 1, 3, 2))
        .transpose(0, 2, 1, 3)
        .reshape(tile_rows, tile_cols)
    )
    hamiltonian = hamiltonian + base_hamiltonian.astype(jnp.float32)
    global_rows = row_index * tile_rows + jnp.arange(tile_rows, dtype=jnp.int32)
    global_cols = col_index * tile_cols + jnp.arange(tile_cols, dtype=jnp.int32)
    diagonal_mask = global_rows[:, None] == global_cols[None, :]
    shifted = jnp.where(diagonal_mask, upper_bound[0], jnp.float32(0.0)) - hamiltonian
    start_density = (shifted / (upper_bound[0] - lower_bound[0])).astype(jnp.bfloat16)
    row_strip = lax.all_gather(start_density, "col", axis=1, tiled=True)
    return jnp.dot(
        row_strip,
        lax.all_gather(start_density, "row", axis=0, tiled=True),
        preferred_element_type=jnp.float32,
    )


def solution(mesh):
    return jax.shard_map(
        shards,
        mesh=mesh,
        in_specs=(P(None, ("row", "col")), P(None, ("row", "col")), P(), P("row", "col"), P(), P()),
        out_specs=P("row", "col"),
        check_vma=False,
    )
```

profile of v0, /device:TPU:4, one launch (start us, length us, event | category | flops | bytes accessed | tf_op | source)
XLA Modules:
  0.0 535.5 jit_solution(13599194972269937933)
XLA Ops:
  6.5 0.0 all-gather.3.cloned.1.call-start
  6.5 0.7 multiply_reduce_fusion
  7.3 0.8 multiply_subtract_fusion
  9.4 0.8 fusion.6
  10.2 0.1 copy.13
  10.3 0.8 copy.14
  11.1 0.1 negate_exponential_fusion
  11.2 0.1 broadcast_multiply_fusion
  11.3 0.1 mul.81
  11.3 0.1 pad_maximum_fusion
  11.4 37.9 %all_gather.9 = f32[146,256]{0,1:T(8,128)S(1)} all-gather(f32[146,8]{0,1:T(8,128)S(1)} %pad_maximum_fusion), channel_id=1, replica_groups=mesh['row'=8,'col'=4] {'row','col'}, dimensions={1}, use_global_device_ids=true | all-gather | bytes 154176 | tf_op jit(solution)/shard_map/all_gather | solution.py:38
  49.3 0.1 slice_convert_fusion
  49.4 0.2 slice_reduce_fusion.1
  49.6 0.1 broadcast_compare_fusion.3
  49.7 0.1 broadcast_compare_fusion.1
  49.8 0.2 convolution_convert_fusion
  50.1 0.0 slice-start
  50.1 0.2 convolution_convert_fusion.1
  50.3 0.0 slice-start.1
  50.3 3.3 convolution_bitcast_fusion.1
  53.6 3.1 copy.17
  56.6 0.0 slice-done
  56.6 0.0 slice-done.1
  56.7 0.8 convolution_bitcast_fusion
  57.4 3.0 copy.18
  60.4 6.6 %copy.15 = f32[6,12,128,128]{2,1,3,0:T(8,128)} copy(f32[6,12,128,128]{3,2,1,0:T(8,128)} %bitcast.52) | data formatting | bytes 9437184 | tf_op jit(solution)/shard_map/reshape | solution.py:77
  67.0 0.0 copy-start
  67.0 7.3 %bitcast_add_fusion = f32[6,12,128,128]{3,1,2,0:T(8,128)S(1)} fusion(f32[6,12,128,128]{2,1,3,0:T(8,128)} %copy.15, f32[6,12,128,128]{3,2,1,0:T(8,128)} %bitcast.51), kind=kLoop, calls=%fused_computation | loop fusion | flops 1179648 | bytes 14155776 | tf_op jit(solution)/shard_map/add | solution.py:81
  74.3 0.0 copy-done
  74.3 4.2 fusion.2
  78.5 0.0 all-gather.3.cloned.1.call-update
  78.5 0.2 all-gather.5.cloned.1.call-start
  78.8 0.5 all-gather.5.cloned.1.call-update
  79.3 63.2 %all-gather.3.cloned.1.call-done = bf16[768,6144]{1,0:T(8,128)(2,1)} async-done(((bf16[768,1536]{1,0:T(8,128)(2,1)}), bf16[768,6144]{1,0:T(8,128)(2,1)}) %all-gather.3.cloned.1.call-update) | async-done | bytes 9437200 | tf_op jit(solution)/shard_map/all_gather | solution.py:91
  142.5 365.2 %all-gather.5.cloned.1.call-done = bf16[6144,1536]{1,0:T(8,128)(2,1)} async-done(((bf16[768,1536]{1,0:T(8,128)(2,1)}), bf16[6144,1536]{1,0:T(8,128)(2,1)}) %all-gather.5.cloned.1.call-update) | async-done | bytes 18874384 | tf_op jit(solution)/shard_map/all_gather | solution.py:94
  507.6 21.0 %fusion.8 = f32[768,1536]{1,0:T(8,128)} fusion(bf16[768,6144]{1,0:T(8,128)(2,1)} %all-gather.3.cloned.1.call-done, bf16[6144,1536]{1,0:T(8,128)(2,1)} %all-gather.5.cloned.1.call-done), kind=kOutput, calls=%fused_computation.42 | convolution fusion | flops 14495514624 | bytes 33030144 | tf_op jit(solution)/shard_map/dot_general | solution.py:92
  (14 shorter events, 0.2 us)
Async XLA Ops:
  6.5 135.9 %all-gather.3.cloned.1.call-start = ((), (), s32[]{:S(2)}) async-start(), calls=%async_computation | async-start | bytes 11796480 | tf_op jit(solution)/shard_map/all_gather | solution.py:91
  50.1 6.6 %slice-start = ((s8[4718592]{0:T(1024)(128)(4,1)}), s8[4194304]{0:T(1024)(128)(4,1)S(1)}, s32[]{:S(2)}) async-start(s8[4718592]{0:T(1024)(128)(4,1)} %bitcast.49), calls=%async_computation.2 | async-start | bytes 8388608
  50.3 6.3 %slice-start.1 = ((s8[4718592]{0:T(1024)(128)(4,1)}), s8[524288]{0:T(1024)(128)(4,1)S(1)}, s32[]{:S(2)}) async-start(s8[4718592]{0:T(1024)(128)(4,1)} %bitcast.49), calls=%async_computation.3 | async-start | bytes 1048576
  67.0 7.3 %copy-start = (bf16[768,1536]{1,0:T(8,128)(2,1)S(1)}, bf16[768,1536]{1,0:T(8,128)(2,1)}, u32[]{:S(2)}) copy-start(bf16[768,1536]{1,0:T(8,128)(2,1)} %param.9) | copy-start | bytes 7077892
  78.5 429.1 %all-gather.5.cloned.1.call-start = ((), (), s32[]{:S(2)}) async-start(), calls=%async_computation.1 | async-start | bytes 21233664 | tf_op jit(solution)/shard_map/all_gather | solution.py:94
Sparse Core Ops, SparseCore 0:
  78.7 63.7 all-gather.2
  144.0 363.6 all-gather.4
where the time goes:
time: 537 us; the launch traced here: 536 us
  waiting for transfers between devices  429 us (80%)
  blocking collectives  37.9 us (7%)
  matrix products  25.6 us (5%)
  between operations  14.8 us (3%)
  other arithmetic  14.3 us (3%)
  local copies, waits for them, and re-layouts  13.9 us (3%)
    all_gather x1, waiting for transfers between devices, shards(): lax.all_gather(start_density, 'row', axis=0, tiled=True)  365 us
    all_gather x1, waiting for transfers between devices, shards(): row_strip = lax.all_gather(start_density, 'col', axis=1, tiled=True)  63.2 us
    all_gather x1, blocking collectives, shards(): gathered = lax.all_gather(packed, ('row', 'col'), axis=1, tiled=True)  37.9 us
    dot_general x1, matrix products, shards(): jnp.dot(row_strip, lax.all_gather(start_density, 'row', axis=0, tiled=Tru...  21 us
  transfers between devices with their start and end apart: 2, of which 2 were waited for; matrix products, arithmetic and copies ran while one was open for 0% of the time, Pallas kernels for 0%

commit v1 on v0

v1 whole, which is shorter than its diff:
```python
import functools

import jax
import jax.numpy as jnp
from jax import lax
from jax.experimental import pallas as pl
from jax.experimental.pallas import tpu as pltpu
from jax.sharding import PartitionSpec as P

ORB = 128
NR = 16
AXES = ("row", "col")
VMEM_BYTES = 60 * 1024 * 1024
EDGE_CHUNK = 256


def features(edge_vec):
    squared = jnp.sum(edge_vec * edge_vec, axis=0)
    radius = jnp.sqrt(squared + 0.25)
    unit_x = edge_vec[0] / radius
    unit_y = edge_vec[1] / radius
    unit_z = edge_vec[2] / radius
    harmonics = jnp.stack(
        [
            jnp.ones_like(unit_x),
            unit_x,
            unit_y,
            unit_z,
            unit_x * unit_y,
            unit_y * unit_z,
            unit_z * unit_x,
            unit_x * unit_x - unit_y * unit_y,
            3.0 * unit_z * unit_z - 1.0,
        ]
    )
    centers = 1.0 + 0.3 * jnp.arange(NR, dtype=jnp.float32)
    radial = jnp.exp(-jnp.square((radius[None, :] - centers[:, None]) / 0.5))
    return (radial[:, None, :] * harmonics[None, :, :]).reshape(NR * 9, edge_vec.shape[1])


def gather_edges(packed, devices):
    current = packed
    bit = 1
    while bit < devices:
        arrived = lax.ppermute(current, AXES, [(d, d ^ bit) for d in range(devices)])
        current = jnp.concatenate([current, arrived], axis=1)
        bit *= 2
    return current


def correction_kernel(edges, chunks, atoms, corner, scale, coefficient, weight, out, blocks):
    strip = pl.program_id(0)
    chunk = pl.program_id(1)
    size = edges // chunks
    rows, cols = out.shape[1:]

    @pl.when((strip == 0) | (chunks > 1))
    def _():
        coef = coefficient[...]

        def expand(i, _):
            at = pl.multiple_of(i * ORB, ORB)
            blocks[pl.ds(i, size, stride=ORB), :] = jnp.dot(
                coef, weight[:, pl.ds(at, ORB)], preferred_element_type=jnp.float32
            )
            return 0

        lax.fori_loop(0, ORB, expand, 0)

    row_atom = corner[0, strip]
    col_atom = corner[1, strip]
    inverse = scale[1]

    @pl.when(chunk == 0)
    def _():
        def fill(i, _):
            at = pl.multiple_of(i * ORB, ORB)
            row_ids = row_atom * ORB + at + lax.broadcasted_iota(jnp.int32, (ORB, cols), 0)
            col_ids = col_atom * ORB + lax.broadcasted_iota(jnp.int32, (ORB, cols), 1)
            out[0, pl.ds(at, ORB), :] = jnp.where(row_ids == col_ids, scale[0], jnp.float32(0.0))
            return 0

        lax.fori_loop(0, rows // ORB, fill, 0)

    def scatter(e, _):
        first = atoms[0, chunk * size + e]
        second = atoms[1, chunk * size + e]
        at = pl.multiple_of(e * ORB, ORB)
        direct_row, direct_col = first - row_atom, second - col_atom
        mirror_row, mirror_col = second - row_atom, first - col_atom

        def inside(row, col):
            return (row >= 0) & (row < rows // ORB) & (col >= 0) & (col < cols // ORB) & (first >= 0)

        @pl.when(inside(direct_row, direct_col))
        def _():
            spot = (
                0,
                pl.ds(pl.multiple_of(direct_row * ORB, ORB), ORB),
                pl.ds(pl.multiple_of(direct_col * ORB, ORB), ORB),
            )
            out[spot] = out[spot] - blocks[pl.ds(at, ORB), :] * inverse

        @pl.when(inside(mirror_row, mirror_col))
        def _():
            spot = (
                0,
                pl.ds(pl.multiple_of(mirror_row * ORB, ORB), ORB),
                pl.ds(pl.multiple_of(mirror_col * ORB, ORB), ORB),
            )
            out[spot] = out[spot] - blocks[pl.ds(at, ORB), :].T * inverse

        return 0

    lax.fori_loop(0, size, scatter, 0)


def corrections(atoms, corner, scale, coefficient, weight, tile):
    edges, feat = coefficient.shape
    chunks = max(1, edges // EDGE_CHUNK)
    strips = corner.shape[1]
    return pl.pallas_call(
        functools.partial(correction_kernel, edges, chunks),
        out_shape=jax.ShapeDtypeStruct((strips,) + tile, jnp.float32),
        grid=(strips, chunks),
        in_specs=[
            pl.BlockSpec(memory_space=pltpu.SMEM),
            pl.BlockSpec(memory_space=pltpu.SMEM),
            pl.BlockSpec(memory_space=pltpu.SMEM),
            pl.BlockSpec((edges // chunks, feat), lambda s, c: (c, 0)),
            pl.BlockSpec(weight.shape, lambda s, c: (0, 0)),
        ],
        out_specs=pl.BlockSpec((1,) + tile, lambda s, c: (s, 0, 0)),
        scratch_shapes=[pltpu.VMEM((edges // chunks * ORB, ORB), jnp.float32)],
        compiler_params=pltpu.CompilerParams(vmem_limit_bytes=VMEM_BYTES),
    )(atoms, corner, scale, coefficient, weight)


def shards(row_size, col_size, edge_vec, edge_atoms, block_weight, base, lower_bound, upper_bound):
    devices = row_size * col_size
    half_rows = row_size // 2
    half_cols = col_size // 2
    tile_rows, tile_cols = base.shape
    cells = tile_cols // tile_rows
    row_atoms, col_atoms = tile_rows // ORB, tile_cols // ORB
    row = lax.axis_index("row")
    col = lax.axis_index("col")
    row_half, row_in = row // half_rows, row % half_rows
    col_half, col_in = col // half_cols, col % half_cols
    on_diagonal = row_half == col_half

    def moves(where):
        pairs = []
        for r in range(row_size):
            for c in range(col_size):
                to = where(r // half_rows, r % half_rows, c // half_cols, c % half_cols)
                if to is not None:
                    h, i, y, k = to
                    pairs.append((r * col_size + c, (h * half_rows + i) * col_size + y * half_cols + k))
        return pairs

    def send(value, where):
        return lax.ppermute(value, AXES, moves(where))

    packed = jnp.concatenate([edge_vec, edge_atoms.astype(jnp.float32)], axis=0)
    everyone = gather_edges(packed, devices)
    base, everyone = lax.optimization_barrier((base, everyone))

    strips = {0: base}
    for mask in range(1, half_rows):
        bits = [1 << b for b in range(half_rows.bit_length()) if mask >> b & 1]
        if len(bits) == 1:
            strips[mask] = send(base, lambda h, i, y, k: (h, i ^ mask, y, k))
            continue
        width = tile_cols // len(bits)
        parts = []
        for at, bit in enumerate(bits):
            piece = strips[mask ^ bit][:, at * width : (at + 1) * width]
            parts.append(send(piece, lambda h, i, y, k: (h, i ^ bit, y, k)))
        strips[mask] = jnp.concatenate(parts, axis=1)
    from_diagonal = send(base, lambda h, i, y, k: (h, i, 1 - y, k) if h == y else None)
    mine = jnp.where(on_diagonal, base, from_diagonal)
    tiles = {0: mine}
    for mask in range(1, half_cols):
        tiles[mask] = send(mine, lambda h, i, y, k: (h, i, y, k ^ mask))

    embedding = features(everyone[:3])
    pair_atoms = everyone[3:].astype(jnp.int32)
    atoms_total = row_atoms * row_size
    position = pair_atoms[0] * atoms_total + pair_atoms[1]
    same = position[:, None] == position[None, :]
    edges = position.shape[0]
    order = jnp.arange(edges, dtype=jnp.int32)
    earlier = jnp.any(same & (order[None, :] < order[:, None]), axis=1)
    coefficient = lax.dot_general(
        same.astype(jnp.float32), embedding, (((1,), (1,)), ((), ())), precision=lax.Precision.HIGHEST
    ).astype(jnp.bfloat16)
    pair_atoms = jnp.where(earlier[None, :], jnp.int32(-1), pair_atoms)
    span = upper_bound[0] - lower_bound[0]
    scale = jnp.stack([upper_bound[0] / span, 1.0 / span])
    corner_rows = jnp.concatenate(
        [
            (row_half * half_rows + jnp.arange(half_rows, dtype=jnp.int32)) * row_atoms,
            jnp.broadcast_to(row * row_atoms, (half_cols,)),
        ]
    )
    corner_cols = jnp.concatenate(
        [
            jnp.broadcast_to(col * col_atoms, (half_rows,)),
            (row_half * half_cols + jnp.arange(half_cols, dtype=jnp.int32)) * col_atoms,
        ]
    )
    corner = jnp.stack([corner_rows, corner_cols]).astype(jnp.int32)
    correction = corrections(pair_atoms, corner, scale, coefficient, block_weight, base.shape)

    def density(tile, corrected):
        return (corrected - tile.astype(jnp.float32) * scale[1]).astype(jnp.bfloat16)

    tall = jnp.zeros((half_rows, tile_rows, tile_cols), jnp.bfloat16)
    for mask in range(half_rows):
        at = row_in ^ mask
        value = density(strips[mask], lax.dynamic_index_in_dim(correction, at, 0, keepdims=False))
        tall = lax.dynamic_update_index_in_dim(tall, value, at, 0)
    tall = tall.reshape(half_rows * tile_rows, tile_cols)
    wide = jnp.zeros((tile_rows, half_cols * tile_cols), jnp.bfloat16)
    for mask in range(half_cols):
        at = col_in ^ mask
        value = density(tiles[mask], lax.dynamic_index_in_dim(correction, half_rows + at, 0, keepdims=False))
        wide = lax.dynamic_update_slice(wide, value, (0, at * tile_cols))

    near = jnp.dot(wide, tall, preferred_element_type=jnp.float32)
    total = near

    own = density(base, lax.dynamic_index_in_dim(correction, row_in, 0, keepdims=False))
    square = lax.dot_general(own, tall, (((1,), (1,)), ((), ())), preferred_element_type=jnp.float32)

    def columns_of(value, k):
        return lax.dynamic_slice(value, (0, k * tile_cols), (tile_rows, tile_cols))

    summed = columns_of(square, col_in)
    for mask in range(1, half_cols):
        part = columns_of(square, col_in ^ mask).astype(jnp.bfloat16)
        summed = summed + send(part, lambda h, i, y, k: (h, i, y, k ^ mask)).astype(jnp.float32)
    total = total + send(
        summed.astype(jnp.bfloat16), lambda h, i, y, k: (h, i, 1 - y, k) if h != y else None
    ).astype(jnp.float32)

    for turn in range(cells):
        slot = (row_in + turn) % cells
        cell = lax.dynamic_slice(near, (0, slot * tile_rows), (tile_rows, tile_rows)).astype(jnp.bfloat16)

        def opposite(h, i, y, k):
            return (1 - h, k * cells + (i + turn) % cells, h, i // cells)

        if turn % 2 == 0:
            arrived = send(cell, lambda h, i, y, k: opposite(h, i, y, k) if h != y else None)
        else:
            def relay(h, i, y, k):
                to = opposite(h, i, y, k)
                return (to[0], to[1], y, to[3])

            arrived = send(cell, lambda h, i, y, k: relay(h, i, y, k) if h != y else None)
            arrived = send(arrived, lambda h, i, y, k: (h, i, 1 - y, k) if h == y else None)
        spot = (row_in - turn) % cells
        spread = jnp.concatenate(
            [jnp.where(spot == s, arrived.T, jnp.zeros_like(arrived)) for s in range(cells)], axis=1
        )
        total = total + spread.astype(jnp.float32)
    return total


def solution(mesh):
    return jax.shard_map(
        functools.partial(shards, mesh.shape["row"], mesh.shape["col"]),
        mesh=mesh,
        in_specs=(P(None, AXES), P(None, AXES), P(), P("row", "col"), P(), P()),
        out_specs=P("row", "col"),
        check_vma=False,
    )
```

time: 537 us -> 338 us (0.63)
  the two profiles are of different devices: /device:TPU:4 before, /device:TPU:16 now
where the time goes in v1:
time: 338 us; the launch traced here: 337 us
  waiting for transfers between devices  112 us (33%)
  Pallas kernels  93.4 us (28%)
  other arithmetic  46.8 us (14%)
  local copies, waits for them, and re-layouts  32.9 us (10%)
  starting transfers between devices  25.6 us (8%)
  matrix products  24.9 us (7%)
    ppermute x11, waiting for transfers between devices, send(): return lax.ppermute(value, AXES, moves(where))  101 us
    pallas_call x1, Pallas kernels, corrections(): pl.pallas_call(functools.partial(correction_kernel, edges, chunks), out_s...  93.4 us
    ppermute x11, starting transfers between devices, send(): return lax.ppermute(value, AXES, moves(where))  21 us
    dynamic_update_slice x4, other arithmetic, shards(): tall = lax.dynamic_update_index_in_dim(tall, value, at, 0)  19.9 us
    dot_general x1, matrix products, shards(): lax.dot_general(own, tall, (((1,), (1,)), ((), ())), preferred_element_ty...  13.1 us
    dot_general x1, matrix products, shards(): near = jnp.dot(wide, tall, preferred_element_type=jnp.float32)  11.4 us
    dynamic_update_slice x2, other arithmetic, shards(): wide = lax.dynamic_update_slice(wide, value, (0, at * tile_cols))  10.7 us
    ppermute x5, waiting for transfers between devices, gather_edges(): lax.ppermute(current, AXES, [(d, d ^ bit) for d in range(devices)])  10.7 us
  transfers between devices with their start and end apart: 16, of which 9 were waited for; matrix products, arithmetic and copies ran while one was open for 26% of the time, Pallas kernels for 28%

profile of v1, /device:TPU:16, one launch (start us, length us, event | category | flops | bytes accessed | tf_op | source)
XLA Modules:
  0.0 337.0 jit_solution(10418285443926554139)
XLA Ops:
  0.0 0.7 convert_element_type.80
  0.7 0.7 pad_maximum_fusion
  3.5 0.7 pad_maximum_fusion.4.scale
  4.2 0.8 pad_maximum_fusion.1
  4.9 1.5 collective-permute-start.1
  6.4 2.1 collective-permute-done.1
  8.5 0.8 pad_maximum_fusion.2
  9.3 1.5 collective-permute-start.2
  10.8 2.1 collective-permute-done.2
  12.9 0.8 pad_maximum_fusion.3
  13.7 1.6 collective-permute-start.3
  15.2 2.0 collective-permute-done.3
  17.5 4.4 %collective-permute-done.4 = f32[5,128]{1,0:T(8,128)S(1)} collective-permute-done((f32[5,128]{1,0:T(8,128)S(1)}, f32[5,128]{1,0:T(8,128)S(1)}, u32[]{:S(2)}, u32[]{:S(2)}) %collective-permute-start.4) | collective-permute-done | bytes 2592 | tf_op jit(solution)/shard_map/ppermute | solution.py:45
  22.0 1.5 collective-permute-start.7
  23.5 1.6 collective-permute-start.8
  25.1 1.3 collective-permute-start.5
  27.1 0.8 copy.22.coefficient
  28.6 93.4 %shard_map.64 = f32[6,768,1536]{2,1,0:T(8,128)} custom-call(s32[2,256]{1,0:T(2,128)} %broadcast_select_fusion.1.atoms, s32[2,6]{1,0:T(2,128)} %pad_add_fusion.corner, f32[2]{0:T(128)} %pad_maximum_fusion.4.scale, bf16[256,144]{1,0:T(8,128)(2,1)} %copy.22.coefficient, bf16[144,16384]{1,0:T(8,128)(2,1)} %weight.1), custom_call_target="tpu_custom_call" | custom-call | tf_op jit(solution)/shard_map/pallas_call | solution.py:122
  122.0 5.5 %broadcast_in_dim.43 = bf16[4,768,1536]{2,1,0:T(8,128)(2,1)} broadcast(bf16[]{:T(256)} %constant.112.clone.1), dimensions={} | broadcast | bytes 9437186 | tf_op jit(solution)/shard_map/broadcast_in_dim | solution.py:219
  127.6 6.3 %bitcast_dynamic-update-slice_fusion = (bf16[4,768,1536]{2,1,0:T(8,128)(2,1)}, bf16[768,1536]{1,0:T(8,128)(2,1)}) fusion(bf16[4,768,1536]{2,1,0:T(8,128)(2,1)} %broadcast_in_dim.43, s32[]{:T(128)S(6)} %select_n.141, f32[]{:T(128)} %div.58, bf16[768,1536]{1,0:T(8,128)(2,1)} %param.9, f32[6,768,1536]{2,1,0:T(8,128)} %shard_map.64, s32[]{:T(128)S(6)} %select_n.140), kind=kLoop, calls=%fused_computation.21 | loop fusion | flops 4718592 | bytes 11797000 | tf_op jit(solution)/shard_map/jit(dynamic_update_index_in_dim)/dynamic_update_slice | solution.py:223
  133.9 2.5 slice.41
  136.6 2.4 slice.42
  139.0 0.6 collective-permute-start.10
  139.7 2.8 broadcast_in_dim.40
  142.4 6.6 %fusion.6 = (bf16[768,3072]{1,0:T(8,128)(2,1)}, bf16[768,1536]{1,0:T(8,128)(2,1)}) fusion(bf16[768,3072]{1,0:T(8,128)(2,1)} %broadcast_in_dim.40, s32[]{:T(128)S(6)} %select_n.136, f32[6,768,1536]{2,1,0:T(8,128)} %shard_map.64, s32[]{:T(128)S(6)} %select_n.132, f32[]{:T(128)} %div.58, bf16[768,1536]{1,0:T(8,128)(2,1)} %param.9, ...), kind=kLoop, calls=%fused_computation.15 | loop fusion | flops 5898240 | bytes 14156297 | tf_op jit(solution)/shard_map/dynamic_update_slice | solution.py:229
  149.1 5.4 %fusion.9 = bf16[4,768,1536]{2,1,0:T(8,128)(2,1)} fusion(bf16[4,768,1536]{2,1,0:T(8,128)(2,1)} %get-tuple-element.9, s32[]{:T(128)S(6)} %select_n.143, bf16[768,1536]{1,0:T(8,128)(2,1)} %collective-permute-done.7, f32[6,768,1536]{2,1,0:T(8,128)} %shard_map.64, s32[]{:T(128)S(6)} %select_n.142, f32[]{:T(128)} %div.58), kind=kLoop, calls=%fused_computation.18 | loop fusion | flops 4718592 | bytes 9437704 | tf_op jit(solution)/shard_map/jit(dynamic_update_index_in_dim)/dynamic_update_slice | solution.py:223
  154.6 4.1 %fusion.11 = bf16[4,768,1536]{2,1,0:T(8,128)(2,1)} fusion(bf16[4,768,1536]{2,1,0:T(8,128)(2,1)} %fusion.9, s32[]{:T(128)S(6)} %select_n.145, bf16[768,1536]{1,0:T(8,128)(2,1)} %collective-permute-done.8, f32[6,768,1536]{2,1,0:T(8,128)S(1)} %bitcast.74, s32[]{:T(128)S(6)} %select_n.144, f32[]{:T(128)} %div.58), kind=kLoop, calls=%fused_computation.20 | loop fusion | flops 4718592 | bytes 9437704 | tf_op jit(solution)/shard_map/jit(dynamic_update_index_in_dim)/dynamic_update_slice | solution.py:223
  158.6 0.7 collective-permute-done.9
  159.3 2.5 collective-permute-done.10
  161.8 4.1 %fusion.5 = bf16[4,768,1536]{2,1,0:T(8,128)(2,1)} fusion(bf16[4,768,1536]{2,1,0:T(8,128)(2,1)} %fusion.11, s32[]{:T(128)S(6)} %select_n.147, f32[6,768,1536]{2,1,0:T(8,128)S(1)} %bitcast.74, s32[]{:T(128)S(6)} %select_n.146, bf16[1,768,768]{2,1,0:T(8,128)(2,1)} %bitcast.18, bf16[1,768,768]{2,1,0:T(8,128)(2,1)} %bitcast.17, f32[]{:T(128)} %div.58), kind=kLoop, calls=%fused_computation.14 | loop fusion | flops 8257536 | bytes 9437704 | tf_op jit(solution)/shard_map/jit(dynamic_update_index_in_dim)/dynamic_update_slice | solution.py:223
  165.8 13.1 %fusion.21 = f32[768,3072]{0,1:T(8,128)} fusion(bf16[768,1536]{1,0:T(8,128)(2,1)} %get-tuple-element.10, bf16[3072,1536]{1,0:T(8,128)(2,1)} %bitcast.75), kind=kOutput, calls=%fused_computation.68 | convolution fusion | flops 7247757312 | bytes 21233664 | tf_op jit(solution)/shard_map/dot_general | solution.py:235
  178.9 4.0 %dynamic-slice_convert_fusion = bf16[768,1536]{0,1:T(8,128)(2,1)} fusion(f32[768,3072]{0,1:T(8,128)} %fusion.21, s32[]{:T(128)S(6)} %select_n.138), kind=kLoop, calls=%fused_computation.12 | loop fusion | bytes 4718596 | tf_op jit(solution)/shard_map/convert_element_type | solution.py:242
  182.9 4.1 %fusion.7 = bf16[768,3072]{1,0:T(8,128)(2,1)} fusion(bf16[768,3072]{1,0:T(8,128)(2,1)} %get-tuple-element.11, s32[]{:T(128)S(6)} %select_n.138, bf16[768,1536]{1,0:T(8,128)(2,1)} %collective-permute-done.6, f32[6,768,1536]{2,1,0:T(8,128)S(1)} %bitcast.74, s32[]{:T(128)S(6)} %select_n.137, f32[]{:T(128)} %div.58), kind=kLoop, calls=%fused_computation.16 | loop fusion | flops 4718592 | bytes 9437704 | tf_op jit(solution)/shard_map/dynamic_update_slice | solution.py:229
  187.0 11.4 %fusion.20 = f32[768,1536]{1,0:T(8,128)S(1)} fusion(bf16[768,3072]{1,0:T(8,128)(2,1)} %fusion.7, bf16[3072,1536]{1,0:T(8,128)(2,1)} %bitcast.76), kind=kOutput, calls=%fused_computation.67 | convolution fusion | flops 7247757312 | bytes 18874368 | tf_op jit(solution)/shard_map/dot_general | solution.py:231
  198.4 2.2 copy-done.1
  200.9 8.3 %collective-permute-start.14 = (bf16[768,768]{1,0:T(8,128)(2,1)S(1)}, bf16[768,768]{1,0:T(8,128)(2,1)}, u32[]{:S(2)}, u32[]{:S(2)}) collective-permute-start(bf16[768,768]{1,0:T(8,128)(2,1)S(1)} %get-tuple-element.20), channel_id=1, source_target_pairs={{2,22},{3,30},{6,18},{7,26},{10,23},{11,31},{14,19},{15,27},{16,4}... | collective-permute-start | bytes 3538952 | tf_op jit(solution)/shard_map/ppermute | solution.py:163
  209.2 3.6 %add_convert_fusion = bf16[768,1536]{0,1:T(8,128)(2,1)S(1)} fusion(bf16[768,1536]{0,1:T(8,128)(2,1)} %collective-permute-done.11, f32[768,3072]{0,1:T(8,128)} %fusion.21, s32[]{:T(128)S(6)} %select_n.136), kind=kLoop, calls=%fused_computation.11 | loop fusion | flops 3538944 | bytes 9437188 | tf_op jit(solution)/shard_map/convert_element_type | solution.py:245
  212.8 2.7 collective-permute-start.12
  215.5 3.4 %collective-permute-start.13 = (bf16[768,768]{1,0:T(8,128)(2,1)S(1)}, bf16[768,768]{1,0:T(8,128)(2,1)}, u32[]{:S(2)}, u32[]{:S(2)}) collective-permute-start(bf16[768,768]{1,0:T(8,128)(2,1)S(1)} %get-tuple-element.21), channel_id=1, source_target_pairs={{2,16},{3,24},{6,20},{7,28},{10,17},{11,25},{14,21},{15,29},{16,2}... | collective-permute-start | bytes 3538952 | tf_op jit(solution)/shard_map/ppermute | solution.py:163
  219.0 65.6 %collective-permute-done.14 = bf16[768,768]{1,0:T(8,128)(2,1)} collective-permute-done((bf16[768,768]{1,0:T(8,128)(2,1)S(1)}, bf16[768,768]{1,0:T(8,128)(2,1)}, u32[]{:S(2)}, u32[]{:S(2)}) %collective-permute-start.14) | collective-permute-done | bytes 1179680 | tf_op jit(solution)/shard_map/ppermute | solution.py:163
  284.6 1.3 collective-permute-start.15
  285.9 6.1 %copy.25 = f32[768,1536]{0,1:T(8,128)} copy(f32[768,1536]{1,0:T(8,128)} %copy-done.1) | data formatting | bytes 9437184 | tf_op jit(solution)/shard_map/dot_general | solution.py:231
  292.0 16.7 %collective-permute-done.13 = bf16[768,768]{1,0:T(8,128)(2,1)} collective-permute-done((bf16[768,768]{1,0:T(8,128)(2,1)S(1)}, bf16[768,768]{1,0:T(8,128)(2,1)}, u32[]{:S(2)}, u32[]{:S(2)}) %collective-permute-start.13) | collective-permute-done | bytes 1179680 | tf_op jit(solution)/shard_map/ppermute | solution.py:163
  308.7 1.4 select_bitcast_fusion.3
  310.1 15.4 %collective-permute-done.15 = bf16[768,768]{1,0:T(8,128)(2,1)} collective-permute-done((bf16[768,768]{1,0:T(8,128)(2,1)}, bf16[768,768]{1,0:T(8,128)(2,1)}, u32[]{:S(2)}, u32[]{:S(2)}) %collective-permute-start.15) | collective-permute-done | bytes 1179680 | tf_op jit(solution)/shard_map/ppermute | solution.py:163
  325.6 1.4 select_bitcast_fusion.1
  327.0 3.9 %convert_add_fusion = f32[768,1536]{0,1:T(8,128)} fusion(f32[768,1536]{0,1:T(8,128)S(1)} %copy-done, bf16[768,1536]{0,1:T(8,128)(2,1)} %collective-permute-done.12, bf16[768,768]{0,1:T(8,128)(2,1)S(1)} %get-tuple-element.25, bf16[768,768]{0,1:T(8,128)(2,1)S(1)} %get-tuple-element.24, bf16[768,768]{0,1:T(8,128)(2,1)S(1)} %get-tuple-element.23, ...), kind=kLoop, calls=%fused_computation.10 | loop fusion | flops 14155776 | bytes 16515072 | tf_op jit(solution)/shard_map/add | solution.py:268
  330.9 6.0 %copy.26 = f32[768,1536]{1,0:T(8,128)} copy(f32[768,1536]{0,1:T(8,128)} %convert_add_fusion) | data formatting | bytes 9437184 | tf_op jit(solution)/shard_map/add | solution.py:268
  (53 shorter events, 2.9 us)
Async XLA Ops:
  1.4 2.8 collective-permute-start
  4.9 3.6 %collective-permute-start.1 = (f32[5,16]{1,0:T(8,128)S(1)}, f32[5,16]{1,0:T(8,128)S(1)}, u32[]{:S(2)}, u32[]{:S(2)}) collective-permute-start(f32[5,16]{1,0:T(8,128)S(1)} %pad_maximum_fusion.1), channel_id=1, source_target_pairs={{0,2},{1,3},{2,0},{3,1},{4,6},{5,7},{6,4},{7,5},{8,10},{9,11},{10,... | collective-permute-start | bytes 968 | tf_op jit(solution)/shard_map/ppermute | solution.py:45
  9.3 3.6 %collective-permute-start.2 = (f32[5,32]{1,0:T(8,128)S(1)}, f32[5,32]{1,0:T(8,128)S(1)}, u32[]{:S(2)}, u32[]{:S(2)}) collective-permute-start(f32[5,32]{1,0:T(8,128)S(1)} %pad_maximum_fusion.2), channel_id=1, source_target_pairs={{0,4},{1,5},{2,6},{3,7},{4,0},{5,1},{6,2},{7,3},{8,12},{9,13},{10,... | collective-permute-start | bytes 1928 | tf_op jit(solution)/shard_map/ppermute | solution.py:45
  13.7 3.6 %collective-permute-start.3 = (f32[5,64]{1,0:T(8,128)S(1)}, f32[5,64]{1,0:T(8,128)S(1)}, u32[]{:S(2)}, u32[]{:S(2)}) collective-permute-start(f32[5,64]{1,0:T(8,128)S(1)} %pad_maximum_fusion.3), channel_id=1, source_target_pairs={{0,8},{1,9},{2,10},{3,11},{4,12},{5,13},{6,14},{7,15},{8,0},{9,1},... | collective-permute-start | bytes 3848 | tf_op jit(solution)/shard_map/ppermute | solution.py:45
  17.3 4.5 %collective-permute-start.4 = (f32[5,128]{1,0:T(8,128)S(1)}, f32[5,128]{1,0:T(8,128)S(1)}, u32[]{:S(2)}, u32[]{:S(2)}) collective-permute-start(f32[5,128]{1,0:T(8,128)S(1)} %concatenate.52), channel_id=1, source_target_pairs={{0,16},{1,17},{2,18},{3,19},{4,20},{5,21},{6,22},{7,23},{8,24},{9,... | collective-permute-start | bytes 7688 | tf_op jit(solution)/shard_map/ppermute | solution.py:45
  22.0 114.6 %collective-permute-start.7 = (bf16[768,1536]{1,0:T(8,128)(2,1)}, bf16[768,1536]{1,0:T(8,128)(2,1)}, u32[]{:S(2)}, u32[]{:S(2)}) collective-permute-start(bf16[768,1536]{1,0:T(8,128)(2,1)} %param.9), channel_id=1, source_target_pairs={{0,4},{1,5},{2,6},{3,7},{4,0},{5,1},{6,2},{7,3},{8,12},{9,13},{10,... | collective-permute-start | bytes 7077896 | tf_op jit(solution)/shard_map/ppermute | solution.py:163
  23.5 110.4 %collective-permute-start.8 = (bf16[768,1536]{1,0:T(8,128)(2,1)}, bf16[768,1536]{1,0:T(8,128)(2,1)}, u32[]{:S(2)}, u32[]{:S(2)}) collective-permute-start(bf16[768,1536]{1,0:T(8,128)(2,1)} %param.9), channel_id=1, source_target_pairs={{0,8},{1,9},{2,10},{3,11},{4,12},{5,13},{6,14},{7,15},{8,0},{9,1},... | collective-permute-start | bytes 7077896 | tf_op jit(solution)/shard_map/ppermute | solution.py:163
  25.1 114.5 %collective-permute-start.5 = (bf16[768,1536]{1,0:T(8,128)(2,1)}, bf16[768,1536]{1,0:T(8,128)(2,1)}, u32[]{:S(2)}, u32[]{:S(2)}) collective-permute-start(bf16[768,1536]{1,0:T(8,128)(2,1)} %param.9), channel_id=1, source_target_pairs={{0,2},{1,3},{4,6},{5,7},{8,10},{9,11},{12,14},{13,15},{18,16},{19,... | collective-permute-start | bytes 7077896 | tf_op jit(solution)/shard_map/ppermute | solution.py:163
  122.0 32.5 %slice-start = ((s8[28311552]{0:T(1024)(128)(4,1)}), s8[4194304]{0:T(1024)(128)(4,1)S(1)}, s32[]{:S(2)}) async-start(s8[28311552]{0:T(1024)(128)(4,1)} %bitcast.73), calls=%async_computation | async-start | bytes 8388608
  122.0 32.5 %slice-start.1 = ((s8[28311552]{0:T(1024)(128)(4,1)}), s8[3145728]{0:T(1024)(128)(4,1)S(1)}, s32[]{:S(2)}) async-start(s8[28311552]{0:T(1024)(128)(4,1)} %bitcast.73), calls=%async_computation.1 | async-start | bytes 6291456
  127.6 26.9 %slice-start.2 = ((s8[28311552]{0:T(1024)(128)(4,1)}), s8[4194304]{0:T(1024)(128)(4,1)S(1)}, s32[]{:S(2)}) async-start(s8[28311552]{0:T(1024)(128)(4,1)} %bitcast.73), calls=%async_computation.2 | async-start | bytes 8388608
  133.9 20.7 %slice-start.3 = ((s8[28311552]{0:T(1024)(128)(4,1)}), s8[4194304]{0:T(1024)(128)(4,1)S(1)}, s32[]{:S(2)}) async-start(s8[28311552]{0:T(1024)(128)(4,1)} %bitcast.73), calls=%async_computation.3 | async-start | bytes 8388608
  136.4 22.9 %collective-permute-start.9 = (bf16[768,768]{1,0:T(8,128)(2,1)}, bf16[768,768]{1,0:T(8,128)(2,1)}, u32[]{:S(2)}, u32[]{:S(2)}) collective-permute-start(bf16[768,768]{1,0:T(8,128)(2,1)} %slice.41), channel_id=1, source_target_pairs={{0,4},{1,5},{2,6},{3,7},{4,0},{5,1},{6,2},{7,3},{8,12},{9,13},{10,... | collective-permute-start | bytes 3538952 | tf_op jit(solution)/shard_map/ppermute | solution.py:163
  139.0 22.8 %collective-permute-start.10 = (bf16[768,768]{1,0:T(8,128)(2,1)}, bf16[768,768]{1,0:T(8,128)(2,1)}, u32[]{:S(2)}, u32[]{:S(2)}) collective-permute-start(bf16[768,768]{1,0:T(8,128)(2,1)} %slice.42), channel_id=1, source_target_pairs={{0,8},{1,9},{2,10},{3,11},{4,12},{5,13},{6,14},{7,15},{8,0},{9,1},... | collective-permute-start | bytes 3538952 | tf_op jit(solution)/shard_map/ppermute | solution.py:163
  142.4 12.1 %slice-start.4 = ((s8[28311552]{0:T(1024)(128)(4,1)}), s8[4194304]{0:T(1024)(128)(4,1)S(1)}, s32[]{:S(2)}) async-start(s8[28311552]{0:T(1024)(128)(4,1)} %bitcast.73), calls=%async_computation.4 | async-start | bytes 8388608
  142.4 12.1 %slice-start.5 = ((s8[28311552]{0:T(1024)(128)(4,1)}), s8[4194304]{0:T(1024)(128)(4,1)S(1)}, s32[]{:S(2)}) async-start(s8[28311552]{0:T(1024)(128)(4,1)} %bitcast.73), calls=%async_computation.5 | async-start | bytes 8388608
  149.1 33.8 %collective-permute-start.6 = (bf16[768,1536]{1,0:T(8,128)(2,1)}, bf16[768,1536]{1,0:T(8,128)(2,1)}, u32[]{:S(2)}, u32[]{:S(2)}) collective-permute-start(bf16[768,1536]{1,0:T(8,128)(2,1)} %get-tuple-element.12), channel_id=1, source_target_pairs={{0,1},{1,0},{2,3},{3,2},{4,5},{5,4},{6,7},{7,6},{8,9},{9,8},{10,11... | collective-permute-start | bytes 7077896 | tf_op jit(solution)/shard_map/ppermute | solution.py:163
  149.1 5.5 %slice-start.6 = ((s8[28311552]{0:T(1024)(128)(4,1)}), s8[4194304]{0:T(1024)(128)(4,1)S(1)}, s32[]{:S(2)}) async-start(s8[28311552]{0:T(1024)(128)(4,1)} %bitcast.73), calls=%async_computation.6 | async-start | bytes 8388608
  182.9 26.3 %collective-permute-start.11 = (bf16[768,1536]{0,1:T(8,128)(2,1)}, bf16[768,1536]{0,1:T(8,128)(2,1)}, u32[]{:S(2)}, u32[]{:S(2)}) collective-permute-start(bf16[768,1536]{0,1:T(8,128)(2,1)} %dynamic-slice_convert_fusion), channel_id=1, source_target_pairs={{0,1},{1,0},{2,3},{3,2},{4,5},{5,4},{6,7},{7,6},{8,9},{9,8},{10,11... | collective-permute-start | bytes 7077896 | tf_op jit(solution)/shard_map/ppermute | solution.py:163
  198.4 2.2 copy-start.1
  200.9 83.7 %collective-permute-start.14 = (bf16[768,768]{1,0:T(8,128)(2,1)S(1)}, bf16[768,768]{1,0:T(8,128)(2,1)}, u32[]{:S(2)}, u32[]{:S(2)}) collective-permute-start(bf16[768,768]{1,0:T(8,128)(2,1)S(1)} %get-tuple-element.20), channel_id=1, source_target_pairs={{2,22},{3,30},{6,18},{7,26},{10,23},{11,31},{14,19},{15,27},{16,4}... | collective-permute-start | bytes 3538952 | tf_op jit(solution)/shard_map/ppermute | solution.py:163
  212.8 114.2 %collective-permute-start.12 = (bf16[768,1536]{0,1:T(8,128)(2,1)S(1)}, bf16[768,1536]{0,1:T(8,128)(2,1)}, u32[]{:S(2)}, u32[]{:S(2)}) collective-permute-start(bf16[768,1536]{0,1:T(8,128)(2,1)S(1)} %add_convert_fusion), channel_id=1, source_target_pairs={{2,0},{3,1},{6,4},{7,5},{10,8},{11,9},{14,12},{15,13},{16,18},{17,... | collective-permute-start | bytes 7077896 | tf_op jit(solution)/shard_map/ppermute | solution.py:163
  215.5 93.2 %collective-permute-start.13 = (bf16[768,768]{1,0:T(8,128)(2,1)S(1)}, bf16[768,768]{1,0:T(8,128)(2,1)}, u32[]{:S(2)}, u32[]{:S(2)}) collective-permute-start(bf16[768,768]{1,0:T(8,128)(2,1)S(1)} %get-tuple-element.21), channel_id=1, source_target_pairs={{2,16},{3,24},{6,20},{7,28},{10,17},{11,25},{14,21},{15,29},{16,2}... | collective-permute-start | bytes 3538952 | tf_op jit(solution)/shard_map/ppermute | solution.py:163
  284.6 41.0 %collective-permute-start.15 = (bf16[768,768]{1,0:T(8,128)(2,1)}, bf16[768,768]{1,0:T(8,128)(2,1)}, u32[]{:S(2)}, u32[]{:S(2)}) collective-permute-start(bf16[768,768]{1,0:T(8,128)(2,1)} %collective-permute-done.14), channel_id=1, source_target_pairs={{0,2},{1,3},{4,6},{5,7},{8,10},{9,11},{12,14},{13,15},{18,16},{19,... | collective-permute-start | bytes 3538952 | tf_op jit(solution)/shard_map/ppermute | solution.py:163
  292.0 35.0 %copy-start = (f32[768,1536]{0,1:T(8,128)S(1)}, f32[768,1536]{0,1:T(8,128)}, u32[]{:S(2)}) copy-start(f32[768,1536]{0,1:T(8,128)} %copy.25) | copy-start | bytes 14155780

commit v2 on v0

v2 whole, which is shorter than its diff:
```python
import functools

import jax
import jax.numpy as jnp
from jax import lax
from jax.experimental import pallas as pl
from jax.experimental.pallas import tpu as pltpu
from jax.sharding import PartitionSpec as P

ORB = 128
NR = 16
AXES = ("row", "col")
VMEM_BYTES = 60 * 1024 * 1024
EDGE_CHUNK = 256
BYTES_PER_US = 1_500_000
STEPS = ((0,), 1, 0, (1,))
CUTS = (6, 0)
PLAN = {
    'density_b_across_rows_2': ('raw_a_across_rows_1', 'raw_a_across_rows_2', 'raw_a_beside'),
    'far_2_3_across_cores': ('near_1_beside',),
    'wide_across_cores': ('density_b_across_rows_1', 'density_b_across_rows_2'),
}


def taking(microseconds):
    return pl.CostEstimate(flops=0, bytes_accessed=int(microseconds * BYTES_PER_US), transcendentals=0)


def prepare_kernel(cells, chunks, atoms, atoms_total, edges, corner, coefficient, hits, embedding):
    count = edges.shape[1]
    size = count // chunks
    vec = edges[0:3, :]
    squared = vec[0:1] * vec[0:1] + vec[1:2] * vec[1:2] + vec[2:3] * vec[2:3]
    radius = jnp.sqrt(squared + 0.25)
    x, y, z = vec[0:1] / radius, vec[1:2] / radius, vec[2:3] / radius
    harmonics = jnp.concatenate(
        [jnp.ones_like(x), x, y, z, x * y, y * z, z * x, x * x - y * y, 3.0 * z * z - 1.0], axis=0
    )
    for k in range(NR):
        away = (radius - (1.0 + 0.3 * k)) / 0.5
        embedding[9 * k : 9 * k + 9, :] = jnp.exp(-(away * away)) * harmonics

    flipped = edges[...].T
    first, second = flipped[:, 3:4], flipped[:, 4:5]
    position = first * atoms_total + second
    position_row = edges[3:4, :] * atoms_total + edges[4:5, :]
    same = position == position_row
    coefficient[...] = lax.dot_general(
        same.astype(jnp.float32),
        embedding[...],
        (((1,), (1,)), ((), ())),
        precision=lax.Precision.HIGHEST,
        preferred_element_type=jnp.float32,
    ).astype(jnp.bfloat16)
    before = lax.broadcasted_iota(jnp.int32, (count, count), 1) < lax.broadcasted_iota(jnp.int32, (count, count), 0)
    repeated = jnp.max(jnp.where(same & before, 1.0, 0.0), axis=1, keepdims=True)

    mirrored = corner[2:3, :]
    row = first + mirrored * (second - first) - corner[0:1, :]
    col = second + mirrored * (first - second) - corner[1:2, :]
    limit = float(atoms)
    found = (row >= 0) & (row < limit) & (col >= 0) & (col < limit) & (corner[3:4, :] > 0) & (repeated < 0.5)
    found = jnp.where(found, 1.0, 0.0)
    lanes = lax.broadcasted_iota(jnp.int32, (1, ORB), 1).astype(jnp.float32)
    index = lax.broadcasted_iota(jnp.int32, (size, 1), 0).astype(jnp.float32)
    upto = lax.broadcasted_iota(jnp.int32, (size, size), 1) <= lax.broadcasted_iota(jnp.int32, (size, size), 0)
    upto = jnp.where(upto, 1.0, 0.0).astype(jnp.bfloat16)
    for chunk in range(chunks):
        part = slice(chunk * size, (chunk + 1) * size)
        here = found[part]
        place = jnp.dot(upto, here.astype(jnp.bfloat16), preferred_element_type=jnp.float32)
        code = (index * 2 + mirrored) * 4096 + row[part] * 64 + col[part]
        place = jnp.where(here > 0.5, place - 1.0, -1000.0)
        total = jnp.sum(here, axis=0, keepdims=True)
        for cell in range(cells):
            other = cells + cell
            direct = total[:, cell : cell + 1]
            at = jnp.where(place[:, cell : cell + 1] == lanes, code[:, cell : cell + 1], 0.0)
            at = at + jnp.where(place[:, other : other + 1] + direct == lanes, code[:, other : other + 1], 0.0)
            codes = jnp.sum(at, axis=0, keepdims=True)
            codes = jnp.where(lanes == ORB - 1, direct + total[:, other : other + 1], codes)
            hits[chunk, cell : cell + 1, :] = codes.astype(jnp.int32)


def prepare(edges, corner, atoms, atoms_total):
    count = edges.shape[1]
    chunks = max(1, count // EDGE_CHUNK)
    cells = corner.shape[1]
    once = jnp.concatenate([corner, jnp.zeros((1, cells), jnp.int32), jnp.ones((1, cells), jnp.int32)])
    twice = jnp.concatenate([corner, jnp.ones((2, cells), jnp.int32)])
    table = jnp.concatenate([once, twice], axis=1).astype(jnp.float32)
    table = jnp.pad(table, ((0, 4), (0, ORB - 2 * cells)))
    return pl.pallas_call(
        functools.partial(prepare_kernel, cells, chunks, atoms, atoms_total),
        out_shape=[
            jax.ShapeDtypeStruct((count, 9 * NR), jnp.bfloat16),
            jax.ShapeDtypeStruct((chunks, cells, ORB), jnp.int32),
        ],
        scratch_shapes=[pltpu.VMEM((9 * NR, count), jnp.float32)],
        cost_estimate=taking(3),
        compiler_params=pltpu.CompilerParams(vmem_limit_bytes=VMEM_BYTES),
    )(edges, table)


def density_kernel(chunks, cells, unread, base, hits, scale, corner, coefficient, weight, *refs):
    raw = refs[:cells]
    out = refs[cells + unread : 2 * cells + unread]
    raw_in, total, ready, blocks, sems = refs[2 * cells + unread :]
    size = coefficient.shape[0] // chunks
    side = total.shape[0]
    wide = 8
    pitch = ORB + 8
    copies = [pltpu.make_async_copy(raw[n], raw_in.at[n], sems.at[0, n]) for n in range(cells)]
    for copy in copies:
        copy.start()
    inverse = scale[1]

    def expand(chunk):
        def step(i, _):
            at = pl.multiple_of(i * (ORB * wide), ORB * wide)
            value = jnp.dot(
                coefficient[pl.ds(chunk * size, size), :],
                weight[:, pl.ds(at, ORB * wide)],
                preferred_element_type=jnp.float32,
            )
            for part in range(wide):
                blocks[pl.ds(i * wide + part, size, stride=pitch), :] = value[:, part * ORB : (part + 1) * ORB]
            return 0

        lax.fori_loop(0, ORB // wide, step, 0)

    if chunks == 1:
        expand(0)
    writes = []
    for n in range(cells):
        copies[n].wait()

        def spread(i, _):
            at = pl.ds(pl.multiple_of(i * ORB, ORB), ORB)
            total[at, :] = raw_in[n, at, :].astype(jnp.float32) * (-inverse)
            return 0

        lax.fori_loop(0, side // ORB, spread, 0)

        @pl.when(corner[0, base + n] == corner[1, base + n])
        def _():
            rows = lax.broadcasted_iota(jnp.int32, (ORB, ORB), 0)
            cols = lax.broadcasted_iota(jnp.int32, (ORB, ORB), 1)
            unit = jnp.where(rows == cols, scale[0], jnp.float32(0.0))
            for at in range(0, side, ORB):
                total[at : at + ORB, at : at + ORB] += unit

        for chunk in range(chunks):
            if chunks > 1:
                expand(chunk)

            def scatter(t, _):
                hit = hits[chunk, base + n, t]
                col = pl.multiple_of((hit % 64) * ORB, ORB)
                row = pl.multiple_of((hit // 64 % 64) * ORB, ORB)
                pair = hit // 4096
                spot = (pl.ds(row, ORB), pl.ds(col, ORB))
                block = blocks[pl.ds(pl.multiple_of(pair // 2 * pitch, 8), ORB), :] * inverse

                @pl.when(pair % 2 == 0)
                def _():
                    total[spot] = total[spot] - block

                @pl.when(pair % 2 == 1)
                def _():
                    total[spot] = total[spot] - block.T

                return 0

            lax.fori_loop(0, hits[chunk, base + n, ORB - 1], scatter, 0)

        def finish(i, _):
            at = pl.ds(pl.multiple_of(i * ORB, ORB), ORB)
            ready[n, at, :] = total[at, :].astype(jnp.bfloat16)
            return 0

        lax.fori_loop(0, side // ORB, finish, 0)
        writes.append(pltpu.make_async_copy(ready.at[n], out[n], sems.at[1, n]))
        writes[-1].start()
    for write in writes:
        write.wait()


def densities(raw, base, corner, hits, scale, coefficient, weight, sooner):
    cells = len(raw)
    side = raw[0].shape[0]
    edges = coefficient.shape[0]
    chunks = max(1, edges // EDGE_CHUNK)
    any_spec = pl.BlockSpec(memory_space=pl.ANY)
    return pl.pallas_call(
        functools.partial(density_kernel, chunks, cells, len(sooner), base),
        out_shape=[jax.ShapeDtypeStruct((side, side), jnp.bfloat16)] * cells,
        in_specs=[pl.BlockSpec(memory_space=pltpu.SMEM)] * 3
        + [pl.BlockSpec(memory_space=pltpu.VMEM)] * 2
        + [any_spec] * (cells + len(sooner)),
        out_specs=[any_spec] * cells,
        scratch_shapes=[
            pltpu.VMEM((cells, side, side), jnp.bfloat16),
            pltpu.VMEM((side, side), jnp.float32),
            pltpu.VMEM((cells, side, side), jnp.bfloat16),
            pltpu.VMEM((edges // chunks * (ORB + 8), ORB), jnp.float32),
            pltpu.SemaphoreType.DMA((2, cells)),
        ],
        cost_estimate=taking(6 + 2.5 * cells),
        compiler_params=pltpu.CompilerParams(vmem_limit_bytes=VMEM_BYTES),
    )(hits, scale, corner, coefficient, weight, *raw, *sooner)


def add_product(total, left, right, transposed, fresh):
    rows = total.shape[0]
    block = rows // 2
    contract = (((1,), (1,)), ((), ())) if transposed else (((1,), (0,)), ((), ()))
    for start in range(0, rows, block):
        at = pl.ds(start, block)
        value = lax.dot_general(left[at, :], right[...], contract, preferred_element_type=jnp.float32)
        total[at, :] = value if fresh else total[at, :] + value


def near_kernel(sides, sources, seeded, last, unread, source, *refs):
    count = len(sides)
    refs = list(refs)
    tall = [refs.pop(0) for _ in range(count)]
    wide = [refs.pop(0) for _ in range(sources)]
    seed = refs.pop(0) if seeded else None
    refs = refs[unread:]
    total = refs.pop(0)
    rounded = refs.pop(0) if last else None
    tall_in, wide_in, sems = refs
    waits = []
    for n in range(count):
        for s in range(sources):

            @pl.when(source[n] == s)
            def _():
                pltpu.make_async_copy(wide[s].at[sides[n]], wide_in.at[n], sems.at[n, 0]).start()

        here = [
            pltpu.make_async_copy(wide[0].at[sides[n]], wide_in.at[n], sems.at[n, 0]),
            pltpu.make_async_copy(tall[n], tall_in.at[n], sems.at[n, 1]),
        ]
        here[1].start()
        if seeded and n == 0:
            here.append(pltpu.make_async_copy(seed, total, sems.at[count, 0]))
            here[-1].start()
        waits.append(here)
    for n in range(count):
        for copy in waits[n]:
            copy.wait()
        add_product(total, wide_in.at[n], tall_in.at[n], False, n == 0 and not seeded)
    if last:
        rounded[...] = total[...].astype(jnp.bfloat16)


def near_share(source, tall, sides, wide, seed, last, sooner):
    cell = tall[0].shape
    sources = len(wide)
    count = len(tall)
    any_spec = pl.BlockSpec(memory_space=pl.ANY)
    operands = [source, *tall, *wide]
    if seed is not None:
        operands.append(seed)
    operands += sooner
    shapes = [jax.ShapeDtypeStruct(cell, jnp.float32)]
    if last:
        shapes.append(jax.ShapeDtypeStruct(cell, jnp.bfloat16))
    return pl.pallas_call(
        functools.partial(near_kernel, sides, sources, seed is not None, last, len(sooner)),
        out_shape=shapes,
        in_specs=[pl.BlockSpec(memory_space=pltpu.SMEM)] + [any_spec] * (len(operands) - 1),
        out_specs=[pl.BlockSpec(memory_space=pltpu.VMEM)] * len(shapes),
        scratch_shapes=[
            pltpu.VMEM((count,) + cell, jnp.bfloat16),
            pltpu.VMEM((count,) + cell, jnp.bfloat16),
            pltpu.SemaphoreType.DMA((count + 1, 2)),
        ],
        cost_estimate=taking(2 + 2.5 * count),
        compiler_params=pltpu.CompilerParams(vmem_limit_bytes=VMEM_BYTES),
    )(*operands)


def far_kernel(count, unread, *refs):
    cells = refs[: 2 + 2 * count]
    out, cells_in, total, sems = refs[2 + 2 * count + unread :]
    copies = [pltpu.make_async_copy(ref, cells_in.at[n], sems.at[n]) for n, ref in enumerate(cells)]
    for copy in copies:
        copy.start()
    copies[0].wait()
    copies[1].wait()
    for m in range(count):
        for q in range(2):
            n = 2 + 2 * m + q
            copies[n].wait()
            add_product(total, cells_in.at[q], cells_in.at[n], True, q == 0)
        out[m] = total[...].astype(jnp.bfloat16)


def far_share(own, tall, sooner):
    cell = own[0].shape
    count = len(tall) // 2
    items = 2 + 2 * count
    any_spec = pl.BlockSpec(memory_space=pl.ANY)
    return pl.pallas_call(
        functools.partial(far_kernel, count, len(sooner)),
        out_shape=jax.ShapeDtypeStruct((count,) + cell, jnp.bfloat16),
        in_specs=[any_spec] * (items + len(sooner)),
        out_specs=pl.BlockSpec(memory_space=pltpu.VMEM),
        scratch_shapes=[
            pltpu.VMEM((items,) + cell, jnp.bfloat16),
            pltpu.VMEM(cell, jnp.float32),
            pltpu.SemaphoreType.DMA((items,)),
        ],
        cost_estimate=taking(3 + 3 * count),
        compiler_params=pltpu.CompilerParams(vmem_limit_bytes=VMEM_BYTES),
    )(*own, *tall, *sooner)


def final_kernel(groups, pieces, slot, *refs):
    refs = list(refs)
    near = [refs.pop(0) for _ in range(2)]
    far = [refs.pop(0) for _ in range(groups)]
    opposite = [[refs.pop(0) for _ in range(n)] for n in pieces]
    out = refs.pop(0)
    turn = pl.program_id(0)
    block = 128
    for q in range(2):

        @pl.when(turn == q)
        def _():
            start = 0
            for piece in opposite[q]:
                rows = piece.shape[0]

                def step(n, _):
                    at = pl.ds(pl.multiple_of(n * block, block), block)
                    to = pl.ds(start, rows)
                    value = near[q][at, to]
                    for share in far:
                        value = value + share[q, at, to].astype(jnp.float32)
                    out[at, to] = value + piece[:, at].astype(jnp.float32).T
                    return 0

                lax.fori_loop(0, out.shape[0] // block, step, 0)
                start += rows


def final_sum(slot, near, far, opposite):
    side = near[0].shape[0]
    operands = [*near, *far, *opposite[0], *opposite[1]]
    return pl.pallas_call(
        functools.partial(final_kernel, len(far), [len(pieces) for pieces in opposite]),
        out_shape=jax.ShapeDtypeStruct((side, 2 * side), jnp.float32),
        grid_spec=pltpu.PrefetchScalarGridSpec(
            num_scalar_prefetch=1,
            grid=(2,),
            in_specs=[pl.BlockSpec(o.shape, lambda t, s, n=len(o.shape): (0,) * n) for o in operands],
            out_specs=pl.BlockSpec((side, side), lambda t, s: (0, s[t])),
        ),
        cost_estimate=taking(9),
        compiler_params=pltpu.CompilerParams(vmem_limit_bytes=VMEM_BYTES),
    )(slot, *operands)


def after(value, *earlier):
    return lax.optimization_barrier((value, *earlier))[0] if earlier else value


def shards(row_size, col_size, edge_vec, edge_atoms, block_weight, base, lower_bound, upper_bound):
    devices = row_size * col_size
    half_rows = row_size // 2
    half_cols = col_size // 2
    side = base.shape[0]
    atoms = side // ORB
    row = lax.axis_index("row")
    col = lax.axis_index("col")
    row_half, row_in = row // half_rows, row % half_rows
    col_half, col_in = col // half_cols, col % half_cols
    on_diagonal = row_half == col_half
    slots = jnp.stack([row_in % 2, 1 - row_in % 2]).astype(jnp.int32)

    def moves(where):
        pairs = []
        for r in range(row_size):
            for c in range(col_size):
                to = where(r // half_rows, r % half_rows, c // half_cols, c % half_cols)
                if to is not None:
                    h, i, y, k = to
                    pairs.append((r * col_size + c, (h * half_rows + i) * col_size + y * half_cols + k))
        return pairs

    made = {}

    def waits(what):
        return [made[name] for name in PLAN.get(what, ()) if name in made]

    def send(value, where, what):
        with jax.named_scope(what):
            made[what] = lax.ppermute(after(value, *waits(what)), AXES, moves(where))
        return made[what]

    def swap_rows(value, bit, what):
        return send(value, lambda h, i, y, k: (h, i ^ bit, y, k), f"{what}_across_rows_{bit}")

    def to_beside(value, from_diagonal, what):
        return send(value, lambda h, i, y, k: (h, i, 1 - y, k) if (h == y) == from_diagonal else None, what)

    raw = [lax.dynamic_slice(base, (0, slots[q] * side), (side, side)) for q in range(2)]
    singles = [1 << b for b in range(half_rows.bit_length() - 1)]
    others = [m for m in range(1, half_rows) if m & (m - 1)]

    edges = jnp.concatenate(
        [edge_vec, edge_atoms.astype(jnp.float32), jnp.zeros((3, edge_vec.shape[1]), jnp.float32)], axis=0
    )
    raw_a = {0: raw[0]}

    def double(value, bit):
        arrived = lax.ppermute(value, AXES, [(d, d ^ bit) for d in range(devices)])
        return jnp.concatenate([value, arrived], axis=1)

    bit = devices // 2
    while bit > col_size:
        edges = double(edges, bit)
        bit //= 2
    for mask in singles[1:]:
        raw_a[mask] = swap_rows(after(raw[0], edges), mask, "raw_a")
    edges = double(edges, col_size)
    raw_a[1] = swap_rows(after(raw[1], edges), 1, "raw_a")
    bit = col_size // 2
    while bit >= half_cols:
        edges = double(edges, bit)
        bit //= 2
    beside_a = to_beside(after(raw[0], edges), True, "raw_a_beside")
    while bit:
        edges = double(edges, bit)
        bit //= 2

    span = upper_bound[0] - lower_bound[0]
    scale = jnp.stack([upper_bound[0] / span, 1.0 / span])

    done = []
    sums = []
    beside = []

    def tall_corner(mask, q):
        return row_half * half_rows + (row_in ^ mask), 2 * col + slots[q]

    corners = [tall_corner(0, q) for q in range(2)] + [tall_corner(m, 0) for m in singles]
    corners += [(row, row_half * half_rows + 2 * col_in + slots[0])]
    corner = jnp.stack([jnp.stack([c[n] for c in corners]) for n in range(2)]).astype(jnp.int32) * atoms
    coefficient, hits = prepare(edges, corner, atoms, atoms * row_size)

    def density(cells, at):
        what = f"density_{at}"
        with jax.named_scope(what):
            got = densities(cells, at, corner, hits, scale, coefficient, block_weight, [*done[-1:], *waits(what)])
        done.append(got[0])
        return got

    tall = {mask: [None, None] for mask in range(half_rows)}
    def near_part(q):
        what = f"near_{q}"
        source = jnp.stack([(row_in // 2) ^ col_in ^ (m // 2) for m in range(half_rows)]).astype(jnp.int32)
        sides = tuple(m % 2 for m in range(half_rows))
        with jax.named_scope(what):
            got = near_share(source, [tall[m][q] for m in tall], sides, wide, None, True, [*done[-1:], *waits(what)])
        done.append(got[0])
        made[what] = got[1]
        return got

    def far_product(masks):
        what = "far_" + "_".join(map(str, masks))
        with jax.named_scope(what):
            part = far_share(own, [tall[m][q] for m in masks for q in range(2)], [*done[-1:], *waits(what)])
        done.append(part)
        made[what] = part
        return part

    def far_sum(masks, part):
        what = "far_" + "_".join(map(str, masks))
        owner = lambda i: (i // 2) ^ (masks[0] // 2)
        summed = part.astype(jnp.float32)
        for turn in range(1, half_cols):
            arrived = send(
                part,
                lambda h, i, y, k: (h, i, y, owner(i)) if h != y and k == owner(i) ^ turn else None,
                what + "_across_cores",
            )
            summed = summed + arrived.astype(jnp.float32)
        return send(
            summed.astype(jnp.bfloat16),
            lambda h, i, y, k: (h, i, 1 - y, k) if h != y and k == owner(i) else None,
            what + "_beside",
        )

    tall[0] = density(raw, 0)
    own = tall[0]
    tall[1][1] = swap_rows(own[0], 1, "density_b")
    beside_b = to_beside(own[1], True, "density_b_beside")
    mine_a = jnp.where(on_diagonal, raw[0], beside_a)
    for mask in singles[1:]:
        tall[mask][1] = swap_rows(own[1], mask, "density_b")
    got = density([raw_a[m] for m in singles] + [mine_a], 2)
    for mask, value in zip(singles, got):
        tall[mask][0] = value
    wide = [jnp.stack([got[len(singles)], jnp.where(on_diagonal, own[1], beside_b)])]
    for turn in range(1, half_cols):
        wide.append(send(wide[0], lambda h, i, y, k: (h, i, y, k ^ turn), "wide_across_cores"))
    for mask in others:
        bit = 1 if mask ^ 1 in singles else mask & ~1 & -(mask & ~1)
        tall[mask][1] = swap_rows(tall[mask ^ bit][0 if bit == 1 else 1], bit, "forward_b")
        bit = 1 << (mask.bit_length() - 1)
        tall[mask][0] = swap_rows(tall[mask ^ bit][0], bit, "forward_a")

    def opposite(h, i, y, k, turn):
        return (1 - h, k * 2 + (i + turn) % 2, h, i // 2)

    def exchange(value, turn, cut):
        across = lambda h, i, y, k: opposite(h, i, y, k, turn) if h != y else None
        onward = lambda h, i, y, k: opposite(h, i, 1 - y, k, turn) if h == y else None
        pieces = []
        if cut > 0:
            pieces.append(send(value[:cut], across, f"near_{turn}_direct"))
        if cut < side:
            ahead = to_beside(value[cut:], False, f"near_{turn}_beside")
            pieces.append(send(ahead, onward, f"near_{turn}_ahead"))
        return pieces

    near, got, parts, far = {}, {}, [], []
    for step in STEPS:
        if isinstance(step, int):
            near[step], value = near_part(step)
            got[step] = exchange(value, step, CUTS[step] * side // 6)
        else:
            for m in range(0, half_rows, 2):
                if min(m // 2, 1) in step:
                    parts.append(([m, m + 1], far_product([m, m + 1])))
    for masks, part in parts:
        far.append(far_sum(masks, part))
    return final_sum(slots, [near[0], near[1]], far, [got[0], got[1]])


def solution(mesh):
    return jax.shard_map(
        functools.partial(shards, mesh.shape["row"], mesh.shape["col"]),
        mesh=mesh,
        in_specs=(P(None, AXES), P(None, AXES), P(), P("row", "col"), P(), P()),
        out_specs=P("row", "col"),
        check_vma=False,
    )
```

time: 537 us -> 218 us (0.41)
  waiting for transfers between devices: 429 us -> 98.5 us
  Pallas kernels: 0 us -> 66.3 us
  blocking collectives: 37.9 us -> 0 us
  starting transfers between devices: 0.22 us -> 34.1 us
  matrix products: 25.6 us -> 0 us
  between operations: 14.8 us -> 1.71 us
  local copies, waits for them, and re-layouts: 13.9 us -> 3.35 us
    all_gather x2 -> x0, waiting for transfers between devices: 428 us -> none  [the longest x1 365 us: shards(): lax.all_gather(start_density, 'row', axis=0, tiled=True)]
    ppermute x0 -> x21, waiting for transfers between devices: none -> 98.5 us  [the longest x16 92.4 us: send(): made[what] = lax.ppermute(after(value, *waits(what)), AXES, moves(where))]
    pallas_call x0 -> x8, Pallas kernels: none -> 66.3 us  [the longest x2 22.7 us: densities(): pl.pallas_call(functools.partial(density_kernel, chunks, cells, len(soone...]
    all_gather x1 -> x0, blocking collectives: 37.9 us -> none  [shards(): gathered = lax.all_gather(packed, ('row', 'col'), axis=1, tiled=True)]
    ppermute x0 -> x21, starting transfers between devices: none -> 34.1 us  [the longest x16 28.2 us: send(): made[what] = lax.ppermute(after(value, *waits(what)), AXES, moves(where))]
    dot_general x5 -> x0, matrix products: 25.6 us -> none  [the longest x1 21 us: shards(): jnp.dot(row_strip, lax.all_gather(start_density, 'row', axis=0, tiled=Tru...]
    add x6 -> x0, other arithmetic: 7.29 us -> none  [the longest x1 7.27 us: shards(): blocks + blocks_back.transpose(0, 1, 3, 2)]
    unnamed x9 -> x26, local copies, waits for them, and re-layouts: 6.82 us -> 0.06 us
  transfers between devices with their start and end apart: 2 -> 21, of which waited for: 2 -> 11; matrix products, arithmetic and copies ran while one was open for 0% -> 6% of each run, Pallas kernels for 0% -> 27%
where the time goes in v2:
time: 218 us
  waiting for transfers between devices  98.5 us (45%)
  Pallas kernels  66.3 us (30%)
  starting transfers between devices  34.1 us (16%)
  other arithmetic  13.9 us (6%)
  local copies, waits for them, and re-layouts  3.35 us (2%)
    ppermute x16, waiting for transfers between devices, send(): made[what] = lax.ppermute(after(value, *waits(what)), AXES, moves(where))  92.4 us
    ppermute x16, starting transfers between devices, send(): made[what] = lax.ppermute(after(value, *waits(what)), AXES, moves(where))  28.2 us
    pallas_call x2, Pallas kernels, densities(): pl.pallas_call(functools.partial(density_kernel, chunks, cells, len(soone...  22.7 us
    pallas_call x2, Pallas kernels, near_share(): pl.pallas_call(functools.partial(near_kernel, sides, sources, seed is not...  16.5 us
    pallas_call x2, Pallas kernels, far_share(): pl.pallas_call(functools.partial(far_kernel, count, len(sooner)), out_sha...  16.1 us
    pallas_call x1, Pallas kernels, final_sum(): pl.pallas_call(functools.partial(final_kernel, len(far), [len(pieces) for...  8.18 us
    ppermute x5, waiting for transfers between devices, double(): arrived = lax.ppermute(value, AXES, [(d, d ^ bit) for d in range(devices)])  6.07 us
    ppermute x5, starting transfers between devices, double(): arrived = lax.ppermute(value, AXES, [(d, d ^ bit) for d in range(devices)])  5.85 us
  transfers between devices with their start and end apart: 21, of which 11 were waited for; matrix products, arithmetic and copies ran while one was open for 6% of the time, Pallas kernels for 27%

profile of v2, /device:TPU:4, one launch (start us, length us, event | category | flops | bytes accessed | tf_op | source)
XLA Modules:
  0.0 217.9 jit_solution(7125244092505221497)
XLA Ops:
  0.0 0.7 convert_element_type.26
  0.7 0.7 pad_maximum_fusion.1
  1.4 2.6 %collective-permute-start = (f32[8,8]{1,0:T(8,128)S(1)}, f32[8,8]{1,0:T(8,128)S(1)}, u32[]{:S(2)}, u32[]{:S(2)}) collective-permute-start(f32[8,8]{1,0:T(8,128)S(1)} %pad_maximum_fusion.1), channel_id=1, source_target_pairs={{0,16},{1,17},{2,18},{3,19},{4,20},{5,21},{6,22},{7,23},{8,24},{9,... | collective-permute-start | bytes 776 | tf_op jit(solution)/shard_map/ppermute | solution.py:421
  4.0 1.9 collective-permute-done
  5.9 0.8 pad_maximum_fusion.2
  6.6 1.6 collective-permute-start.1
  8.2 2.0 collective-permute-done.1
  10.2 0.8 pad_maximum_fusion.3
  11.0 1.5 collective-permute-start.2
  12.5 2.1 collective-permute-done.2
  14.6 0.8 pad_maximum_fusion.4
  15.5 1.8 constant_dynamic-slice_fusion
  17.4 2.0 collective-permute-start.6
  19.3 1.5 collective-permute-start.5
  20.9 1.3 collective-permute-start.7
  23.9 0.7 pad_maximum_fusion.5.scale
  25.2 0.7 concatenate.36.edges
  25.8 2.8 %shard_map.64 = (bf16[256,144]{1,0:T(8,128)(2,1)}, s32[1,5,128]{2,1,0:T(8,128)}) custom-call(f32[8,256]{1,0:T(8,128)} %concatenate.36.edges, f32[8,128]{1,0:T(8,128)} %pad.5.corner), custom_call_target="tpu_custom_call" | custom-call | bytes 4500000 | tf_op jit(solution)/shard_map/pallas_call | solution.py:93
  28.7 10.6 %density_0.1 = (bf16[768,768]{1,0:T(8,128)(2,1)}, bf16[768,768]{1,0:T(8,128)(2,1)}) custom-call(s32[1,5,128]{2,1,0:T(8,128)} %get-tuple-element.22.hits, f32[2]{0:T(128)} %pad_maximum_fusion.5.scale, s32[2,5]{1,0:T(2,128)} %copy-done.11, bf16[256,144]{1,0:T(8,128)(2,1)} %get-tuple-element.23.coefficient, bf16[144,16384]{1,0:T(8,128)(2,1)} %weight.3, ...), custom_call_target="tpu_custom_call" | custom-call | bytes 16500000 | tf_op jit(solution)/shard_map/density_0/pallas_call | solution.py:195
  39.3 1.3 collective-permute-start.9
  40.6 1.0 collective-permute-start.10
  41.8 1.3 collective-permute-done.5.refs_0_
  43.1 3.2 %collective-permute-done.7 = bf16[768,768]{1,0:T(8,128)(2,1)} collective-permute-done((bf16[768,768]{1,0:T(8,128)(2,1)S(1)}, bf16[768,768]{1,0:T(8,128)(2,1)}, u32[]{:S(2)}, u32[]{:S(2)}) %collective-permute-start.7) | collective-permute-done | bytes 1179680 | tf_op jit(solution)/shard_map/raw_a_beside/ppermute | solution.py:402
  46.3 1.4 collective-permute-start.11
  47.7 2.4 %broadcast_select_fusion.refs_2_ = bf16[768,768]{1,0:T(8,128)(2,1)} fusion(bf16[768,768]{1,0:T(8,128)(2,1)} %copy-done.2, bf16[768,768]{1,0:T(8,128)(2,1)} %collective-permute-done.7, pred[]{:T(512)S(6)} %eq.8), kind=kLoop, calls=%fused_computation.4 | loop fusion | flops 589824 | bytes 3538945 | tf_op jit(solution)/shard_map/jit(_where)/select_n | solution.py:503
  50.1 12.1 %density_2.1 = (bf16[768,768]{1,0:T(8,128)(2,1)}, bf16[768,768]{1,0:T(8,128)(2,1)}, bf16[768,768]{1,0:T(8,128)(2,1)}) custom-call(s32[1,5,128]{2,1,0:T(8,128)} %get-tuple-element.22.hits, f32[2]{0:T(128)} %pad_maximum_fusion.5.scale, s32[2,5]{1,0:T(2,128)} %copy-done.11, bf16[256,144]{1,0:T(8,128)(2,1)} %get-tuple-element.23.coefficient, ...), custom_call_target="tpu_custom_call" | custom-call | bytes 20250000 | tf_op jit(solution)/shard_map/density_2/pallas_call | solution.py:195
  62.2 9.3 %collective-permute-done.9 = bf16[768,768]{1,0:T(8,128)(2,1)} collective-permute-done((bf16[768,768]{1,0:T(8,128)(2,1)}, bf16[768,768]{1,0:T(8,128)(2,1)}, u32[]{:S(2)}, u32[]{:S(2)}) %collective-permute-start.9) | collective-permute-done | bytes 1179680 | tf_op jit(solution)/shard_map/density_b_beside/ppermute | solution.py:402
  71.6 1.4 select_bitcast_fusion
  73.0 1.6 pad_maximum_fusion.refs_4_
  75.3 0.6 pad_add_fusion.1.source
  76.0 0.8 collective-permute-start.8
  76.8 8.4 %far_0_1.1.refs_6_ = bf16[2,768,768]{2,1,0:T(8,128)(2,1)} custom-call(bf16[768,768]{1,0:T(8,128)(2,1)} %get-tuple-element.24.refs_3_.refs_0_.refs_2_, bf16[768,768]{1,0:T(8,128)(2,1)} %get-tuple-element.32.refs_1_.refs_3_.refs_0_, bf16[768,768]{1,0:T(8,128)(2,1)} %get-tuple-element.24.refs_3_.refs_0_.refs_2_, ...), custom_call_target="tpu_custom_call" | custom-call | bytes 13500000 | tf_op jit(solution)/shard_map/far_0_1/pallas_call | solution.py:307
  85.2 18.2 %collective-permute-done.13.refs_3_.refs_5_ = bf16[768,768]{1,0:T(8,128)(2,1)} collective-permute-done((bf16[768,768]{1,0:T(8,128)(2,1)}, bf16[768,768]{1,0:T(8,128)(2,1)}, u32[]{:S(2)}, u32[]{:S(2)}) %collective-permute-start.13) | collective-permute-done | bytes 1179680 | tf_op jit(solution)/shard_map/forward_b_across_rows_1/ppermute | solution.py:402
  103.4 8.2 %near_1.1 = (f32[768,768]{1,0:T(8,128)}, bf16[768,768]{1,0:T(8,128)(2,1)}) custom-call(s32[4]{0:T(128)} %pad_add_fusion.1.source, bf16[768,768]{1,0:T(8,128)(2,1)} %get-tuple-element.32.refs_1_.refs_3_.refs_0_, bf16[768,768]{1,0:T(8,128)(2,1)} %copy-done.7, bf16[768,768]{1,0:T(8,128)(2,1)} %copy-done.5, ...), custom_call_target="tpu_custom_call" | custom-call | bytes 18000000 | tf_op jit(solution)/shard_map/near_1/pallas_call | solution.py:271
  111.6 2.8 %collective-permute-start.16 = (bf16[768,768]{1,0:T(8,128)(2,1)}, bf16[768,768]{1,0:T(8,128)(2,1)}, u32[]{:S(2)}, u32[]{:S(2)}) collective-permute-start(bf16[768,768]{1,0:T(8,128)(2,1)} %get-tuple-element.36), channel_id=1, source_target_pairs={{2,0},{3,1},{6,4},{7,5},{10,8},{11,9},{14,12},{15,13},{16,18},{17,... | collective-permute-start | bytes 3538952 | tf_op jit(solution)/shard_map/near_1_beside/ppermute | solution.py:402
  114.4 1.5 collective-permute-start.14
  115.9 8.3 %near_0.1 = (f32[768,768]{1,0:T(8,128)}, bf16[768,768]{1,0:T(8,128)(2,1)}) custom-call(s32[4]{0:T(128)} %pad_add_fusion.1.source, bf16[768,768]{1,0:T(8,128)(2,1)} %get-tuple-element.24.refs_3_.refs_0_.refs_2_, bf16[768,768]{1,0:T(8,128)(2,1)} %get-tuple-element.28.refs_4_.refs_6_.refs_1_, bf16[768,768]{1,0:T(8,128)(2,1)} %get-tuple-element.29.refs_2_, ...), custom_call_target="tpu_custom_call" | custom-call | bytes 18000000 | tf_op jit(solution)/shard_map/near_0/pallas_call | solution.py:271
  124.2 7.6 %far_2_3.1 = bf16[2,768,768]{2,1,0:T(8,128)(2,1)} custom-call(bf16[768,768]{1,0:T(8,128)(2,1)} %get-tuple-element.24.refs_3_.refs_0_.refs_2_, bf16[768,768]{1,0:T(8,128)(2,1)} %get-tuple-element.32.refs_1_.refs_3_.refs_0_, bf16[768,768]{1,0:T(8,128)(2,1)} %get-tuple-element.29.refs_2_, bf16[768,768]{1,0:T(8,128)(2,1)} %copy-done.5, ...), custom_call_target="tpu_custom_call" | custom-call | bytes 13500000 | tf_op jit(solution)/shard_map/far_2_3/pallas_call | solution.py:307
  131.9 6.9 %collective-permute-done.16 = bf16[768,768]{1,0:T(8,128)(2,1)} collective-permute-done((bf16[768,768]{1,0:T(8,128)(2,1)}, bf16[768,768]{1,0:T(8,128)(2,1)}, u32[]{:S(2)}, u32[]{:S(2)}) %collective-permute-start.16) | collective-permute-done | bytes 1179680 | tf_op jit(solution)/shard_map/near_1_beside/ppermute | solution.py:402
  138.8 1.4 collective-permute-start.17
  140.3 2.4 %add_convert_fusion.1 = bf16[2,768,768]{2,1,0:T(8,128)(2,1)S(1)} fusion(bf16[2,768,768]{2,1,0:T(8,128)(2,1)} %collective-permute-done.14, bf16[2,768,768]{2,1,0:T(8,128)(2,1)S(1)} %copy-done.1), kind=kLoop, calls=%fused_computation.1 | loop fusion | flops 4718592 | bytes 7077888 | tf_op jit(solution)/shard_map/convert_element_type | solution.py:494
  142.6 4.0 %collective-permute-start.15 = (bf16[2,768,768]{2,1,0:T(8,128)(2,1)S(1)}, bf16[2,768,768]{2,1,0:T(8,128)(2,1)S(1)}, u32[]{:S(2)}, u32[]{:S(2)}) collective-permute-start(bf16[2,768,768]{2,1,0:T(8,128)(2,1)S(1)} %add_convert_fusion.1), channel_id=1, source_target_pairs={{2,0},{6,4},{11,9},{15,13},{16,18},{20,22},{25,27},{29,31}} | collective-permute-start | bytes 7077896 | tf_op jit(solution)/shard_map/far_0_1_beside/ppermute | solution.py:402
  147.3 2.1 collective-permute-start.18
  149.4 5.2 %collective-permute-start.19 = (bf16[768,768]{1,0:T(8,128)(2,1)S(1)}, bf16[768,768]{1,0:T(8,128)(2,1)S(1)}, u32[]{:S(2)}, u32[]{:S(2)}) collective-permute-start(bf16[768,768]{1,0:T(8,128)(2,1)S(1)} %copy-done.12), channel_id=1, source_target_pairs={{2,16},{3,24},{6,20},{7,28},{10,17},{11,25},{14,21},{15,29},{16,2}... | collective-permute-start | bytes 3538952 | tf_op jit(solution)/shard_map/near_0_direct/ppermute | solution.py:402
  154.6 1.3 collective-permute-start.20
  156.5 48.9 %collective-permute-done.19.refs_4_ = bf16[768,768]{1,0:T(8,128)(2,1)S(1)} collective-permute-done((bf16[768,768]{1,0:T(8,128)(2,1)S(1)}, bf16[768,768]{1,0:T(8,128)(2,1)S(1)}, u32[]{:S(2)}, u32[]{:S(2)}) %collective-permute-start.19) | collective-permute-done | bytes 1179680 | tf_op jit(solution)/shard_map/near_0_direct/ppermute | solution.py:402
  205.4 4.3 %collective-permute-done.20.refs_5_ = bf16[768,768]{1,0:T(8,128)(2,1)} collective-permute-done((bf16[768,768]{1,0:T(8,128)(2,1)}, bf16[768,768]{1,0:T(8,128)(2,1)}, u32[]{:S(2)}, u32[]{:S(2)}) %collective-permute-start.20) | collective-permute-done | bytes 1179680 | tf_op jit(solution)/shard_map/near_1_ahead/ppermute | solution.py:402
  209.7 8.2 %shard_map.65 = f32[768,1536]{1,0:T(8,128)} custom-call(s32[2]{0:T(128)} %pad_add_fusion.slot, f32[768,768]{1,0:T(8,128)} %get-tuple-element.35.refs_6_.refs_0_, f32[768,768]{1,0:T(8,128)} %get-tuple-element.34.refs_6_.refs_1_, bf16[2,768,768]{2,1,0:T(8,128)(2,1)} %copy-done.8, bf16[2,768,768]{2,1,0:T(8,128)(2,1)} %collective-permute-done.18.refs_3_, ...), custom_call_target="tpu_custom_call" | custom-call | bytes 13500000 | tf_op jit(solution)/shard_map/pallas_call | solution.py:354
  (52 shorter events, 3.3 us)
Async XLA Ops:
  1.4 4.5 %collective-permute-start = (f32[8,8]{1,0:T(8,128)S(1)}, f32[8,8]{1,0:T(8,128)S(1)}, u32[]{:S(2)}, u32[]{:S(2)}) collective-permute-start(f32[8,8]{1,0:T(8,128)S(1)} %pad_maximum_fusion.1), channel_id=1, source_target_pairs={{0,16},{1,17},{2,18},{3,19},{4,20},{5,21},{6,22},{7,23},{8,24},{9,... | collective-permute-start | bytes 776 | tf_op jit(solution)/shard_map/ppermute | solution.py:421
  6.6 3.6 %collective-permute-start.1 = (f32[8,16]{1,0:T(8,128)S(1)}, f32[8,16]{1,0:T(8,128)S(1)}, u32[]{:S(2)}, u32[]{:S(2)}) collective-permute-start(f32[8,16]{1,0:T(8,128)S(1)} %pad_maximum_fusion.2), channel_id=1, source_target_pairs={{0,8},{1,9},{2,10},{3,11},{4,12},{5,13},{6,14},{7,15},{8,0},{9,1},... | collective-permute-start | bytes 1544 | tf_op jit(solution)/shard_map/ppermute | solution.py:421
  11.0 3.6 %collective-permute-start.2 = (f32[8,32]{1,0:T(8,128)S(1)}, f32[8,32]{1,0:T(8,128)S(1)}, u32[]{:S(2)}, u32[]{:S(2)}) collective-permute-start(f32[8,32]{1,0:T(8,128)S(1)} %pad_maximum_fusion.3), channel_id=1, source_target_pairs={{0,4},{1,5},{2,6},{3,7},{4,0},{5,1},{6,2},{7,3},{8,12},{9,13},{10,... | collective-permute-start | bytes 3080 | tf_op jit(solution)/shard_map/ppermute | solution.py:421
  15.4 5.4 %collective-permute-start.3 = (f32[8,64]{1,0:T(8,128)S(1)}, f32[8,64]{1,0:T(8,128)S(1)}, u32[]{:S(2)}, u32[]{:S(2)}) collective-permute-start(f32[8,64]{1,0:T(8,128)S(1)} %pad_maximum_fusion.4), channel_id=1, source_target_pairs={{0,2},{1,3},{2,0},{3,1},{4,6},{5,7},{6,4},{7,5},{8,10},{9,11},{10,... | collective-permute-start | bytes 6152 | tf_op jit(solution)/shard_map/ppermute | solution.py:421
  17.3 11.3 %copy-start.2 = (bf16[768,768]{1,0:T(8,128)(2,1)}, bf16[768,768]{1,0:T(8,128)(2,1)S(1)}, u32[]{:S(2)}) copy-start(bf16[768,768]{1,0:T(8,128)(2,1)S(1)} %get-tuple-element.27.refs_0_) | copy-start | bytes 3538948
  17.3 11.3 %copy-start.6 = (bf16[768,768]{1,0:T(8,128)(2,1)}, bf16[768,768]{1,0:T(8,128)(2,1)S(1)}, u32[]{:S(2)}) copy-start(bf16[768,768]{1,0:T(8,128)(2,1)S(1)} %get-tuple-element.25.refs_1_) | copy-start | bytes 3538948
  17.4 24.4 %collective-permute-start.6 = (bf16[768,768]{1,0:T(8,128)(2,1)S(1)}, bf16[768,768]{1,0:T(8,128)(2,1)}, u32[]{:S(2)}, u32[]{:S(2)}) collective-permute-start(bf16[768,768]{1,0:T(8,128)(2,1)S(1)} %get-tuple-element.27.refs_0_), channel_id=1, source_target_pairs={{0,8},{1,9},{2,10},{3,11},{4,12},{5,13},{6,14},{7,15},{8,0},{9,1},... | collective-permute-start | bytes 3538952 | tf_op jit(solution)/shard_map/raw_a_across_rows_2/ppermute | solution.py:402
  19.3 23.8 %collective-permute-start.5 = (bf16[768,768]{1,0:T(8,128)(2,1)S(1)}, bf16[768,768]{1,0:T(8,128)(2,1)}, u32[]{:S(2)}, u32[]{:S(2)}) collective-permute-start(bf16[768,768]{1,0:T(8,128)(2,1)S(1)} %get-tuple-element.25.refs_1_), channel_id=1, source_target_pairs={{0,4},{1,5},{2,6},{3,7},{4,0},{5,1},{6,2},{7,3},{8,12},{9,13},{10,... | collective-permute-start | bytes 3538952 | tf_op jit(solution)/shard_map/raw_a_across_rows_1/ppermute | solution.py:402
  20.9 25.4 %collective-permute-start.7 = (bf16[768,768]{1,0:T(8,128)(2,1)S(1)}, bf16[768,768]{1,0:T(8,128)(2,1)}, u32[]{:S(2)}, u32[]{:S(2)}) collective-permute-start(bf16[768,768]{1,0:T(8,128)(2,1)S(1)} %get-tuple-element.27.refs_0_), channel_id=1, source_target_pairs={{0,2},{1,3},{4,6},{5,7},{8,10},{9,11},{12,14},{13,15},{18,16},{19,... | collective-permute-start | bytes 3538952 | tf_op jit(solution)/shard_map/raw_a_beside/ppermute | solution.py:402
  23.8 4.9 %copy-start.11 = (s32[2,5]{1,0:T(2,128)}, s32[2,5]{1,0:T(2,128)S(1)}, u32[]{:S(2)}) copy-start(s32[2,5]{1,0:T(2,128)S(1)} %add_multiply_fusion.corner) | copy-start | bytes 124
  23.9 1.3 collective-permute-start.4
  39.3 32.3 %collective-permute-start.9 = (bf16[768,768]{1,0:T(8,128)(2,1)}, bf16[768,768]{1,0:T(8,128)(2,1)}, u32[]{:S(2)}, u32[]{:S(2)}) collective-permute-start(bf16[768,768]{1,0:T(8,128)(2,1)} %get-tuple-element.32.refs_1_.refs_3_.refs_0_), channel_id=1, source_target_pairs={{0,2},{1,3},{4,6},{5,7},{8,10},{9,11},{12,14},{13,15},{18,16},{19,... | collective-permute-start | bytes 3538952 | tf_op jit(solution)/shard_map/density_b_beside/ppermute | solution.py:402
  40.6 34.0 %collective-permute-start.10 = (bf16[768,768]{1,0:T(8,128)(2,1)}, bf16[768,768]{1,0:T(8,128)(2,1)S(1)}, u32[]{:S(2)}, u32[]{:S(2)}) collective-permute-start(bf16[768,768]{1,0:T(8,128)(2,1)} %get-tuple-element.24.refs_3_.refs_0_.refs_2_), channel_id=1, source_target_pairs={{0,4},{1,5},{2,6},{3,7},{4,0},{5,1},{6,2},{7,3},{8,12},{9,13},{10,... | collective-permute-start | bytes 3538952 | tf_op jit(solution)/shard_map/density_b_across_rows_1/ppermute | solution.py:402
  46.3 28.3 %collective-permute-start.11 = (bf16[768,768]{1,0:T(8,128)(2,1)}, bf16[768,768]{1,0:T(8,128)(2,1)S(1)}, u32[]{:S(2)}, u32[]{:S(2)}) collective-permute-start(bf16[768,768]{1,0:T(8,128)(2,1)} %get-tuple-element.32.refs_1_.refs_3_.refs_0_), channel_id=1, source_target_pairs={{0,8},{1,9},{2,10},{3,11},{4,12},{5,13},{6,14},{7,15},{8,0},{9,1},... | collective-permute-start | bytes 3538952 | tf_op jit(solution)/shard_map/density_b_across_rows_2/ppermute | solution.py:402
  50.1 21.5 %copy-start = (bf16[768,768]{1,0:T(8,128)(2,1)S(1)}, bf16[768,768]{1,0:T(8,128)(2,1)}, u32[]{:S(2)}) copy-start(bf16[768,768]{1,0:T(8,128)(2,1)} %get-tuple-element.32.refs_1_.refs_3_.refs_0_) | copy-start | bytes 3538948
  62.2 10.8 %copy-start.10 = (bf16[768,768]{1,0:T(8,128)(2,1)S(1)}, bf16[768,768]{1,0:T(8,128)(2,1)}, u32[]{:S(2)}) copy-start(bf16[768,768]{1,0:T(8,128)(2,1)} %get-tuple-element.30) | copy-start | bytes 3538948
  73.0 3.0 %copy-start.3 = (bf16[768,768]{1,0:T(8,128)(2,1)S(1)}, bf16[768,768]{1,0:T(8,128)(2,1)}, u32[]{:S(2)}) copy-start(bf16[768,768]{1,0:T(8,128)(2,1)} %get-tuple-element.28.refs_4_.refs_6_.refs_1_) | copy-start | bytes 3538948
  74.6 2.1 copy-start.7
  74.6 2.1 copy-start.5
  74.6 28.8 %collective-permute-start.12 = (bf16[2,768,768]{2,1,0:T(8,128)(2,1)}, bf16[2,768,768]{2,1,0:T(8,128)(2,1)}, u32[]{:S(2)}, u32[]{:S(2)}) collective-permute-start(bf16[2,768,768]{2,1,0:T(8,128)(2,1)} %pad_maximum_fusion.refs_4_), channel_id=1, source_target_pairs={{0,1},{1,0},{2,3},{3,2},{4,5},{5,4},{6,7},{7,6},{8,9},{9,8},{10,11... | collective-permute-start | bytes 7077896 | tf_op jit(solution)/shard_map/wide_across_cores/ppermute | solution.py:402
  74.8 28.6 %collective-permute-start.13 = (bf16[768,768]{1,0:T(8,128)(2,1)}, bf16[768,768]{1,0:T(8,128)(2,1)}, u32[]{:S(2)}, u32[]{:S(2)}) collective-permute-start(bf16[768,768]{1,0:T(8,128)(2,1)} %get-tuple-element.29.refs_2_), channel_id=1, source_target_pairs={{0,4},{1,5},{2,6},{3,7},{4,0},{5,1},{6,2},{7,3},{8,12},{9,13},{10,... | collective-permute-start | bytes 3538952 | tf_op jit(solution)/shard_map/forward_b_across_rows_1/ppermute | solution.py:402
  76.0 39.9 %collective-permute-start.8 = (bf16[768,768]{1,0:T(8,128)(2,1)S(1)}, bf16[768,768]{1,0:T(8,128)(2,1)}, u32[]{:S(2)}, u32[]{:S(2)}) collective-permute-start(bf16[768,768]{1,0:T(8,128)(2,1)S(1)} %copy-done.3), channel_id=1, source_target_pairs={{0,8},{1,9},{2,10},{3,11},{4,12},{5,13},{6,14},{7,15},{8,0},{9,1},... | collective-permute-start | bytes 3538952 | tf_op jit(solution)/shard_map/forward_a_across_rows_2/ppermute | solution.py:402
  85.2 29.2 %copy-start.1 = (bf16[2,768,768]{2,1,0:T(8,128)(2,1)S(1)}, bf16[2,768,768]{2,1,0:T(8,128)(2,1)}, u32[]{:S(2)}) copy-start(bf16[2,768,768]{2,1,0:T(8,128)(2,1)} %far_0_1.1.refs_6_) | copy-start | bytes 7077892
  111.6 27.1 %collective-permute-start.16 = (bf16[768,768]{1,0:T(8,128)(2,1)}, bf16[768,768]{1,0:T(8,128)(2,1)}, u32[]{:S(2)}, u32[]{:S(2)}) collective-permute-start(bf16[768,768]{1,0:T(8,128)(2,1)} %get-tuple-element.36), channel_id=1, source_target_pairs={{2,0},{3,1},{6,4},{7,5},{10,8},{11,9},{14,12},{15,13},{16,18},{17,... | collective-permute-start | bytes 3538952 | tf_op jit(solution)/shard_map/near_1_beside/ppermute | solution.py:402
  114.4 25.8 %collective-permute-start.14 = (bf16[2,768,768]{2,1,0:T(8,128)(2,1)S(1)}, bf16[2,768,768]{2,1,0:T(8,128)(2,1)}, u32[]{:S(2)}, u32[]{:S(2)}) collective-permute-start(bf16[2,768,768]{2,1,0:T(8,128)(2,1)S(1)} %copy-done.1), channel_id=1, source_target_pairs={{3,2},{7,6},{10,11},{14,15},{17,16},{21,20},{24,25},{28,29}} | collective-permute-start | bytes 7077896 | tf_op jit(solution)/shard_map/far_0_1_across_cores/ppermute | solution.py:402
  138.8 7.9 %collective-permute-start.17 = (bf16[2,768,768]{2,1,0:T(8,128)(2,1)}, bf16[2,768,768]{2,1,0:T(8,128)(2,1)S(1)}, u32[]{:S(2)}, u32[]{:S(2)}) collective-permute-start(bf16[2,768,768]{2,1,0:T(8,128)(2,1)} %far_2_3.1), channel_id=1, source_target_pairs={{2,3},{6,7},{11,10},{15,14},{16,17},{20,21},{25,24},{29,28}} | collective-permute-start | bytes 7077896 | tf_op jit(solution)/shard_map/far_2_3_across_cores/ppermute | solution.py:402
  140.2 6.5 %copy-start.4 = (bf16[2,768,768]{2,1,0:T(8,128)(2,1)S(1)}, bf16[2,768,768]{2,1,0:T(8,128)(2,1)}, u32[]{:S(2)}) copy-start(bf16[2,768,768]{2,1,0:T(8,128)(2,1)} %far_2_3.1) | copy-start | bytes 7077892
  142.6 6.8 %copy-start.12 = (bf16[768,768]{1,0:T(8,128)(2,1)S(1)}, bf16[768,768]{1,0:T(8,128)(2,1)}, u32[]{:S(2)}) copy-start(bf16[768,768]{1,0:T(8,128)(2,1)} %get-tuple-element.38) | copy-start | bytes 3538948
  142.6 62.8 %collective-permute-start.15 = (bf16[2,768,768]{2,1,0:T(8,128)(2,1)S(1)}, bf16[2,768,768]{2,1,0:T(8,128)(2,1)S(1)}, u32[]{:S(2)}, u32[]{:S(2)}) collective-permute-start(bf16[2,768,768]{2,1,0:T(8,128)(2,1)S(1)} %add_convert_fusion.1), channel_id=1, source_target_pairs={{2,0},{6,4},{11,9},{15,13},{16,18},{20,22},{25,27},{29,31}} | collective-permute-start | bytes 7077896 | tf_op jit(solution)/shard_map/far_0_1_beside/ppermute | solution.py:402
  147.3 62.4 %collective-permute-start.18 = (bf16[2,768,768]{2,1,0:T(8,128)(2,1)S(1)}, bf16[2,768,768]{2,1,0:T(8,128)(2,1)}, u32[]{:S(2)}, u32[]{:S(2)}) collective-permute-start(bf16[2,768,768]{2,1,0:T(8,128)(2,1)S(1)} %add_convert_fusion), channel_id=1, source_target_pairs={{3,1},{7,5},{10,8},{14,12},{17,19},{21,23},{24,26},{28,30}} | collective-permute-start | bytes 7077896 | tf_op jit(solution)/shard_map/far_2_3_beside/ppermute | solution.py:402
  149.4 56.0 %collective-permute-start.19 = (bf16[768,768]{1,0:T(8,128)(2,1)S(1)}, bf16[768,768]{1,0:T(8,128)(2,1)S(1)}, u32[]{:S(2)}, u32[]{:S(2)}) collective-permute-start(bf16[768,768]{1,0:T(8,128)(2,1)S(1)} %copy-done.12), channel_id=1, source_target_pairs={{2,16},{3,24},{6,20},{7,28},{10,17},{11,25},{14,21},{15,29},{16,2}... | collective-permute-start | bytes 3538952 | tf_op jit(solution)/shard_map/near_0_direct/ppermute | solution.py:402
  154.6 55.1 %collective-permute-start.20 = (bf16[768,768]{1,0:T(8,128)(2,1)}, bf16[768,768]{1,0:T(8,128)(2,1)}, u32[]{:S(2)}, u32[]{:S(2)}) collective-permute-start(bf16[768,768]{1,0:T(8,128)(2,1)} %collective-permute-done.16), channel_id=1, source_target_pairs={{0,20},{1,28},{4,16},{5,24},{8,21},{9,29},{12,17},{13,25},{18,6},{... | collective-permute-start | bytes 3538952 | tf_op jit(solution)/shard_map/near_1_ahead/ppermute | solution.py:402
  205.4 4.3 %copy-start.9 = (bf16[768,768]{1,0:T(8,128)(2,1)}, bf16[768,768]{1,0:T(8,128)(2,1)S(1)}, u32[]{:S(2)}) copy-start(bf16[768,768]{1,0:T(8,128)(2,1)S(1)} %collective-permute-done.19.refs_4_) | copy-start | bytes 3538948
  205.4 4.3 %copy-start.8 = (bf16[2,768,768]{2,1,0:T(8,128)(2,1)}, bf16[2,768,768]{2,1,0:T(8,128)(2,1)S(1)}, u32[]{:S(2)}) copy-start(bf16[2,768,768]{2,1,0:T(8,128)(2,1)S(1)} %collective-permute-done.15.refs_2_) | copy-start | bytes 7077892

commit v3 on v2

--- a/solution.py
+++ b/solution.py
@@ -10,7 +10,7 @@
 ORB = 128
 NR = 16
 AXES = ("row", "col")
-VMEM_BYTES = 60 * 1024 * 1024
+VMEM_BYTES = 127 * 512 * 1024
 EDGE_CHUNK = 256
 BYTES_PER_US = 1_500_000
 STEPS = ((0,), 1, 0, (1,))
@@ -18,7 +18,7 @@
 PLAN = {
     'density_b_across_rows_2': ('raw_a_across_rows_1', 'raw_a_across_rows_2', 'raw_a_beside'),
     'far_2_3_across_cores': ('near_1_beside',),
-    'wide_across_cores': ('density_b_across_rows_1', 'density_b_across_rows_2'),
+    'wide_b_across_cores': ('density_b_across_rows_1', 'density_b_across_rows_2'),
 }
 
 
@@ -82,14 +82,17 @@
             hits[chunk, cell : cell + 1, :] = codes.astype(jnp.int32)
 
 
-def prepare(edges, corner, atoms, atoms_total):
-    count = edges.shape[1]
-    chunks = max(1, count // EDGE_CHUNK)
+def cell_table(corner):
     cells = corner.shape[1]
     once = jnp.concatenate([corner, jnp.zeros((1, cells), jnp.int32), jnp.ones((1, cells), jnp.int32)])
     twice = jnp.concatenate([corner, jnp.ones((2, cells), jnp.int32)])
     table = jnp.concatenate([once, twice], axis=1).astype(jnp.float32)
-    table = jnp.pad(table, ((0, 4), (0, ORB - 2 * cells)))
+    return jnp.pad(table, ((0, 4), (0, ORB - 2 * cells)))
+
+
+def prepare(edges, table, cells, atoms, atoms_total):
+    count = edges.shape[1]
+    chunks = max(1, count // EDGE_CHUNK)
     return pl.pallas_call(
         functools.partial(prepare_kernel, cells, chunks, atoms, atoms_total),
         out_shape=[
@@ -225,7 +228,7 @@
     count = len(sides)
     refs = list(refs)
     tall = [refs.pop(0) for _ in range(count)]
-    wide = [refs.pop(0) for _ in range(sources)]
+    wide = [[refs.pop(0) for _ in range(sources)] for _ in range(2)]
     seed = refs.pop(0) if seeded else None
     refs = refs[unread:]
     total = refs.pop(0)
@@ -237,10 +240,10 @@
 
             @pl.when(source[n] == s)
             def _():
-                pltpu.make_async_copy(wide[s].at[sides[n]], wide_in.at[n], sems.at[n, 0]).start()
+                pltpu.make_async_copy(wide[sides[n]][s], wide_in.at[n], sems.at[n, 0]).start()
 
         here = [
-            pltpu.make_async_copy(wide[0].at[sides[n]], wide_in.at[n], sems.at[n, 0]),
+            pltpu.make_async_copy(wide[sides[n]][0], wide_in.at[n], sems.at[n, 0]),
             pltpu.make_async_copy(tall[n], tall_in.at[n], sems.at[n, 1]),
         ]
         here[1].start()
@@ -258,10 +261,10 @@
 
 def near_share(source, tall, sides, wide, seed, last, sooner):
     cell = tall[0].shape
-    sources = len(wide)
+    sources = len(wide[0])
     count = len(tall)
     any_spec = pl.BlockSpec(memory_space=pl.ANY)
-    operands = [source, *tall, *wide]
+    operands = [source, *tall, *wide[0], *wide[1]]
     if seed is not None:
         operands.append(seed)
     operands += sooner
@@ -319,10 +322,10 @@
     )(*own, *tall, *sooner)
 
 
-def final_kernel(groups, pieces, slot, *refs):
+def final_kernel(parts, pieces, slot, *refs):
     refs = list(refs)
     near = [refs.pop(0) for _ in range(2)]
-    far = [refs.pop(0) for _ in range(groups)]
+    far = [[refs.pop(0) for _ in range(n)] for n in parts]
     opposite = [[refs.pop(0) for _ in range(n)] for n in pieces]
     out = refs.pop(0)
     turn = pl.program_id(0)
@@ -340,7 +343,8 @@
                     to = pl.ds(start, rows)
                     value = near[q][at, to]
                     for share in far:
-                        value = value + share[q, at, to].astype(jnp.float32)
+                        part = share[q][0, at, to] if len(share) == 2 else share[0][q, at, to]
+                        value = value + part.astype(jnp.float32)
                     out[at, to] = value + piece[:, at].astype(jnp.float32).T
                     return 0
 
@@ -350,9 +354,9 @@
 
 def final_sum(slot, near, far, opposite):
     side = near[0].shape[0]
-    operands = [*near, *far, *opposite[0], *opposite[1]]
+    operands = [*near, *[part for share in far for part in share], *opposite[0], *opposite[1]]
     return pl.pallas_call(
-        functools.partial(final_kernel, len(far), [len(pieces) for pieces in opposite]),
+        functools.partial(final_kernel, [len(share) for share in far], [len(pieces) for pieces in opposite]),
         out_shape=jax.ShapeDtypeStruct((side, 2 * side), jnp.float32),
         grid_spec=pltpu.PrefetchScalarGridSpec(
             num_scalar_prefetch=1,
@@ -412,6 +416,17 @@
     singles = [1 << b for b in range(half_rows.bit_length() - 1)]
     others = [m for m in range(1, half_rows) if m & (m - 1)]
 
+    span = upper_bound[0] - lower_bound[0]
+    scale = jnp.stack([upper_bound[0] / span, 1.0 / span])
+
+    def tall_corner(mask, q):
+        return row_half * half_rows + (row_in ^ mask), 2 * col + slots[q]
+
+    corners = [tall_corner(0, q) for q in range(2)] + [tall_corner(m, 0) for m in singles]
+    corners += [(row, row_half * half_rows + 2 * col_in + slots[0])]
+    corner = jnp.stack([jnp.stack([c[n] for c in corners]) for n in range(2)]).astype(jnp.int32) * atoms
+    table = cell_table(corner)
+
     edges = jnp.concatenate(
         [edge_vec, edge_atoms.astype(jnp.float32), jnp.zeros((3, edge_vec.shape[1]), jnp.float32)], axis=0
     )
@@ -425,6 +440,7 @@
     while bit > col_size:
         edges = double(edges, bit)
         bit //= 2
+        edges = after(edges, *((raw[0], raw[1]) if bit == col_size else (table, scale, corner)))
     for mask in singles[1:]:
         raw_a[mask] = swap_rows(after(raw[0], edges), mask, "raw_a")
     edges = double(edges, col_size)
@@ -438,20 +454,11 @@
         edges = double(edges, bit)
         bit //= 2
 
-    span = upper_bound[0] - lower_bound[0]
-    scale = jnp.stack([upper_bound[0] / span, 1.0 / span])
-
     done = []
     sums = []
     beside = []
 
-    def tall_corner(mask, q):
-        return row_half * half_rows + (row_in ^ mask), 2 * col + slots[q]
-
-    corners = [tall_corner(0, q) for q in range(2)] + [tall_corner(m, 0) for m in singles]
-    corners += [(row, row_half * half_rows + 2 * col_in + slots[0])]
-    corner = jnp.stack([jnp.stack([c[n] for c in corners]) for n in range(2)]).astype(jnp.int32) * atoms
-    coefficient, hits = prepare(edges, corner, atoms, atoms * row_size)
+    coefficient, hits = prepare(edges, table, len(corners), atoms, atoms * row_size)
 
     def density(cells, at):
         what = f"density_{at}"
@@ -463,7 +470,8 @@
     tall = {mask: [None, None] for mask in range(half_rows)}
     def near_part(q):
         what = f"near_{q}"
-        source = jnp.stack([(row_in // 2) ^ col_in ^ (m // 2) for m in range(half_rows)]).astype(jnp.int32)
+        place = after((row_in // 2) ^ col_in, *waits(what + "_source"))
+        source = jnp.stack([place ^ (m // 2) for m in range(half_rows)]).astype(jnp.int32)
         sides = tuple(m % 2 for m in range(half_rows))
         with jax.named_scope(what):
             got = near_share(source, [tall[m][q] for m in tall], sides, wide, None, True, [*done[-1:], *waits(what)])
@@ -490,11 +498,11 @@
                 what + "_across_cores",
             )
             summed = summed + arrived.astype(jnp.float32)
-        return send(
-            summed.astype(jnp.bfloat16),
-            lambda h, i, y, k: (h, i, 1 - y, k) if h != y and k == owner(i) else None,
-            what + "_beside",
-        )
+        across = lambda h, i, y, k: (h, i, 1 - y, k) if h != y and k == owner(i) else None
+        summed = summed.astype(jnp.bfloat16)
+        if masks[0] == 0:
+            return [send(summed, across, f"{what}_beside")]
+        return [send(summed[n : n + 1], across, f"{what}_beside_{n}") for n in range(2)]
 
     tall[0] = density(raw, 0)
     own = tall[0]
@@ -506,9 +514,11 @@
     got = density([raw_a[m] for m in singles] + [mine_a], 2)
     for mask, value in zip(singles, got):
         tall[mask][0] = value
-    wide = [jnp.stack([got[len(singles)], jnp.where(on_diagonal, own[1], beside_b)])]
-    for turn in range(1, half_cols):
-        wide.append(send(wide[0], lambda h, i, y, k: (h, i, y, k ^ turn), "wide_across_cores"))
+    wide = [[got[len(singles)]], [jnp.where(on_diagonal, own[1], beside_b)]]
+    for group, name in zip(wide, ("a", "b")):
+        for turn in range(1, half_cols):
+            across = lambda h, i, y, k: (h, i, y, k ^ turn)
+            group.append(send(group[0], across, f"wide_{name}_across_cores"))
     for mask in others:
         bit = 1 if mask ^ 1 in singles else mask & ~1 & -(mask & ~1)
         tall[mask][1] = swap_rows(tall[mask ^ bit][0 if bit == 1 else 1], bit, "forward_b")

time: 218 us -> 208 us (0.954)
  waiting for transfers between devices: 98.5 us -> 83.3 us
  local copies, waits for them, and re-layouts: 3.35 us -> 6.13 us
  starting transfers between devices: 34.1 us -> 36.3 us
    ppermute x16 -> x18, waiting for transfers between devices: 92.4 us -> 78.8 us  [send(): made[what] = lax.ppermute(after(value, *waits(what)), AXES, moves(where))]
    another operation x3 -> x1, other arithmetic: 3.63 us -> 0.62 us  [near_part(): jnp.stack([place ^ m // 2 for m in range(half_rows)]).astype(jnp.int32)]
    select_n x0 -> x1, other arithmetic: none -> 2.43 us  [shards(): wide = [[got[len(singles)]], [jnp.where(on_diagonal, own[1], beside_b)]]]
    ppermute x16 -> x18, starting transfers between devices: 28.2 us -> 30 us  [send(): made[what] = lax.ppermute(after(value, *waits(what)), AXES, moves(where))]
  transfers between devices with their start and end apart: 21 -> 23, of which waited for: 11 -> 11; matrix products, arithmetic and copies ran while one was open for 6% -> 7% of each run, Pallas kernels for 27% -> 28%
where the time goes in v3:
time: 208 us; the launch traced here: 207 us
  waiting for transfers between devices  83.3 us (40%)
  Pallas kernels  66.3 us (32%)
  starting transfers between devices  36.3 us (17%)
  other arithmetic  13.5 us (6%)
  local copies, waits for them, and re-layouts  6.13 us (3%)
    ppermute x18, waiting for transfers between devices, send(): made[what] = lax.ppermute(after(value, *waits(what)), AXES, moves(where))  78.8 us
    ppermute x18, starting transfers between devices, send(): made[what] = lax.ppermute(after(value, *waits(what)), AXES, moves(where))  30 us
    pallas_call x2, Pallas kernels, densities(): pl.pallas_call(functools.partial(density_kernel, chunks, cells, len(soone...  22.6 us
    pallas_call x2, Pallas kernels, near_share(): pl.pallas_call(functools.partial(near_kernel, sides, sources, seed is not...  16.5 us
    pallas_call x2, Pallas kernels, far_share(): pl.pallas_call(functools.partial(far_kernel, count, len(sooner)), out_sha...  16.3 us
    pallas_call x1, Pallas kernels, final_sum(): pl.pallas_call(functools.partial(final_kernel, [len(share) for share in f...  8.18 us
    ppermute x5, starting transfers between devices, double(): arrived = lax.ppermute(value, AXES, [(d, d ^ bit) for d in range(devices)])  6.23 us
    ppermute x5, waiting for transfers between devices, double(): arrived = lax.ppermute(value, AXES, [(d, d ^ bit) for d in range(devices)])  4.43 us
  transfers between devices with their start and end apart: 23, of which 11 were waited for; matrix products, arithmetic and copies ran while one was open for 7% of the time, Pallas kernels for 28%

profile of v3, /device:TPU:4, one launch (start us, length us, event | category | flops | bytes accessed | tf_op | source)
XLA Modules:
  0.0 207.2 jit_solution(7573484835580102414)
XLA Ops:
  0.0 0.7 convert_element_type.26
  0.7 0.7 pad_maximum_fusion.1
  1.4 2.6 %collective-permute-start = (f32[8,8]{1,0:T(8,128)S(1)}, f32[8,8]{1,0:T(8,128)S(1)}, u32[]{:S(2)}, u32[]{:S(2)}) collective-permute-start(f32[8,8]{1,0:T(8,128)S(1)} %pad_maximum_fusion.1), channel_id=1, source_target_pairs={{0,16},{1,17},{2,18},{3,19},{4,20},{5,21},{6,22},{7,23},{8,24},{9,... | collective-permute-start | bytes 776 | tf_op jit(solution)/shard_map/ppermute | solution.py:436
  5.3 0.6 pad_maximum_fusion.6.scale
  6.9 0.8 pad_maximum_fusion.2
  7.6 1.6 collective-permute-start.1
  9.2 3.2 %constant_dynamic-slice_fusion = (bf16[768,768]{1,0:T(8,128)(2,1)}, bf16[768,768]{1,0:T(8,128)(2,1)}) fusion(bf16[768,1536]{1,0:T(8,128)(2,1)} %param.9, s32[]{:T(128)S(6)} %select_n.52, s32[]{:T(128)S(6)} %select_n.51), kind=kLoop, calls=%fused_computation.17 | loop fusion | bytes 4718600 | tf_op jit(solution)/shard_map/dynamic_slice | solution.py:415
  12.5 1.5 collective-permute-start.2
  14.0 2.1 %collective-permute-done.2 = f32[8,32]{1,0:T(8,128)S(1)} collective-permute-done((f32[8,32]{1,0:T(8,128)S(1)}, f32[8,32]{1,0:T(8,128)S(1)}, u32[]{:S(2)}, u32[]{:S(2)}) %collective-permute-start.2) | collective-permute-done | bytes 1056 | tf_op jit(solution)/shard_map/ppermute | solution.py:436
  17.1 1.5 collective-permute-start.5
  18.6 1.2 collective-permute-done.3
  19.8 1.3 collective-permute-start.7
  21.2 1.2 collective-permute-done.4
  22.4 0.7 pad_maximum_fusion.edges
  23.0 2.8 %shard_map.64 = (bf16[256,144]{1,0:T(8,128)(2,1)}, s32[1,5,128]{2,1,0:T(8,128)}) custom-call(f32[8,256]{1,0:T(8,128)} %pad_maximum_fusion.edges, f32[8,128]{1,0:T(8,128)} %pad.5.corner), custom_call_target="tpu_custom_call" | custom-call | bytes 4500000 | tf_op jit(solution)/shard_map/pallas_call | solution.py:96
  25.8 10.7 %density_0.1 = (bf16[768,768]{1,0:T(8,128)(2,1)}, bf16[768,768]{1,0:T(8,128)(2,1)}) custom-call(s32[1,5,128]{2,1,0:T(8,128)} %get-tuple-element.26.hits, f32[2]{0:T(128)} %pad_maximum_fusion.6.scale, s32[2,5]{1,0:T(2,128)} %copy-done.4, bf16[256,144]{1,0:T(8,128)(2,1)} %get-tuple-element.27.coefficient, bf16[144,16384]{1,0:T(8,128)(2,1)} %weight.3, ...), custom_call_target="tpu_custom_call" | custom-call | bytes 16500000 | tf_op jit(solution)/shard_map/density_0/pallas_call | solution.py:198
  36.5 1.3 collective-permute-start.10
  37.8 2.0 collective-permute-start.11
  39.8 2.9 %collective-permute-done.6.refs_1_ = bf16[768,768]{1,0:T(8,128)(2,1)} collective-permute-done((bf16[768,768]{1,0:T(8,128)(2,1)}, bf16[768,768]{1,0:T(8,128)(2,1)}, u32[]{:S(2)}, u32[]{:S(2)}) %collective-permute-start.6) | collective-permute-done | bytes 1179680 | tf_op jit(solution)/shard_map/raw_a_across_rows_2/ppermute | solution.py:406
  42.7 2.0 collective-permute-done.5.refs_0_
  44.7 6.3 %collective-permute-done.7 = bf16[768,768]{1,0:T(8,128)(2,1)} collective-permute-done((bf16[768,768]{1,0:T(8,128)(2,1)}, bf16[768,768]{1,0:T(8,128)(2,1)}, u32[]{:S(2)}, u32[]{:S(2)}) %collective-permute-start.7) | collective-permute-done | bytes 1179680 | tf_op jit(solution)/shard_map/raw_a_beside/ppermute | solution.py:406
  51.4 2.4 %broadcast_select_fusion.1.refs_2_ = bf16[768,768]{1,0:T(8,128)(2,1)} fusion(bf16[768,768]{1,0:T(8,128)(2,1)} %get-tuple-element.31.refs_0_, bf16[768,768]{1,0:T(8,128)(2,1)} %collective-permute-done.7, pred[]{:T(512)S(6)} %eq.8), kind=kLoop, calls=%fused_computation.3 | loop fusion | flops 589824 | bytes 3538945 | tf_op jit(solution)/shard_map/jit(_where)/select_n | solution.py:511
  53.8 11.9 %density_2.1 = (bf16[768,768]{1,0:T(8,128)(2,1)}, bf16[768,768]{1,0:T(8,128)(2,1)}, bf16[768,768]{1,0:T(8,128)(2,1)}) custom-call(s32[1,5,128]{2,1,0:T(8,128)} %get-tuple-element.26.hits, f32[2]{0:T(128)} %pad_maximum_fusion.6.scale, s32[2,5]{1,0:T(2,128)} %copy-done.4, bf16[256,144]{1,0:T(8,128)(2,1)} %get-tuple-element.27.coefficient, ...), custom_call_target="tpu_custom_call" | custom-call | bytes 20250000 | tf_op jit(solution)/shard_map/density_2/pallas_call | solution.py:198
  65.7 1.4 collective-permute-start.14
  67.1 5.0 %collective-permute-done.10 = bf16[768,768]{1,0:T(8,128)(2,1)} collective-permute-done((bf16[768,768]{1,0:T(8,128)(2,1)}, bf16[768,768]{1,0:T(8,128)(2,1)}, u32[]{:S(2)}, u32[]{:S(2)}) %collective-permute-start.10) | collective-permute-done | bytes 1179680 | tf_op jit(solution)/shard_map/density_b_beside/ppermute | solution.py:406
  72.2 2.4 %broadcast_select_fusion.refs_6_ = bf16[768,768]{1,0:T(8,128)(2,1)} fusion(bf16[768,768]{1,0:T(8,128)(2,1)} %get-tuple-element.36.refs_1_.refs_3_.refs_0_, bf16[768,768]{1,0:T(8,128)(2,1)} %collective-permute-done.10, pred[]{:T(512)S(6)} %eq.8), kind=kLoop, calls=%fused_computation.2 | loop fusion | flops 589824 | bytes 3538945 | tf_op jit(solution)/shard_map/jit(_where)/select_n | solution.py:517
  75.3 0.7 collective-permute-start.8
  76.0 8.5 %far_0_1.1.refs_8_ = bf16[2,768,768]{2,1,0:T(8,128)(2,1)} custom-call(bf16[768,768]{1,0:T(8,128)(2,1)} %get-tuple-element.28.refs_3_.refs_0_.refs_2_, bf16[768,768]{1,0:T(8,128)(2,1)} %get-tuple-element.36.refs_1_.refs_3_.refs_0_, bf16[768,768]{1,0:T(8,128)(2,1)} %get-tuple-element.28.refs_3_.refs_0_.refs_2_, ...), custom_call_target="tpu_custom_call" | custom-call | bytes 13500000 | tf_op jit(solution)/shard_map/far_0_1/pallas_call | solution.py:310
  84.5 8.9 %collective-permute-done.14.refs_3_.refs_5_ = bf16[768,768]{1,0:T(8,128)(2,1)} collective-permute-done((bf16[768,768]{1,0:T(8,128)(2,1)}, bf16[768,768]{1,0:T(8,128)(2,1)}, u32[]{:S(2)}, u32[]{:S(2)}) %collective-permute-start.14) | collective-permute-done | bytes 1179680 | tf_op jit(solution)/shard_map/forward_b_across_rows_1/ppermute | solution.py:406
  93.4 8.3 %near_1.1 = (f32[768,768]{1,0:T(8,128)}, bf16[768,768]{1,0:T(8,128)(2,1)}) custom-call(s32[4]{0:T(128)} %pad_add_fusion.1.source, bf16[768,768]{1,0:T(8,128)(2,1)} %get-tuple-element.36.refs_1_.refs_3_.refs_0_, bf16[768,768]{1,0:T(8,128)(2,1)} %collective-permute-done.11.refs_5_.refs_1_, bf16[768,768]{1,0:T(8,128)(2,1)} %collective-permute-done.12.refs_2_.refs_3_, ...), custom_call_target="tpu_custom_call" | custom-call | bytes 18000000 | tf_op jit(solution)/shard_map/near_1/pallas_call | solution.py:274
  101.7 5.4 %collective-permute-start.17 = (bf16[768,768]{1,0:T(8,128)(2,1)}, bf16[768,768]{1,0:T(8,128)(2,1)}, u32[]{:S(2)}, u32[]{:S(2)}) collective-permute-start(bf16[768,768]{1,0:T(8,128)(2,1)} %get-tuple-element.40), channel_id=1, source_target_pairs={{2,0},{3,1},{6,4},{7,5},{10,8},{11,9},{14,12},{15,13},{16,18},{17,... | collective-permute-start | bytes 3538952 | tf_op jit(solution)/shard_map/near_1_beside/ppermute | solution.py:406
  107.2 1.5 collective-permute-start.15
  108.7 8.3 %near_0.1 = (f32[768,768]{1,0:T(8,128)}, bf16[768,768]{1,0:T(8,128)(2,1)}) custom-call(s32[4]{0:T(128)} %pad_add_fusion.1.source, bf16[768,768]{1,0:T(8,128)(2,1)} %get-tuple-element.28.refs_3_.refs_0_.refs_2_, bf16[768,768]{1,0:T(8,128)(2,1)} %get-tuple-element.32.refs_4_.refs_6_.refs_1_, bf16[768,768]{1,0:T(8,128)(2,1)} %get-tuple-element.33.refs_2_, ...), custom_call_target="tpu_custom_call" | custom-call | bytes 18000000 | tf_op jit(solution)/shard_map/near_0/pallas_call | solution.py:274
  116.9 7.7 %far_2_3.1 = bf16[2,768,768]{2,1,0:T(8,128)(2,1)} custom-call(bf16[768,768]{1,0:T(8,128)(2,1)} %get-tuple-element.28.refs_3_.refs_0_.refs_2_, bf16[768,768]{1,0:T(8,128)(2,1)} %get-tuple-element.36.refs_1_.refs_3_.refs_0_, bf16[768,768]{1,0:T(8,128)(2,1)} %get-tuple-element.33.refs_2_, bf16[768,768]{1,0:T(8,128)(2,1)} %collective-permute-done.12.refs_2_.refs_3_, ...), custom_call_target="tpu_custom_call" | custom-call | bytes 13500000 | tf_op jit(solution)/shard_map/far_2_3/pallas_call | solution.py:310
  124.7 5.7 %collective-permute-done.17 = bf16[768,768]{1,0:T(8,128)(2,1)} collective-permute-done((bf16[768,768]{1,0:T(8,128)(2,1)}, bf16[768,768]{1,0:T(8,128)(2,1)}, u32[]{:S(2)}, u32[]{:S(2)}) %collective-permute-start.17) | collective-permute-done | bytes 1179680 | tf_op jit(solution)/shard_map/near_1_beside/ppermute | solution.py:406
  130.3 1.4 collective-permute-start.18
  131.8 3.1 %add_convert_fusion.1 = bf16[2,768,768]{2,1,0:T(8,128)(2,1)S(1)} fusion(bf16[2,768,768]{2,1,0:T(8,128)(2,1)} %collective-permute-done.15, bf16[2,768,768]{2,1,0:T(8,128)(2,1)} %far_0_1.1.refs_8_), kind=kLoop, calls=%fused_computation.1 | loop fusion | flops 4718592 | bytes 7077888 | tf_op jit(solution)/shard_map/convert_element_type | solution.py:502
  134.9 5.2 %collective-permute-start.16 = (bf16[2,768,768]{2,1,0:T(8,128)(2,1)S(1)}, bf16[2,768,768]{2,1,0:T(8,128)(2,1)}, u32[]{:S(2)}, u32[]{:S(2)}) collective-permute-start(bf16[2,768,768]{2,1,0:T(8,128)(2,1)S(1)} %add_convert_fusion.1), channel_id=1, source_target_pairs={{2,0},{6,4},{11,9},{15,13},{16,18},{20,22},{25,27},{29,31}} | collective-permute-start | bytes 7077896 | tf_op jit(solution)/shard_map/far_0_1_beside/ppermute | solution.py:406
  140.1 3.6 %collective-permute-start.21 = (bf16[768,768]{1,0:T(8,128)(2,1)S(1)}, bf16[768,768]{1,0:T(8,128)(2,1)S(1)}, u32[]{:S(2)}, u32[]{:S(2)}) collective-permute-start(bf16[768,768]{1,0:T(8,128)(2,1)S(1)} %copy-done.5), channel_id=1, source_target_pairs={{2,16},{3,24},{6,20},{7,28},{10,17},{11,25},{14,21},{15,29},{16,2}... | collective-permute-start | bytes 3538952 | tf_op jit(solution)/shard_map/near_0_direct/ppermute | solution.py:406
  143.7 1.3 collective-permute-start.22
  145.8 0.7 collective-permute-start.20
  146.5 1.8 collective-permute-start.19
  148.3 0.6 pad_add_fusion.slot
  148.9 44.2 %collective-permute-done.21.refs_5_ = bf16[768,768]{1,0:T(8,128)(2,1)S(1)} collective-permute-done((bf16[768,768]{1,0:T(8,128)(2,1)S(1)}, bf16[768,768]{1,0:T(8,128)(2,1)S(1)}, u32[]{:S(2)}, u32[]{:S(2)}) %collective-permute-start.21) | collective-permute-done | bytes 1179680 | tf_op jit(solution)/shard_map/near_0_direct/ppermute | solution.py:406
  193.1 3.9 %collective-permute-done.22.refs_6_ = bf16[768,768]{1,0:T(8,128)(2,1)S(1)} collective-permute-done((bf16[768,768]{1,0:T(8,128)(2,1)}, bf16[768,768]{1,0:T(8,128)(2,1)S(1)}, u32[]{:S(2)}, u32[]{:S(2)}) %collective-permute-start.22) | collective-permute-done | bytes 1179680 | tf_op jit(solution)/shard_map/near_1_ahead/ppermute | solution.py:406
  197.0 1.0 copy-done.2
  198.0 1.0 copy-done.3
  199.0 8.2 %shard_map.65 = f32[768,1536]{1,0:T(8,128)} custom-call(s32[2]{0:T(128)} %pad_add_fusion.slot, f32[768,768]{1,0:T(8,128)} %get-tuple-element.39.refs_6_.refs_0_, f32[768,768]{1,0:T(8,128)} %get-tuple-element.38.refs_8_.refs_1_, bf16[2,768,768]{2,1,0:T(8,128)(2,1)} %collective-permute-done.16.refs_2_, bf16[1,768,768]{2,1,0:T(8,128)(2,1)} %collective-permute-done.19.refs_3_, ...), custom_call_target="tpu_custom_call" | custom-call | bytes 13500000 | tf_op jit(solution)/shard_map/pallas_call | solution.py:358
  (42 shorter events, 3.9 us)
Async XLA Ops:
  1.4 5.5 %collective-permute-start = (f32[8,8]{1,0:T(8,128)S(1)}, f32[8,8]{1,0:T(8,128)S(1)}, u32[]{:S(2)}, u32[]{:S(2)}) collective-permute-start(f32[8,8]{1,0:T(8,128)S(1)} %pad_maximum_fusion.1), channel_id=1, source_target_pairs={{0,16},{1,17},{2,18},{3,19},{4,20},{5,21},{6,22},{7,23},{8,24},{9,... | collective-permute-start | bytes 776 | tf_op jit(solution)/shard_map/ppermute | solution.py:436
  6.2 6.2 %copy-start.4 = (s32[2,5]{1,0:T(2,128)}, s32[2,5]{1,0:T(2,128)S(1)}, u32[]{:S(2)}) copy-start(s32[2,5]{1,0:T(2,128)S(1)} %add_multiply_fusion.corner) | copy-start | bytes 124
  7.6 4.8 %collective-permute-start.1 = (f32[8,16]{1,0:T(8,128)S(1)}, f32[8,16]{1,0:T(8,128)S(1)}, u32[]{:S(2)}, u32[]{:S(2)}) collective-permute-start(f32[8,16]{1,0:T(8,128)S(1)} %pad_maximum_fusion.2), channel_id=1, source_target_pairs={{0,8},{1,9},{2,10},{3,11},{4,12},{5,13},{6,14},{7,15},{8,0},{9,1},... | collective-permute-start | bytes 1544 | tf_op jit(solution)/shard_map/ppermute | solution.py:436
  12.5 3.6 %collective-permute-start.2 = (f32[8,32]{1,0:T(8,128)S(1)}, f32[8,32]{1,0:T(8,128)S(1)}, u32[]{:S(2)}, u32[]{:S(2)}) collective-permute-start(f32[8,32]{1,0:T(8,128)S(1)} %pad_maximum_fusion.3), channel_id=1, source_target_pairs={{0,4},{1,5},{2,6},{3,7},{4,0},{5,1},{6,2},{7,3},{8,12},{9,13},{10,... | collective-permute-start | bytes 3080 | tf_op jit(solution)/shard_map/ppermute | solution.py:436
  16.2 3.6 %collective-permute-start.3 = (f32[8,64]{1,0:T(8,128)S(1)}, f32[8,64]{1,0:T(8,128)S(1)}, u32[]{:S(2)}, u32[]{:S(2)}) collective-permute-start(f32[8,64]{1,0:T(8,128)S(1)} %pad_maximum_fusion.4), channel_id=1, source_target_pairs={{0,2},{1,3},{2,0},{3,1},{4,6},{5,7},{6,4},{7,5},{8,10},{9,11},{10,... | collective-permute-start | bytes 6152 | tf_op jit(solution)/shard_map/ppermute | solution.py:436
  16.7 26.0 %collective-permute-start.6 = (bf16[768,768]{1,0:T(8,128)(2,1)}, bf16[768,768]{1,0:T(8,128)(2,1)}, u32[]{:S(2)}, u32[]{:S(2)}) collective-permute-start(bf16[768,768]{1,0:T(8,128)(2,1)} %get-tuple-element.31.refs_0_), channel_id=1, source_target_pairs={{0,8},{1,9},{2,10},{3,11},{4,12},{5,13},{6,14},{7,15},{8,0},{9,1},... | collective-permute-start | bytes 3538952 | tf_op jit(solution)/shard_map/raw_a_across_rows_2/ppermute | solution.py:406
  17.1 27.5 %collective-permute-start.5 = (bf16[768,768]{1,0:T(8,128)(2,1)}, bf16[768,768]{1,0:T(8,128)(2,1)}, u32[]{:S(2)}, u32[]{:S(2)}) collective-permute-start(bf16[768,768]{1,0:T(8,128)(2,1)} %get-tuple-element.29.refs_1_), channel_id=1, source_target_pairs={{0,4},{1,5},{2,6},{3,7},{4,0},{5,1},{6,2},{7,3},{8,12},{9,13},{10,... | collective-permute-start | bytes 3538952 | tf_op jit(solution)/shard_map/raw_a_across_rows_1/ppermute | solution.py:406
  19.8 31.1 %collective-permute-start.7 = (bf16[768,768]{1,0:T(8,128)(2,1)}, bf16[768,768]{1,0:T(8,128)(2,1)}, u32[]{:S(2)}, u32[]{:S(2)}) collective-permute-start(bf16[768,768]{1,0:T(8,128)(2,1)} %get-tuple-element.31.refs_0_), channel_id=1, source_target_pairs={{0,2},{1,3},{4,6},{5,7},{8,10},{9,11},{12,14},{13,15},{18,16},{19,... | collective-permute-start | bytes 3538952 | tf_op jit(solution)/shard_map/raw_a_beside/ppermute | solution.py:406
  21.1 1.2 collective-permute-start.4
  36.5 35.7 %collective-permute-start.10 = (bf16[768,768]{1,0:T(8,128)(2,1)}, bf16[768,768]{1,0:T(8,128)(2,1)}, u32[]{:S(2)}, u32[]{:S(2)}) collective-permute-start(bf16[768,768]{1,0:T(8,128)(2,1)} %get-tuple-element.36.refs_1_.refs_3_.refs_0_), channel_id=1, source_target_pairs={{0,2},{1,3},{4,6},{5,7},{8,10},{9,11},{12,14},{13,15},{18,16},{19,... | collective-permute-start | bytes 3538952 | tf_op jit(solution)/shard_map/density_b_beside/ppermute | solution.py:406
  37.8 36.8 %collective-permute-start.11 = (bf16[768,768]{1,0:T(8,128)(2,1)}, bf16[768,768]{1,0:T(8,128)(2,1)}, u32[]{:S(2)}, u32[]{:S(2)}) collective-permute-start(bf16[768,768]{1,0:T(8,128)(2,1)} %get-tuple-element.28.refs_3_.refs_0_.refs_2_), channel_id=1, source_target_pairs={{0,4},{1,5},{2,6},{3,7},{4,0},{5,1},{6,2},{7,3},{8,12},{9,13},{10,... | collective-permute-start | bytes 3538952 | tf_op jit(solution)/shard_map/density_b_across_rows_1/ppermute | solution.py:406
  51.0 23.7 %collective-permute-start.12 = (bf16[768,768]{1,0:T(8,128)(2,1)}, bf16[768,768]{1,0:T(8,128)(2,1)}, u32[]{:S(2)}, u32[]{:S(2)}) collective-permute-start(bf16[768,768]{1,0:T(8,128)(2,1)} %get-tuple-element.36.refs_1_.refs_3_.refs_0_), channel_id=1, source_target_pairs={{0,8},{1,9},{2,10},{3,11},{4,12},{5,13},{6,14},{7,15},{8,0},{9,1},... | collective-permute-start | bytes 3538952 | tf_op jit(solution)/shard_map/density_b_across_rows_2/ppermute | solution.py:406
  65.7 27.7 %collective-permute-start.14 = (bf16[768,768]{1,0:T(8,128)(2,1)}, bf16[768,768]{1,0:T(8,128)(2,1)}, u32[]{:S(2)}, u32[]{:S(2)}) collective-permute-start(bf16[768,768]{1,0:T(8,128)(2,1)} %get-tuple-element.33.refs_2_), channel_id=1, source_target_pairs={{0,4},{1,5},{2,6},{3,7},{4,0},{5,1},{6,2},{7,3},{8,12},{9,13},{10,... | collective-permute-start | bytes 3538952 | tf_op jit(solution)/shard_map/forward_b_across_rows_1/ppermute | solution.py:406
  67.1 26.3 %collective-permute-start.9 = (bf16[768,768]{1,0:T(8,128)(2,1)}, bf16[768,768]{1,0:T(8,128)(2,1)}, u32[]{:S(2)}, u32[]{:S(2)}) collective-permute-start(bf16[768,768]{1,0:T(8,128)(2,1)} %get-tuple-element.34.refs_4_), channel_id=1, source_target_pairs={{0,1},{1,0},{2,3},{3,2},{4,5},{5,4},{6,7},{7,6},{8,9},{9,8},{10,11... | collective-permute-start | bytes 3538952 | tf_op jit(solution)/shard_map/wide_a_across_cores/ppermute | solution.py:406
  74.6 18.8 %collective-permute-start.13 = (bf16[768,768]{1,0:T(8,128)(2,1)}, bf16[768,768]{1,0:T(8,128)(2,1)}, u32[]{:S(2)}, u32[]{:S(2)}) collective-permute-start(bf16[768,768]{1,0:T(8,128)(2,1)} %broadcast_select_fusion.refs_6_), channel_id=1, source_target_pairs={{0,1},{1,0},{2,3},{3,2},{4,5},{5,4},{6,7},{7,6},{8,9},{9,8},{10,11... | collective-permute-start | bytes 3538952 | tf_op jit(solution)/shard_map/wide_b_across_cores/ppermute | solution.py:406
  75.3 33.4 %collective-permute-start.8 = (bf16[768,768]{1,0:T(8,128)(2,1)}, bf16[768,768]{1,0:T(8,128)(2,1)}, u32[]{:S(2)}, u32[]{:S(2)}) collective-permute-start(bf16[768,768]{1,0:T(8,128)(2,1)} %get-tuple-element.32.refs_4_.refs_6_.refs_1_), channel_id=1, source_target_pairs={{0,8},{1,9},{2,10},{3,11},{4,12},{5,13},{6,14},{7,15},{8,0},{9,1},... | collective-permute-start | bytes 3538952 | tf_op jit(solution)/shard_map/forward_a_across_rows_2/ppermute | solution.py:406
  101.7 28.6 %collective-permute-start.17 = (bf16[768,768]{1,0:T(8,128)(2,1)}, bf16[768,768]{1,0:T(8,128)(2,1)}, u32[]{:S(2)}, u32[]{:S(2)}) collective-permute-start(bf16[768,768]{1,0:T(8,128)(2,1)} %get-tuple-element.40), channel_id=1, source_target_pairs={{2,0},{3,1},{6,4},{7,5},{10,8},{11,9},{14,12},{15,13},{16,18},{17,... | collective-permute-start | bytes 3538952 | tf_op jit(solution)/shard_map/near_1_beside/ppermute | solution.py:406
  107.2 24.6 %collective-permute-start.15 = (bf16[2,768,768]{2,1,0:T(8,128)(2,1)}, bf16[2,768,768]{2,1,0:T(8,128)(2,1)}, u32[]{:S(2)}, u32[]{:S(2)}) collective-permute-start(bf16[2,768,768]{2,1,0:T(8,128)(2,1)} %far_0_1.1.refs_8_), channel_id=1, source_target_pairs={{3,2},{7,6},{10,11},{14,15},{17,16},{21,20},{24,25},{28,29}} | collective-permute-start | bytes 7077896 | tf_op jit(solution)/shard_map/far_0_1_across_cores/ppermute | solution.py:406
  124.7 15.4 %copy-start.5 = (bf16[768,768]{1,0:T(8,128)(2,1)S(1)}, bf16[768,768]{1,0:T(8,128)(2,1)}, u32[]{:S(2)}) copy-start(bf16[768,768]{1,0:T(8,128)(2,1)} %get-tuple-element.42) | copy-start | bytes 3538948
  130.3 14.7 %collective-permute-start.18 = (bf16[2,768,768]{2,1,0:T(8,128)(2,1)}, bf16[2,768,768]{2,1,0:T(8,128)(2,1)S(1)}, u32[]{:S(2)}, u32[]{:S(2)}) collective-permute-start(bf16[2,768,768]{2,1,0:T(8,128)(2,1)} %far_2_3.1), channel_id=1, source_target_pairs={{2,3},{6,7},{11,10},{15,14},{16,17},{20,21},{25,24},{29,28}} | collective-permute-start | bytes 7077896 | tf_op jit(solution)/shard_map/far_2_3_across_cores/ppermute | solution.py:406
  131.8 13.2 %copy-start = (bf16[2,768,768]{2,1,0:T(8,128)(2,1)S(1)}, bf16[2,768,768]{2,1,0:T(8,128)(2,1)}, u32[]{:S(2)}) copy-start(bf16[2,768,768]{2,1,0:T(8,128)(2,1)} %far_2_3.1) | copy-start | bytes 7077892
  134.9 62.1 %collective-permute-start.16 = (bf16[2,768,768]{2,1,0:T(8,128)(2,1)S(1)}, bf16[2,768,768]{2,1,0:T(8,128)(2,1)}, u32[]{:S(2)}, u32[]{:S(2)}) collective-permute-start(bf16[2,768,768]{2,1,0:T(8,128)(2,1)S(1)} %add_convert_fusion.1), channel_id=1, source_target_pairs={{2,0},{6,4},{11,9},{15,13},{16,18},{20,22},{25,27},{29,31}} | collective-permute-start | bytes 7077896 | tf_op jit(solution)/shard_map/far_0_1_beside/ppermute | solution.py:406
  140.1 53.0 %collective-permute-start.21 = (bf16[768,768]{1,0:T(8,128)(2,1)S(1)}, bf16[768,768]{1,0:T(8,128)(2,1)S(1)}, u32[]{:S(2)}, u32[]{:S(2)}) collective-permute-start(bf16[768,768]{1,0:T(8,128)(2,1)S(1)} %copy-done.5), channel_id=1, source_target_pairs={{2,16},{3,24},{6,20},{7,28},{10,17},{11,25},{14,21},{15,29},{16,2}... | collective-permute-start | bytes 3538952 | tf_op jit(solution)/shard_map/near_0_direct/ppermute | solution.py:406
  143.7 53.3 %collective-permute-start.22 = (bf16[768,768]{1,0:T(8,128)(2,1)}, bf16[768,768]{1,0:T(8,128)(2,1)S(1)}, u32[]{:S(2)}, u32[]{:S(2)}) collective-permute-start(bf16[768,768]{1,0:T(8,128)(2,1)} %collective-permute-done.17), channel_id=1, source_target_pairs={{0,20},{1,28},{4,16},{5,24},{8,21},{9,29},{12,17},{13,25},{18,6},{... | collective-permute-start | bytes 3538952 | tf_op jit(solution)/shard_map/near_1_ahead/ppermute | solution.py:406
  145.8 51.2 %collective-permute-start.20 = (bf16[1,768,768]{2,1,0:T(8,128)(2,1)S(1)}, bf16[1,768,768]{2,1,0:T(8,128)(2,1)S(1)}, u32[]{:S(2)}, u32[]{:S(2)}) collective-permute-start(bf16[1,768,768]{2,1,0:T(8,128)(2,1)S(1)} %get-tuple-element.43), channel_id=1, source_target_pairs={{3,1},{7,5},{10,8},{14,12},{17,19},{21,23},{24,26},{28,30}} | collective-permute-start | bytes 3538952 | tf_op jit(solution)/shard_map/far_2_3_beside_1/ppermute | solution.py:406
  146.5 52.5 %collective-permute-start.19 = (bf16[1,768,768]{2,1,0:T(8,128)(2,1)S(1)}, bf16[1,768,768]{2,1,0:T(8,128)(2,1)}, u32[]{:S(2)}, u32[]{:S(2)}) collective-permute-start(bf16[1,768,768]{2,1,0:T(8,128)(2,1)S(1)} %get-tuple-element.44), channel_id=1, source_target_pairs={{3,1},{7,5},{10,8},{14,12},{17,19},{21,23},{24,26},{28,30}} | collective-permute-start | bytes 3538952 | tf_op jit(solution)/shard_map/far_2_3_beside_0/ppermute | solution.py:406
  193.1 3.9 %copy-start.1 = (bf16[768,768]{1,0:T(8,128)(2,1)}, bf16[768,768]{1,0:T(8,128)(2,1)S(1)}, u32[]{:S(2)}) copy-start(bf16[768,768]{1,0:T(8,128)(2,1)S(1)} %collective-permute-done.21.refs_5_) | copy-start | bytes 3538948
  197.0 1.0 copy-start.2
  198.0 1.0 copy-start.3

commit v4 on v3

--- a/solution.py
+++ b/solution.py
@@ -14,10 +14,10 @@
 EDGE_CHUNK = 256
 BYTES_PER_US = 1_500_000
 STEPS = ((0,), 1, 0, (1,))
-CUTS = (6, 0)
+CUTS = (6, 2)
 PLAN = {
     'density_b_across_rows_2': ('raw_a_across_rows_1', 'raw_a_across_rows_2', 'raw_a_beside'),
-    'far_2_3_across_cores': ('near_1_beside',),
+    'far_2_3_across_cores': ('near_1_beside', 'near_1_direct'),
     'wide_b_across_cores': ('density_b_across_rows_1', 'density_b_across_rows_2'),
 }
 
@@ -105,17 +105,25 @@
     )(edges, table)
 
 
-def density_kernel(chunks, cells, unread, base, hits, scale, corner, coefficient, weight, *refs):
-    raw = refs[:cells]
-    out = refs[cells + unread : 2 * cells + unread]
-    raw_in, total, ready, blocks, sems = refs[2 * cells + unread :]
+def density_kernel(chunks, sources, unread, base, hits, scale, corner, coefficient, weight, *refs):
+    cells = len(sources)
+    refs = list(refs)
+    raw = [[refs.pop(0) for _ in range(n)] for n in sources]
+    refs = refs[unread:]
+    out, (raw_in, total, ready, blocks, sems) = refs[:cells], refs[cells:]
     size = coefficient.shape[0] // chunks
     side = total.shape[0]
     wide = 8
     pitch = ORB + 8
-    copies = [pltpu.make_async_copy(raw[n], raw_in.at[n], sems.at[0, n]) for n in range(cells)]
-    for copy in copies:
-        copy.start()
+    copies = []
+    for n, refs_of in enumerate(raw):
+        ways = [pltpu.make_async_copy(ref, raw_in.at[n], sems.at[0, n]) for ref in refs_of]
+        copies.append(ways[0])
+        if len(ways) == 1:
+            ways[0].start()
+        else:
+            pl.when(scale[2] > 0.5)(ways[0].start)
+            pl.when(scale[2] < 0.5)(ways[1].start)
     inverse = scale[1]
 
     def expand(chunk):
@@ -191,16 +199,18 @@
 
 def densities(raw, base, corner, hits, scale, coefficient, weight, sooner):
     cells = len(raw)
+    sources = [len(refs) for refs in raw]
+    raw = [ref for refs in raw for ref in refs]
     side = raw[0].shape[0]
     edges = coefficient.shape[0]
     chunks = max(1, edges // EDGE_CHUNK)
     any_spec = pl.BlockSpec(memory_space=pl.ANY)
     return pl.pallas_call(
-        functools.partial(density_kernel, chunks, cells, len(sooner), base),
+        functools.partial(density_kernel, chunks, sources, len(sooner), base),
         out_shape=[jax.ShapeDtypeStruct((side, side), jnp.bfloat16)] * cells,
         in_specs=[pl.BlockSpec(memory_space=pltpu.SMEM)] * 3
         + [pl.BlockSpec(memory_space=pltpu.VMEM)] * 2
-        + [any_spec] * (cells + len(sooner)),
+        + [any_spec] * (len(raw) + len(sooner)),
         out_specs=[any_spec] * cells,
         scratch_shapes=[
             pltpu.VMEM((cells, side, side), jnp.bfloat16),
@@ -417,7 +427,7 @@
     others = [m for m in range(1, half_rows) if m & (m - 1)]
 
     span = upper_bound[0] - lower_bound[0]
-    scale = jnp.stack([upper_bound[0] / span, 1.0 / span])
+    scale = jnp.stack([upper_bound[0] / span, 1.0 / span, on_diagonal.astype(jnp.float32)])
 
     def tall_corner(mask, q):
         return row_half * half_rows + (row_in ^ mask), 2 * col + slots[q]
@@ -504,14 +514,13 @@
             return [send(summed, across, f"{what}_beside")]
         return [send(summed[n : n + 1], across, f"{what}_beside_{n}") for n in range(2)]
 
-    tall[0] = density(raw, 0)
+    tall[0] = density([[cell] for cell in raw], 0)
     own = tall[0]
     tall[1][1] = swap_rows(own[0], 1, "density_b")
     beside_b = to_beside(own[1], True, "density_b_beside")
-    mine_a = jnp.where(on_diagonal, raw[0], beside_a)
     for mask in singles[1:]:
         tall[mask][1] = swap_rows(own[1], mask, "density_b")
-    got = density([raw_a[m] for m in singles] + [mine_a], 2)
+    got = density([[raw_a[m]] for m in singles] + [[raw[0], beside_a]], 2)
     for mask, value in zip(singles, got):
         tall[mask][0] = value
     wide = [[got[len(singles)]], [jnp.where(on_diagonal, own[1], beside_b)]]

time: 208 us -> 207 us (level)
  local copies, waits for them, and re-layouts: 6.13 us -> 9.52 us
  waiting for transfers between devices: 83.3 us -> 80.4 us
  other arithmetic: 13.5 us -> 11.1 us
    slice x0 -> x2, local copies, waits for them, and re-layouts: none -> 3.1 us  [the longest x1 2.08 us: exchange(): ahead = to_beside(value[cut:], False, f'near_{turn}_beside')]
    ppermute x18 -> x19, waiting for transfers between devices: 78.8 us -> 75.9 us  [send(): made[what] = lax.ppermute(after(value, *waits(what)), AXES, moves(where))]
    select_n x1 -> x0, other arithmetic: 2.41 us -> none  [shards(): mine_a = jnp.where(on_diagonal, raw[0], beside_a)]
    ppermute x18 -> x19, starting transfers between devices: 30 us -> 30.4 us  [send(): made[what] = lax.ppermute(after(value, *waits(what)), AXES, moves(where))]
  transfers between devices with their start and end apart: 23 -> 24, of which waited for: 11 -> 10; matrix products, arithmetic and copies ran while one was open for 7% -> 8% of each run, Pallas kernels for 28% -> 28%
where the time goes in v4:
time: 207 us; the launch traced here: 206 us
  waiting for transfers between devices  80.4 us (39%)
  Pallas kernels  66.9 us (32%)
  starting transfers between devices  36.6 us (18%)
  other arithmetic  11.1 us (5%)
  local copies, waits for them, and re-layouts  9.52 us (5%)
    ppermute x19, waiting for transfers between devices, send(): made[what] = lax.ppermute(after(value, *waits(what)), AXES, moves(where))  75.9 us
    ppermute x19, starting transfers between devices, send(): made[what] = lax.ppermute(after(value, *waits(what)), AXES, moves(where))  30.4 us
    pallas_call x2, Pallas kernels, densities(): pl.pallas_call(functools.partial(density_kernel, chunks, sources, len(soo...  22.7 us
    pallas_call x2, Pallas kernels, near_share(): pl.pallas_call(functools.partial(near_kernel, sides, sources, seed is not...  16.6 us
    pallas_call x2, Pallas kernels, far_share(): pl.pallas_call(functools.partial(far_kernel, count, len(sooner)), out_sha...  16.2 us
    pallas_call x1, Pallas kernels, final_sum(): pl.pallas_call(functools.partial(final_kernel, [len(share) for share in f...  8.58 us
    ppermute x5, starting transfers between devices, double(): arrived = lax.ppermute(value, AXES, [(d, d ^ bit) for d in range(devices)])  6.23 us
    ppermute x5, waiting for transfers between devices, double(): arrived = lax.ppermute(value, AXES, [(d, d ^ bit) for d in range(devices)])  4.43 us
  transfers between devices with their start and end apart: 24, of which 10 were waited for; matrix products, arithmetic and copies ran while one was open for 8% of the time, Pallas kernels for 28%

profile of v4, /device:TPU:4, one launch (start us, length us, event | category | flops | bytes accessed | tf_op | source)
XLA Modules:
  0.0 206.1 jit_solution(3126695989770033123)
XLA Ops:
  0.0 0.7 convert_element_type.27
  0.7 0.7 pad_maximum_fusion.1
  1.4 2.6 %collective-permute-start = (f32[8,8]{1,0:T(8,128)S(1)}, f32[8,8]{1,0:T(8,128)S(1)}, u32[]{:S(2)}, u32[]{:S(2)}) collective-permute-start(f32[8,8]{1,0:T(8,128)S(1)} %pad_maximum_fusion.1), channel_id=1, source_target_pairs={{0,16},{1,17},{2,18},{3,19},{4,20},{5,21},{6,22},{7,23},{8,24},{9,... | collective-permute-start | bytes 776 | tf_op jit(solution)/shard_map/ppermute | solution.py:446
  5.5 0.7 pad_maximum_fusion.6.scale
  6.9 0.8 pad_maximum_fusion.2
  7.6 1.6 collective-permute-start.1
  9.2 3.2 %constant_dynamic-slice_fusion = (bf16[768,768]{1,0:T(8,128)(2,1)}, bf16[768,768]{1,0:T(8,128)(2,1)}) fusion(bf16[768,1536]{1,0:T(8,128)(2,1)} %param.9, s32[]{:T(128)S(6)} %select_n.49, s32[]{:T(128)S(6)} %select_n.48), kind=kLoop, calls=%fused_computation.16 | loop fusion | bytes 4718600 | tf_op jit(solution)/shard_map/dynamic_slice | solution.py:425
  12.5 1.5 collective-permute-start.2
  14.0 2.1 %collective-permute-done.2 = f32[8,32]{1,0:T(8,128)S(1)} collective-permute-done((f32[8,32]{1,0:T(8,128)S(1)}, f32[8,32]{1,0:T(8,128)S(1)}, u32[]{:S(2)}, u32[]{:S(2)}) %collective-permute-start.2) | collective-permute-done | bytes 1056 | tf_op jit(solution)/shard_map/ppermute | solution.py:446
  17.1 1.5 collective-permute-start.5
  18.6 1.2 collective-permute-done.3
  19.9 1.3 collective-permute-start.7
  21.2 1.2 collective-permute-done.4
  23.0 2.8 %shard_map.64 = (bf16[256,144]{1,0:T(8,128)(2,1)}, s32[1,5,128]{2,1,0:T(8,128)}) custom-call(f32[8,256]{1,0:T(8,128)} %pad_maximum_fusion.edges, f32[8,128]{1,0:T(8,128)} %pad.5.corner), custom_call_target="tpu_custom_call" | custom-call | bytes 4500000 | tf_op jit(solution)/shard_map/pallas_call | solution.py:96
  25.8 10.7 %density_0.1 = (bf16[768,768]{1,0:T(8,128)(2,1)}, bf16[768,768]{1,0:T(8,128)(2,1)}) custom-call(s32[1,5,128]{2,1,0:T(8,128)} %get-tuple-element.26.hits, f32[3]{0:T(128)} %pad_maximum_fusion.6.scale, s32[2,5]{1,0:T(2,128)} %copy-done.4, bf16[256,144]{1,0:T(8,128)(2,1)} %get-tuple-element.27.coefficient, bf16[144,16384]{1,0:T(8,128)(2,1)} %weight.3, ...), custom_call_target="tpu_custom_call" | custom-call | bytes 16500000 | tf_op jit(solution)/shard_map/density_0/pallas_call | solution.py:208
  36.5 1.3 collective-permute-start.10
  37.8 1.6 collective-permute-start.11
  39.4 3.3 %collective-permute-done.6.refs_1_ = bf16[768,768]{1,0:T(8,128)(2,1)} collective-permute-done((bf16[768,768]{1,0:T(8,128)(2,1)}, bf16[768,768]{1,0:T(8,128)(2,1)}, u32[]{:S(2)}, u32[]{:S(2)}) %collective-permute-start.6) | collective-permute-done | bytes 1179680 | tf_op jit(solution)/shard_map/raw_a_across_rows_2/ppermute | solution.py:416
  42.7 2.5 %collective-permute-done.5.refs_0_ = bf16[768,768]{1,0:T(8,128)(2,1)} collective-permute-done((bf16[768,768]{1,0:T(8,128)(2,1)}, bf16[768,768]{1,0:T(8,128)(2,1)}, u32[]{:S(2)}, u32[]{:S(2)}) %collective-permute-start.5) | collective-permute-done | bytes 1179680 | tf_op jit(solution)/shard_map/raw_a_across_rows_1/ppermute | solution.py:416
  45.2 5.5 %collective-permute-done.7.refs_3_ = bf16[768,768]{1,0:T(8,128)(2,1)} collective-permute-done((bf16[768,768]{1,0:T(8,128)(2,1)}, bf16[768,768]{1,0:T(8,128)(2,1)}, u32[]{:S(2)}, u32[]{:S(2)}) %collective-permute-start.7) | collective-permute-done | bytes 1179680 | tf_op jit(solution)/shard_map/raw_a_beside/ppermute | solution.py:416
  50.7 0.7 collective-permute-start.12
  51.4 12.0 %density_2.1 = (bf16[768,768]{1,0:T(8,128)(2,1)}, bf16[768,768]{1,0:T(8,128)(2,1)}, bf16[768,768]{1,0:T(8,128)(2,1)}) custom-call(s32[1,5,128]{2,1,0:T(8,128)} %get-tuple-element.26.hits, f32[3]{0:T(128)} %pad_maximum_fusion.6.scale, s32[2,5]{1,0:T(2,128)} %copy-done.4, bf16[256,144]{1,0:T(8,128)(2,1)} %get-tuple-element.27.coefficient, ...), custom_call_target="tpu_custom_call" | custom-call | bytes 20250000 | tf_op jit(solution)/shard_map/density_2/pallas_call | solution.py:208
  63.4 1.4 collective-permute-start.14
  64.8 7.4 %collective-permute-done.10 = bf16[768,768]{1,0:T(8,128)(2,1)} collective-permute-done((bf16[768,768]{1,0:T(8,128)(2,1)}, bf16[768,768]{1,0:T(8,128)(2,1)}, u32[]{:S(2)}, u32[]{:S(2)}) %collective-permute-start.10) | collective-permute-done | bytes 1179680 | tf_op jit(solution)/shard_map/density_b_beside/ppermute | solution.py:416
  72.2 2.4 %broadcast_select_fusion.refs_6_ = bf16[768,768]{1,0:T(8,128)(2,1)} fusion(bf16[768,768]{1,0:T(8,128)(2,1)} %get-tuple-element.36.refs_1_.refs_3_.refs_0_, bf16[768,768]{1,0:T(8,128)(2,1)} %collective-permute-done.10, pred[]{:T(512)S(6)} %eq.8), kind=kLoop, calls=%fused_computation.2 | loop fusion | flops 589824 | bytes 3538945 | tf_op jit(solution)/shard_map/jit(_where)/select_n | solution.py:526
  74.6 0.8 collective-permute-start.8
  75.4 8.5 %far_0_1.1.refs_8_ = bf16[2,768,768]{2,1,0:T(8,128)(2,1)} custom-call(bf16[768,768]{1,0:T(8,128)(2,1)} %get-tuple-element.28.refs_4_.refs_0_.refs_2_, bf16[768,768]{1,0:T(8,128)(2,1)} %get-tuple-element.36.refs_1_.refs_3_.refs_0_, bf16[768,768]{1,0:T(8,128)(2,1)} %get-tuple-element.28.refs_4_.refs_0_.refs_2_, ...), custom_call_target="tpu_custom_call" | custom-call | bytes 13500000 | tf_op jit(solution)/shard_map/far_0_1/pallas_call | solution.py:320
  83.9 1.3 collective-permute-start.15
  85.9 7.6 %collective-permute-done.14.refs_3_.refs_5_ = bf16[768,768]{1,0:T(8,128)(2,1)} collective-permute-done((bf16[768,768]{1,0:T(8,128)(2,1)}, bf16[768,768]{1,0:T(8,128)(2,1)}, u32[]{:S(2)}, u32[]{:S(2)}) %collective-permute-start.14) | collective-permute-done | bytes 1179680 | tf_op jit(solution)/shard_map/forward_b_across_rows_1/ppermute | solution.py:416
  93.4 8.3 %near_1.1 = (f32[768,768]{1,0:T(8,128)}, bf16[768,768]{1,0:T(8,128)(2,1)}) custom-call(s32[4]{0:T(128)} %pad_add_fusion.1.source, bf16[768,768]{1,0:T(8,128)(2,1)} %get-tuple-element.36.refs_1_.refs_3_.refs_0_, bf16[768,768]{1,0:T(8,128)(2,1)} %collective-permute-done.11.refs_5_.refs_1_, bf16[768,768]{1,0:T(8,128)(2,1)} %collective-permute-done.12.refs_2_.refs_3_, ...), custom_call_target="tpu_custom_call" | custom-call | bytes 18000000 | tf_op jit(solution)/shard_map/near_1/pallas_call | solution.py:284
  101.7 2.1 %slice.12 = bf16[512,768]{1,0:T(8,128)(2,1)} slice(bf16[768,768]{1,0:T(8,128)(2,1)} %get-tuple-element.40), slice={[256:768], [0:768]} | slice | bytes 1572864 | tf_op jit(solution)/shard_map/slice | solution.py:547
  103.8 5.7 %collective-permute-start.17 = (bf16[512,768]{1,0:T(8,128)(2,1)}, bf16[512,768]{1,0:T(8,128)(2,1)}, u32[]{:S(2)}, u32[]{:S(2)}) collective-permute-start(bf16[512,768]{1,0:T(8,128)(2,1)} %slice.12), channel_id=1, source_target_pairs={{2,0},{3,1},{6,4},{7,5},{10,8},{11,9},{14,12},{15,13},{16,18},{17,... | collective-permute-start | bytes 2359304 | tf_op jit(solution)/shard_map/near_1_beside/ppermute | solution.py:416
  109.5 1.0 slice.13
  110.6 3.8 %collective-permute-start.18 = (bf16[256,768]{1,0:T(8,128)(2,1)S(1)}, bf16[256,768]{1,0:T(8,128)(2,1)}, u32[]{:S(2)}, u32[]{:S(2)}) collective-permute-start(bf16[256,768]{1,0:T(8,128)(2,1)S(1)} %slice.13), channel_id=1, source_target_pairs={{2,20},{3,28},{6,16},{7,24},{10,21},{11,29},{14,17},{15,25},{16,6}... | collective-permute-start | bytes 1179656 | tf_op jit(solution)/shard_map/near_1_direct/ppermute | solution.py:416
  114.3 8.3 %near_0.1 = (f32[768,768]{1,0:T(8,128)}, bf16[768,768]{1,0:T(8,128)(2,1)}) custom-call(s32[4]{0:T(128)} %pad_add_fusion.1.source, bf16[768,768]{1,0:T(8,128)(2,1)} %get-tuple-element.28.refs_4_.refs_0_.refs_2_, bf16[768,768]{1,0:T(8,128)(2,1)} %get-tuple-element.32.refs_4_.refs_6_.refs_1_, bf16[768,768]{1,0:T(8,128)(2,1)} %get-tuple-element.33.refs_2_, ...), custom_call_target="tpu_custom_call" | custom-call | bytes 18000000 | tf_op jit(solution)/shard_map/near_0/pallas_call | solution.py:284
  122.6 7.7 %far_2_3.1 = bf16[2,768,768]{2,1,0:T(8,128)(2,1)} custom-call(bf16[768,768]{1,0:T(8,128)(2,1)} %get-tuple-element.28.refs_4_.refs_0_.refs_2_, bf16[768,768]{1,0:T(8,128)(2,1)} %get-tuple-element.36.refs_1_.refs_3_.refs_0_, bf16[768,768]{1,0:T(8,128)(2,1)} %get-tuple-element.33.refs_2_, bf16[768,768]{1,0:T(8,128)(2,1)} %collective-permute-done.12.refs_2_.refs_3_, ...), custom_call_target="tpu_custom_call" | custom-call | bytes 13500000 | tf_op jit(solution)/shard_map/far_2_3/pallas_call | solution.py:320
  130.4 3.5 %collective-permute-done.18.refs_6_ = bf16[256,768]{1,0:T(8,128)(2,1)} collective-permute-done((bf16[256,768]{1,0:T(8,128)(2,1)S(1)}, bf16[256,768]{1,0:T(8,128)(2,1)}, u32[]{:S(2)}, u32[]{:S(2)}) %collective-permute-start.18) | collective-permute-done | bytes 393248 | tf_op jit(solution)/shard_map/near_1_direct/ppermute | solution.py:416
  133.9 1.4 collective-permute-start.19
  135.4 3.1 %add_convert_fusion.1 = bf16[2,768,768]{2,1,0:T(8,128)(2,1)S(1)} fusion(bf16[2,768,768]{2,1,0:T(8,128)(2,1)} %collective-permute-done.15, bf16[2,768,768]{2,1,0:T(8,128)(2,1)} %far_0_1.1.refs_8_), kind=kLoop, calls=%fused_computation.1 | loop fusion | flops 4718592 | bytes 7077888 | tf_op jit(solution)/shard_map/convert_element_type | solution.py:512
  138.5 2.7 %collective-permute-start.16 = (bf16[2,768,768]{2,1,0:T(8,128)(2,1)S(1)}, bf16[2,768,768]{2,1,0:T(8,128)(2,1)}, u32[]{:S(2)}, u32[]{:S(2)}) collective-permute-start(bf16[2,768,768]{2,1,0:T(8,128)(2,1)S(1)} %add_convert_fusion.1), channel_id=1, source_target_pairs={{2,0},{6,4},{11,9},{15,13},{16,18},{20,22},{25,27},{29,31}} | collective-permute-start | bytes 7077896 | tf_op jit(solution)/shard_map/far_0_1_beside/ppermute | solution.py:416
  141.2 2.7 %collective-permute-start.22 = (bf16[768,768]{1,0:T(8,128)(2,1)S(1)}, bf16[768,768]{1,0:T(8,128)(2,1)S(1)}, u32[]{:S(2)}, u32[]{:S(2)}) collective-permute-start(bf16[768,768]{1,0:T(8,128)(2,1)S(1)} %copy-done.5), channel_id=1, source_target_pairs={{2,16},{3,24},{6,20},{7,28},{10,17},{11,25},{14,21},{15,29},{16,2}... | collective-permute-start | bytes 3538952 | tf_op jit(solution)/shard_map/near_0_direct/ppermute | solution.py:416
  144.6 0.7 collective-permute-start.21
  145.4 1.8 collective-permute-start.20
  147.2 1.3 collective-permute-start.23
  149.1 46.1 %collective-permute-done.22.refs_5_ = bf16[768,768]{1,0:T(8,128)(2,1)S(1)} collective-permute-done((bf16[768,768]{1,0:T(8,128)(2,1)S(1)}, bf16[768,768]{1,0:T(8,128)(2,1)S(1)}, u32[]{:S(2)}, u32[]{:S(2)}) %collective-permute-start.22) | collective-permute-done | bytes 1179680 | tf_op jit(solution)/shard_map/near_0_direct/ppermute | solution.py:416
  195.2 1.1 copy-done.1
  196.5 1.0 copy-done.2
  197.5 8.6 %shard_map.65 = f32[768,1536]{1,0:T(8,128)} custom-call(s32[2]{0:T(128)} %pad_add_fusion.slot, f32[768,768]{1,0:T(8,128)} %get-tuple-element.39.refs_6_.refs_0_, f32[768,768]{1,0:T(8,128)} %get-tuple-element.38.refs_8_.refs_1_, bf16[2,768,768]{2,1,0:T(8,128)(2,1)} %collective-permute-done.16.refs_2_, bf16[1,768,768]{2,1,0:T(8,128)(2,1)} %collective-permute-done.20.refs_3_, ...), custom_call_target="tpu_custom_call" | custom-call | bytes 13500000 | tf_op jit(solution)/shard_map/pallas_call | solution.py:368
  (45 shorter events, 5.0 us)
Async XLA Ops:
  1.4 5.5 %collective-permute-start = (f32[8,8]{1,0:T(8,128)S(1)}, f32[8,8]{1,0:T(8,128)S(1)}, u32[]{:S(2)}, u32[]{:S(2)}) collective-permute-start(f32[8,8]{1,0:T(8,128)S(1)} %pad_maximum_fusion.1), channel_id=1, source_target_pairs={{0,16},{1,17},{2,18},{3,19},{4,20},{5,21},{6,22},{7,23},{8,24},{9,... | collective-permute-start | bytes 776 | tf_op jit(solution)/shard_map/ppermute | solution.py:446
  5.5 6.9 %copy-start.4 = (s32[2,5]{1,0:T(2,128)}, s32[2,5]{1,0:T(2,128)S(1)}, u32[]{:S(2)}) copy-start(s32[2,5]{1,0:T(2,128)S(1)} %add_multiply_fusion.corner) | copy-start | bytes 124
  7.6 4.8 %collective-permute-start.1 = (f32[8,16]{1,0:T(8,128)S(1)}, f32[8,16]{1,0:T(8,128)S(1)}, u32[]{:S(2)}, u32[]{:S(2)}) collective-permute-start(f32[8,16]{1,0:T(8,128)S(1)} %pad_maximum_fusion.2), channel_id=1, source_target_pairs={{0,8},{1,9},{2,10},{3,11},{4,12},{5,13},{6,14},{7,15},{8,0},{9,1},... | collective-permute-start | bytes 1544 | tf_op jit(solution)/shard_map/ppermute | solution.py:446
  12.5 3.6 %collective-permute-start.2 = (f32[8,32]{1,0:T(8,128)S(1)}, f32[8,32]{1,0:T(8,128)S(1)}, u32[]{:S(2)}, u32[]{:S(2)}) collective-permute-start(f32[8,32]{1,0:T(8,128)S(1)} %pad_maximum_fusion.3), channel_id=1, source_target_pairs={{0,4},{1,5},{2,6},{3,7},{4,0},{5,1},{6,2},{7,3},{8,12},{9,13},{10,... | collective-permute-start | bytes 3080 | tf_op jit(solution)/shard_map/ppermute | solution.py:446
  16.2 3.6 %collective-permute-start.3 = (f32[8,64]{1,0:T(8,128)S(1)}, f32[8,64]{1,0:T(8,128)S(1)}, u32[]{:S(2)}, u32[]{:S(2)}) collective-permute-start(f32[8,64]{1,0:T(8,128)S(1)} %pad_maximum_fusion.4), channel_id=1, source_target_pairs={{0,2},{1,3},{2,0},{3,1},{4,6},{5,7},{6,4},{7,5},{8,10},{9,11},{10,... | collective-permute-start | bytes 6152 | tf_op jit(solution)/shard_map/ppermute | solution.py:446
  16.7 26.0 %collective-permute-start.6 = (bf16[768,768]{1,0:T(8,128)(2,1)}, bf16[768,768]{1,0:T(8,128)(2,1)}, u32[]{:S(2)}, u32[]{:S(2)}) collective-permute-start(bf16[768,768]{1,0:T(8,128)(2,1)} %get-tuple-element.31.refs_0_.refs_2_), channel_id=1, source_target_pairs={{0,8},{1,9},{2,10},{3,11},{4,12},{5,13},{6,14},{7,15},{8,0},{9,1},... | collective-permute-start | bytes 3538952 | tf_op jit(solution)/shard_map/raw_a_across_rows_2/ppermute | solution.py:416
  17.1 28.1 %collective-permute-start.5 = (bf16[768,768]{1,0:T(8,128)(2,1)}, bf16[768,768]{1,0:T(8,128)(2,1)}, u32[]{:S(2)}, u32[]{:S(2)}) collective-permute-start(bf16[768,768]{1,0:T(8,128)(2,1)} %get-tuple-element.29.refs_1_), channel_id=1, source_target_pairs={{0,4},{1,5},{2,6},{3,7},{4,0},{5,1},{6,2},{7,3},{8,12},{9,13},{10,... | collective-permute-start | bytes 3538952 | tf_op jit(solution)/shard_map/raw_a_across_rows_1/ppermute | solution.py:416
  19.9 30.8 %collective-permute-start.7 = (bf16[768,768]{1,0:T(8,128)(2,1)}, bf16[768,768]{1,0:T(8,128)(2,1)}, u32[]{:S(2)}, u32[]{:S(2)}) collective-permute-start(bf16[768,768]{1,0:T(8,128)(2,1)} %get-tuple-element.31.refs_0_.refs_2_), channel_id=1, source_target_pairs={{0,2},{1,3},{4,6},{5,7},{8,10},{9,11},{12,14},{13,15},{18,16},{19,... | collective-permute-start | bytes 3538952 | tf_op jit(solution)/shard_map/raw_a_beside/ppermute | solution.py:416
  21.1 1.2 collective-permute-start.4
  36.5 35.7 %collective-permute-start.10 = (bf16[768,768]{1,0:T(8,128)(2,1)}, bf16[768,768]{1,0:T(8,128)(2,1)}, u32[]{:S(2)}, u32[]{:S(2)}) collective-permute-start(bf16[768,768]{1,0:T(8,128)(2,1)} %get-tuple-element.36.refs_1_.refs_3_.refs_0_), channel_id=1, source_target_pairs={{0,2},{1,3},{4,6},{5,7},{8,10},{9,11},{12,14},{13,15},{18,16},{19,... | collective-permute-start | bytes 3538952 | tf_op jit(solution)/shard_map/density_b_beside/ppermute | solution.py:416
  37.8 36.8 %collective-permute-start.11 = (bf16[768,768]{1,0:T(8,128)(2,1)}, bf16[768,768]{1,0:T(8,128)(2,1)}, u32[]{:S(2)}, u32[]{:S(2)}) collective-permute-start(bf16[768,768]{1,0:T(8,128)(2,1)} %get-tuple-element.28.refs_4_.refs_0_.refs_2_), channel_id=1, source_target_pairs={{0,4},{1,5},{2,6},{3,7},{4,0},{5,1},{6,2},{7,3},{8,12},{9,13},{10,... | collective-permute-start | bytes 3538952 | tf_op jit(solution)/shard_map/density_b_across_rows_1/ppermute | solution.py:416
  50.7 23.9 %collective-permute-start.12 = (bf16[768,768]{1,0:T(8,128)(2,1)}, bf16[768,768]{1,0:T(8,128)(2,1)}, u32[]{:S(2)}, u32[]{:S(2)}) collective-permute-start(bf16[768,768]{1,0:T(8,128)(2,1)} %get-tuple-element.36.refs_1_.refs_3_.refs_0_), channel_id=1, source_target_pairs={{0,8},{1,9},{2,10},{3,11},{4,12},{5,13},{6,14},{7,15},{8,0},{9,1},... | collective-permute-start | bytes 3538952 | tf_op jit(solution)/shard_map/density_b_across_rows_2/ppermute | solution.py:416
  63.4 30.0 %collective-permute-start.14 = (bf16[768,768]{1,0:T(8,128)(2,1)}, bf16[768,768]{1,0:T(8,128)(2,1)}, u32[]{:S(2)}, u32[]{:S(2)}) collective-permute-start(bf16[768,768]{1,0:T(8,128)(2,1)} %get-tuple-element.33.refs_2_), channel_id=1, source_target_pairs={{0,4},{1,5},{2,6},{3,7},{4,0},{5,1},{6,2},{7,3},{8,12},{9,13},{10,... | collective-permute-start | bytes 3538952 | tf_op jit(solution)/shard_map/forward_b_across_rows_1/ppermute | solution.py:416
  64.8 28.6 %collective-permute-start.9 = (bf16[768,768]{1,0:T(8,128)(2,1)}, bf16[768,768]{1,0:T(8,128)(2,1)}, u32[]{:S(2)}, u32[]{:S(2)}) collective-permute-start(bf16[768,768]{1,0:T(8,128)(2,1)} %get-tuple-element.34.refs_4_), channel_id=1, source_target_pairs={{0,1},{1,0},{2,3},{3,2},{4,5},{5,4},{6,7},{7,6},{8,9},{9,8},{10,11... | collective-permute-start | bytes 3538952 | tf_op jit(solution)/shard_map/wide_a_across_cores/ppermute | solution.py:416
  74.6 18.9 %collective-permute-start.13 = (bf16[768,768]{1,0:T(8,128)(2,1)}, bf16[768,768]{1,0:T(8,128)(2,1)}, u32[]{:S(2)}, u32[]{:S(2)}) collective-permute-start(bf16[768,768]{1,0:T(8,128)(2,1)} %broadcast_select_fusion.refs_6_), channel_id=1, source_target_pairs={{0,1},{1,0},{2,3},{3,2},{4,5},{5,4},{6,7},{7,6},{8,9},{9,8},{10,11... | collective-permute-start | bytes 3538952 | tf_op jit(solution)/shard_map/wide_b_across_cores/ppermute | solution.py:416
  74.6 39.7 %collective-permute-start.8 = (bf16[768,768]{1,0:T(8,128)(2,1)}, bf16[768,768]{1,0:T(8,128)(2,1)}, u32[]{:S(2)}, u32[]{:S(2)}) collective-permute-start(bf16[768,768]{1,0:T(8,128)(2,1)} %get-tuple-element.32.refs_4_.refs_6_.refs_1_), channel_id=1, source_target_pairs={{0,8},{1,9},{2,10},{3,11},{4,12},{5,13},{6,14},{7,15},{8,0},{9,1},... | collective-permute-start | bytes 3538952 | tf_op jit(solution)/shard_map/forward_a_across_rows_2/ppermute | solution.py:416
  83.9 51.4 %collective-permute-start.15 = (bf16[2,768,768]{2,1,0:T(8,128)(2,1)}, bf16[2,768,768]{2,1,0:T(8,128)(2,1)}, u32[]{:S(2)}, u32[]{:S(2)}) collective-permute-start(bf16[2,768,768]{2,1,0:T(8,128)(2,1)} %far_0_1.1.refs_8_), channel_id=1, source_target_pairs={{3,2},{7,6},{10,11},{14,15},{17,16},{21,20},{24,25},{28,29}} | collective-permute-start | bytes 7077896 | tf_op jit(solution)/shard_map/far_0_1_across_cores/ppermute | solution.py:416
  103.8 30.1 %collective-permute-start.17 = (bf16[512,768]{1,0:T(8,128)(2,1)}, bf16[512,768]{1,0:T(8,128)(2,1)}, u32[]{:S(2)}, u32[]{:S(2)}) collective-permute-start(bf16[512,768]{1,0:T(8,128)(2,1)} %slice.12), channel_id=1, source_target_pairs={{2,0},{3,1},{6,4},{7,5},{10,8},{11,9},{14,12},{15,13},{16,18},{17,... | collective-permute-start | bytes 2359304 | tf_op jit(solution)/shard_map/near_1_beside/ppermute | solution.py:416
  110.6 23.3 %collective-permute-start.18 = (bf16[256,768]{1,0:T(8,128)(2,1)S(1)}, bf16[256,768]{1,0:T(8,128)(2,1)}, u32[]{:S(2)}, u32[]{:S(2)}) collective-permute-start(bf16[256,768]{1,0:T(8,128)(2,1)S(1)} %slice.13), channel_id=1, source_target_pairs={{2,20},{3,28},{6,16},{7,24},{10,21},{11,29},{14,17},{15,25},{16,6}... | collective-permute-start | bytes 1179656 | tf_op jit(solution)/shard_map/near_1_direct/ppermute | solution.py:416
  130.4 10.8 %copy-start.5 = (bf16[768,768]{1,0:T(8,128)(2,1)S(1)}, bf16[768,768]{1,0:T(8,128)(2,1)}, u32[]{:S(2)}) copy-start(bf16[768,768]{1,0:T(8,128)(2,1)} %get-tuple-element.42) | copy-start | bytes 3538948
  133.9 10.0 %collective-permute-start.19 = (bf16[2,768,768]{2,1,0:T(8,128)(2,1)}, bf16[2,768,768]{2,1,0:T(8,128)(2,1)S(1)}, u32[]{:S(2)}, u32[]{:S(2)}) collective-permute-start(bf16[2,768,768]{2,1,0:T(8,128)(2,1)} %far_2_3.1), channel_id=1, source_target_pairs={{2,3},{6,7},{11,10},{15,14},{16,17},{20,21},{25,24},{29,28}} | collective-permute-start | bytes 7077896 | tf_op jit(solution)/shard_map/far_2_3_across_cores/ppermute | solution.py:416
  135.4 8.5 %copy-start = (bf16[2,768,768]{2,1,0:T(8,128)(2,1)S(1)}, bf16[2,768,768]{2,1,0:T(8,128)(2,1)}, u32[]{:S(2)}) copy-start(bf16[2,768,768]{2,1,0:T(8,128)(2,1)} %far_2_3.1) | copy-start | bytes 7077892
  138.5 56.7 %collective-permute-start.16 = (bf16[2,768,768]{2,1,0:T(8,128)(2,1)S(1)}, bf16[2,768,768]{2,1,0:T(8,128)(2,1)}, u32[]{:S(2)}, u32[]{:S(2)}) collective-permute-start(bf16[2,768,768]{2,1,0:T(8,128)(2,1)S(1)} %add_convert_fusion.1), channel_id=1, source_target_pairs={{2,0},{6,4},{11,9},{15,13},{16,18},{20,22},{25,27},{29,31}} | collective-permute-start | bytes 7077896 | tf_op jit(solution)/shard_map/far_0_1_beside/ppermute | solution.py:416
  141.2 54.0 %collective-permute-start.22 = (bf16[768,768]{1,0:T(8,128)(2,1)S(1)}, bf16[768,768]{1,0:T(8,128)(2,1)S(1)}, u32[]{:S(2)}, u32[]{:S(2)}) collective-permute-start(bf16[768,768]{1,0:T(8,128)(2,1)S(1)} %copy-done.5), channel_id=1, source_target_pairs={{2,16},{3,24},{6,20},{7,28},{10,17},{11,25},{14,21},{15,29},{16,2}... | collective-permute-start | bytes 3538952 | tf_op jit(solution)/shard_map/near_0_direct/ppermute | solution.py:416
  144.6 51.7 %collective-permute-start.21 = (bf16[1,768,768]{2,1,0:T(8,128)(2,1)S(1)}, bf16[1,768,768]{2,1,0:T(8,128)(2,1)S(1)}, u32[]{:S(2)}, u32[]{:S(2)}) collective-permute-start(bf16[1,768,768]{2,1,0:T(8,128)(2,1)S(1)} %get-tuple-element.43), channel_id=1, source_target_pairs={{3,1},{7,5},{10,8},{14,12},{17,19},{21,23},{24,26},{28,30}} | collective-permute-start | bytes 3538952 | tf_op jit(solution)/shard_map/far_2_3_beside_1/ppermute | solution.py:416
  145.4 52.1 %collective-permute-start.20 = (bf16[1,768,768]{2,1,0:T(8,128)(2,1)S(1)}, bf16[1,768,768]{2,1,0:T(8,128)(2,1)}, u32[]{:S(2)}, u32[]{:S(2)}) collective-permute-start(bf16[1,768,768]{2,1,0:T(8,128)(2,1)S(1)} %get-tuple-element.44), channel_id=1, source_target_pairs={{3,1},{7,5},{10,8},{14,12},{17,19},{21,23},{24,26},{28,30}} | collective-permute-start | bytes 3538952 | tf_op jit(solution)/shard_map/far_2_3_beside_0/ppermute | solution.py:416
  147.2 48.0 %collective-permute-start.23 = (bf16[512,768]{1,0:T(8,128)(2,1)}, bf16[512,768]{1,0:T(8,128)(2,1)S(1)}, u32[]{:S(2)}, u32[]{:S(2)}) collective-permute-start(bf16[512,768]{1,0:T(8,128)(2,1)} %collective-permute-done.17), channel_id=1, source_target_pairs={{0,20},{1,28},{4,16},{5,24},{8,21},{9,29},{12,17},{13,25},{18,6},{... | collective-permute-start | bytes 2359304 | tf_op jit(solution)/shard_map/near_1_ahead/ppermute | solution.py:416
  195.2 1.1 copy-start.1
  195.2 1.3 copy-start.3
  196.5 1.0 copy-start.2

commit v5 on v4

--- a/solution.py
+++ b/solution.py
@@ -337,33 +337,50 @@
     near = [refs.pop(0) for _ in range(2)]
     far = [[refs.pop(0) for _ in range(n)] for n in parts]
     opposite = [[refs.pop(0) for _ in range(n)] for n in pieces]
-    out = refs.pop(0)
+    out, near_in, far_in, opposite_in, sems = refs
     turn = pl.program_id(0)
     block = 128
+    groups = len(far)
+    copies = []
+    for q in range(2):
+        here = [pltpu.make_async_copy(near[q], near_in.at[q], sems.at[q, 0])]
+        for n, share in enumerate(far):
+            part = share[q].at[0] if len(share) == 2 else share[0].at[q]
+            here.append(pltpu.make_async_copy(part, far_in.at[q, n], sems.at[q, 1 + n]))
+        at = 0
+        for n, piece in enumerate(opposite[q]):
+            to = opposite_in.at[q, pl.ds(at, piece.shape[0])]
+            here.append(pltpu.make_async_copy(piece, to, sems.at[q, 1 + groups + n]))
+            at += piece.shape[0]
+        copies.append(here)
+
+    @pl.when(turn == 0)
+    def _():
+        for here in copies:
+            for copy in here:
+                copy.start()
+
     for q in range(2):
 
         @pl.when(turn == q)
         def _():
-            start = 0
-            for piece in opposite[q]:
-                rows = piece.shape[0]
-
-                def step(n, _):
-                    at = pl.ds(pl.multiple_of(n * block, block), block)
-                    to = pl.ds(start, rows)
-                    value = near[q][at, to]
-                    for share in far:
-                        part = share[q][0, at, to] if len(share) == 2 else share[0][q, at, to]
-                        value = value + part.astype(jnp.float32)
-                    out[at, to] = value + piece[:, at].astype(jnp.float32).T
-                    return 0
-
-                lax.fori_loop(0, out.shape[0] // block, step, 0)
-                start += rows
+            for copy in copies[q]:
+                copy.wait()
+
+            def step(n, _):
+                at = pl.ds(pl.multiple_of(n * block, block), block)
+                value = near_in[q, at, :]
+                for n in range(groups):
+                    value = value + far_in[q, n, at, :].astype(jnp.float32)
+                out[at, :] = value + opposite_in[q, :, at].astype(jnp.float32).T
+                return 0
+
+            lax.fori_loop(0, out.shape[0] // block, step, 0)
 
 
 def final_sum(slot, near, far, opposite):
     side = near[0].shape[0]
+    groups = len(far)
     operands = [*near, *[part for share in far for part in share], *opposite[0], *opposite[1]]
     return pl.pallas_call(
         functools.partial(final_kernel, [len(share) for share in far], [len(pieces) for pieces in opposite]),
@@ -371,8 +388,14 @@
         grid_spec=pltpu.PrefetchScalarGridSpec(
             num_scalar_prefetch=1,
             grid=(2,),
-            in_specs=[pl.BlockSpec(o.shape, lambda t, s, n=len(o.shape): (0,) * n) for o in operands],
+            in_specs=[pl.BlockSpec(memory_space=pl.ANY)] * len(operands),
             out_specs=pl.BlockSpec((side, side), lambda t, s: (0, s[t])),
+            scratch_shapes=[
+                pltpu.VMEM((2, side, side), jnp.float32),
+                pltpu.VMEM((2, groups, side, side), jnp.bfloat16),
+                pltpu.VMEM((2, side, side), jnp.bfloat16),
+                pltpu.SemaphoreType.DMA((2, groups + 3)),
+            ],
         ),
         cost_estimate=taking(9),
         compiler_params=pltpu.CompilerParams(vmem_limit_bytes=VMEM_BYTES),

time: 207 us -> 206 us (level)
  Pallas kernels: 66.9 us -> 63.6 us
  starting transfers between devices: 36.6 us -> 38.8 us
    ppermute x19, starting transfers between devices: 30.4 us -> 32.5 us  [send(): made[what] = lax.ppermute(after(value, *waits(what)), AXES, moves(where))]
  transfers between devices with their start and end apart: 24 -> 24, of which waited for: 10 -> 10; matrix products, arithmetic and copies ran while one was open for 8% -> 8% of each run, Pallas kernels for 28% -> 27%
where the time goes in v5:
time: 206 us; the launch traced here: 205 us
  waiting for transfers between devices  80.5 us (39%)
  Pallas kernels  63.6 us (31%)
  starting transfers between devices  38.8 us (19%)
  other arithmetic  11.1 us (5%)
  local copies, waits for them, and re-layouts  9.52 us (5%)
    ppermute x19, waiting for transfers between devices, send(): made[what] = lax.ppermute(after(value, *waits(what)), AXES, moves(where))  76 us
    ppermute x19, starting transfers between devices, send(): made[what] = lax.ppermute(after(value, *waits(what)), AXES, moves(where))  32.5 us
    pallas_call x2, Pallas kernels, densities(): pl.pallas_call(functools.partial(density_kernel, chunks, sources, len(soo...  20.7 us
    pallas_call x2, Pallas kernels, near_share(): pl.pallas_call(functools.partial(near_kernel, sides, sources, seed is not...  16.6 us
    pallas_call x2, Pallas kernels, far_share(): pl.pallas_call(functools.partial(far_kernel, count, len(sooner)), out_sha...  16.2 us
    pallas_call x1, Pallas kernels, final_sum(): pl.pallas_call(functools.partial(final_kernel, [len(share) for share in f...  7.35 us
    ppermute x5, starting transfers between devices, double(): arrived = lax.ppermute(value, AXES, [(d, d ^ bit) for d in range(devices)])  6.23 us
    ppermute x5, waiting for transfers between devices, double(): arrived = lax.ppermute(value, AXES, [(d, d ^ bit) for d in range(devices)])  4.43 us
  transfers between devices with their start and end apart: 24, of which 10 were waited for; matrix products, arithmetic and copies ran while one was open for 8% of the time, Pallas kernels for 27%

profile of v5, /device:TPU:4, one launch (start us, length us, event | category | flops | bytes accessed | tf_op | source)
XLA Modules:
  0.0 205.3 jit_solution(9471597153306937477)
XLA Ops:
  0.0 0.7 convert_element_type.27
  0.7 0.7 pad_maximum_fusion.1
  1.4 2.6 %collective-permute-start = (f32[8,8]{1,0:T(8,128)S(1)}, f32[8,8]{1,0:T(8,128)S(1)}, u32[]{:S(2)}, u32[]{:S(2)}) collective-permute-start(f32[8,8]{1,0:T(8,128)S(1)} %pad_maximum_fusion.1), channel_id=1, source_target_pairs={{0,16},{1,17},{2,18},{3,19},{4,20},{5,21},{6,22},{7,23},{8,24},{9,... | collective-permute-start | bytes 776 | tf_op jit(solution)/shard_map/ppermute | solution.py:469
  5.5 0.7 pad_maximum_fusion.6.scale
  6.9 0.8 pad_maximum_fusion.2
  7.6 1.6 collective-permute-start.1
  9.2 3.2 %constant_dynamic-slice_fusion = (bf16[768,768]{1,0:T(8,128)(2,1)}, bf16[768,768]{1,0:T(8,128)(2,1)}) fusion(bf16[768,1536]{1,0:T(8,128)(2,1)} %param.9, s32[]{:T(128)S(6)} %select_n.49, s32[]{:T(128)S(6)} %select_n.48), kind=kLoop, calls=%fused_computation.16 | loop fusion | bytes 4718600 | tf_op jit(solution)/shard_map/dynamic_slice | solution.py:448
  12.5 1.5 collective-permute-start.2
  14.0 2.1 %collective-permute-done.2 = f32[8,32]{1,0:T(8,128)S(1)} collective-permute-done((f32[8,32]{1,0:T(8,128)S(1)}, f32[8,32]{1,0:T(8,128)S(1)}, u32[]{:S(2)}, u32[]{:S(2)}) %collective-permute-start.2) | collective-permute-done | bytes 1056 | tf_op jit(solution)/shard_map/ppermute | solution.py:469
  17.1 1.5 collective-permute-start.5
  18.6 1.2 collective-permute-done.3
  19.9 1.3 collective-permute-start.7
  21.2 1.2 collective-permute-done.4
  22.4 0.7 pad_maximum_fusion.edges
  23.0 2.8 %shard_map.64 = (bf16[256,144]{1,0:T(8,128)(2,1)}, s32[1,5,128]{2,1,0:T(8,128)}) custom-call(f32[8,256]{1,0:T(8,128)} %pad_maximum_fusion.edges, f32[8,128]{1,0:T(8,128)} %pad.5.corner), custom_call_target="tpu_custom_call" | custom-call | bytes 4500000 | tf_op jit(solution)/shard_map/pallas_call | solution.py:96
  25.8 10.0 %density_0.1 = (bf16[768,768]{1,0:T(8,128)(2,1)}, bf16[768,768]{1,0:T(8,128)(2,1)}) custom-call(s32[1,5,128]{2,1,0:T(8,128)} %get-tuple-element.26.hits, f32[3]{0:T(128)} %pad_maximum_fusion.6.scale, s32[2,5]{1,0:T(2,128)} %copy-done.4, bf16[256,144]{1,0:T(8,128)(2,1)} %get-tuple-element.27.coefficient, bf16[144,16384]{1,0:T(8,128)(2,1)} %weight.3, ...), custom_call_target="tpu_custom_call" | custom-call | bytes 16500000 | tf_op jit(solution)/shard_map/density_0/pallas_call | solution.py:208
  35.9 1.3 collective-permute-start.10
  37.2 1.2 collective-permute-start.11
  38.3 4.4 %collective-permute-done.6.refs_1_ = bf16[768,768]{1,0:T(8,128)(2,1)} collective-permute-done((bf16[768,768]{1,0:T(8,128)(2,1)}, bf16[768,768]{1,0:T(8,128)(2,1)}, u32[]{:S(2)}, u32[]{:S(2)}) %collective-permute-start.6) | collective-permute-done | bytes 1179680 | tf_op jit(solution)/shard_map/raw_a_across_rows_2/ppermute | solution.py:439
  42.7 2.1 %collective-permute-done.5.refs_0_ = bf16[768,768]{1,0:T(8,128)(2,1)} collective-permute-done((bf16[768,768]{1,0:T(8,128)(2,1)}, bf16[768,768]{1,0:T(8,128)(2,1)}, u32[]{:S(2)}, u32[]{:S(2)}) %collective-permute-start.5) | collective-permute-done | bytes 1179680 | tf_op jit(solution)/shard_map/raw_a_across_rows_1/ppermute | solution.py:439
  44.8 6.1 %collective-permute-done.7.refs_3_ = bf16[768,768]{1,0:T(8,128)(2,1)} collective-permute-done((bf16[768,768]{1,0:T(8,128)(2,1)}, bf16[768,768]{1,0:T(8,128)(2,1)}, u32[]{:S(2)}, u32[]{:S(2)}) %collective-permute-start.7) | collective-permute-done | bytes 1179680 | tf_op jit(solution)/shard_map/raw_a_beside/ppermute | solution.py:439
  51.0 10.7 %density_2.1 = (bf16[768,768]{1,0:T(8,128)(2,1)}, bf16[768,768]{1,0:T(8,128)(2,1)}, bf16[768,768]{1,0:T(8,128)(2,1)}) custom-call(s32[1,5,128]{2,1,0:T(8,128)} %get-tuple-element.26.hits, f32[3]{0:T(128)} %pad_maximum_fusion.6.scale, s32[2,5]{1,0:T(2,128)} %copy-done.4, bf16[256,144]{1,0:T(8,128)(2,1)} %get-tuple-element.27.coefficient, ...), custom_call_target="tpu_custom_call" | custom-call | bytes 20250000 | tf_op jit(solution)/shard_map/density_2/pallas_call | solution.py:208
  61.6 2.8 %collective-permute-start.14 = (bf16[768,768]{1,0:T(8,128)(2,1)}, bf16[768,768]{1,0:T(8,128)(2,1)}, u32[]{:S(2)}, u32[]{:S(2)}) collective-permute-start(bf16[768,768]{1,0:T(8,128)(2,1)} %get-tuple-element.33.refs_2_), channel_id=1, source_target_pairs={{0,4},{1,5},{2,6},{3,7},{4,0},{5,1},{6,2},{7,3},{8,12},{9,13},{10,... | collective-permute-start | bytes 3538952 | tf_op jit(solution)/shard_map/forward_b_across_rows_1/ppermute | solution.py:439
  64.4 7.8 %collective-permute-done.10 = bf16[768,768]{1,0:T(8,128)(2,1)} collective-permute-done((bf16[768,768]{1,0:T(8,128)(2,1)}, bf16[768,768]{1,0:T(8,128)(2,1)}, u32[]{:S(2)}, u32[]{:S(2)}) %collective-permute-start.10) | collective-permute-done | bytes 1179680 | tf_op jit(solution)/shard_map/density_b_beside/ppermute | solution.py:439
  72.2 2.4 %broadcast_select_fusion.refs_6_ = bf16[768,768]{1,0:T(8,128)(2,1)} fusion(bf16[768,768]{1,0:T(8,128)(2,1)} %get-tuple-element.36.refs_1_.refs_3_.refs_0_, bf16[768,768]{1,0:T(8,128)(2,1)} %collective-permute-done.10, pred[]{:T(512)S(6)} %eq.8), kind=kLoop, calls=%fused_computation.2 | loop fusion | flops 589824 | bytes 3538945 | tf_op jit(solution)/shard_map/jit(_where)/select_n | solution.py:549
  74.6 0.8 collective-permute-start.8
  75.4 8.5 %far_0_1.1.refs_8_ = bf16[2,768,768]{2,1,0:T(8,128)(2,1)} custom-call(bf16[768,768]{1,0:T(8,128)(2,1)} %get-tuple-element.28.refs_4_.refs_0_.refs_2_, bf16[768,768]{1,0:T(8,128)(2,1)} %get-tuple-element.36.refs_1_.refs_3_.refs_0_, bf16[768,768]{1,0:T(8,128)(2,1)} %get-tuple-element.28.refs_4_.refs_0_.refs_2_, ...), custom_call_target="tpu_custom_call" | custom-call | bytes 13500000 | tf_op jit(solution)/shard_map/far_0_1/pallas_call | solution.py:320
  83.9 1.3 collective-permute-start.15
  85.9 7.6 %collective-permute-done.14.refs_3_.refs_5_ = bf16[768,768]{1,0:T(8,128)(2,1)} collective-permute-done((bf16[768,768]{1,0:T(8,128)(2,1)}, bf16[768,768]{1,0:T(8,128)(2,1)}, u32[]{:S(2)}, u32[]{:S(2)}) %collective-permute-start.14) | collective-permute-done | bytes 1179680 | tf_op jit(solution)/shard_map/forward_b_across_rows_1/ppermute | solution.py:439
  93.4 8.3 %near_1.1 = (f32[768,768]{1,0:T(8,128)}, bf16[768,768]{1,0:T(8,128)(2,1)}) custom-call(s32[4]{0:T(128)} %pad_add_fusion.1.source, bf16[768,768]{1,0:T(8,128)(2,1)} %get-tuple-element.36.refs_1_.refs_3_.refs_0_, bf16[768,768]{1,0:T(8,128)(2,1)} %collective-permute-done.11.refs_5_.refs_1_, bf16[768,768]{1,0:T(8,128)(2,1)} %collective-permute-done.12.refs_2_.refs_3_, ...), custom_call_target="tpu_custom_call" | custom-call | bytes 18000000 | tf_op jit(solution)/shard_map/near_1/pallas_call | solution.py:284
  101.7 2.1 %slice.12 = bf16[512,768]{1,0:T(8,128)(2,1)} slice(bf16[768,768]{1,0:T(8,128)(2,1)} %get-tuple-element.40), slice={[256:768], [0:768]} | slice | bytes 1572864 | tf_op jit(solution)/shard_map/slice | solution.py:570
  103.8 5.0 %collective-permute-start.17 = (bf16[512,768]{1,0:T(8,128)(2,1)}, bf16[512,768]{1,0:T(8,128)(2,1)}, u32[]{:S(2)}, u32[]{:S(2)}) collective-permute-start(bf16[512,768]{1,0:T(8,128)(2,1)} %slice.12), channel_id=1, source_target_pairs={{2,0},{3,1},{6,4},{7,5},{10,8},{11,9},{14,12},{15,13},{16,18},{17,... | collective-permute-start | bytes 2359304 | tf_op jit(solution)/shard_map/near_1_beside/ppermute | solution.py:439
  108.8 1.0 slice.13
  109.8 5.4 %collective-permute-start.18 = (bf16[256,768]{1,0:T(8,128)(2,1)S(1)}, bf16[256,768]{1,0:T(8,128)(2,1)}, u32[]{:S(2)}, u32[]{:S(2)}) collective-permute-start(bf16[256,768]{1,0:T(8,128)(2,1)S(1)} %slice.13), channel_id=1, source_target_pairs={{2,20},{3,28},{6,16},{7,24},{10,21},{11,29},{14,17},{15,25},{16,6}... | collective-permute-start | bytes 1179656 | tf_op jit(solution)/shard_map/near_1_direct/ppermute | solution.py:439
  115.3 8.3 %near_0.1 = (f32[768,768]{1,0:T(8,128)}, bf16[768,768]{1,0:T(8,128)(2,1)}) custom-call(s32[4]{0:T(128)} %pad_add_fusion.1.source, bf16[768,768]{1,0:T(8,128)(2,1)} %get-tuple-element.28.refs_4_.refs_0_.refs_2_, bf16[768,768]{1,0:T(8,128)(2,1)} %get-tuple-element.32.refs_4_.refs_6_.refs_1_, bf16[768,768]{1,0:T(8,128)(2,1)} %get-tuple-element.33.refs_2_, ...), custom_call_target="tpu_custom_call" | custom-call | bytes 18000000 | tf_op jit(solution)/shard_map/near_0/pallas_call | solution.py:284
  123.6 7.7 %far_2_3.1 = bf16[2,768,768]{2,1,0:T(8,128)(2,1)} custom-call(bf16[768,768]{1,0:T(8,128)(2,1)} %get-tuple-element.28.refs_4_.refs_0_.refs_2_, bf16[768,768]{1,0:T(8,128)(2,1)} %get-tuple-element.36.refs_1_.refs_3_.refs_0_, bf16[768,768]{1,0:T(8,128)(2,1)} %get-tuple-element.33.refs_2_, bf16[768,768]{1,0:T(8,128)(2,1)} %collective-permute-done.12.refs_2_.refs_3_, ...), custom_call_target="tpu_custom_call" | custom-call | bytes 13500000 | tf_op jit(solution)/shard_map/far_2_3/pallas_call | solution.py:320
  131.3 2.5 %collective-permute-done.18.refs_6_ = bf16[256,768]{1,0:T(8,128)(2,1)} collective-permute-done((bf16[256,768]{1,0:T(8,128)(2,1)S(1)}, bf16[256,768]{1,0:T(8,128)(2,1)}, u32[]{:S(2)}, u32[]{:S(2)}) %collective-permute-start.18) | collective-permute-done | bytes 393248 | tf_op jit(solution)/shard_map/near_1_direct/ppermute | solution.py:439
  133.8 1.4 collective-permute-start.19
  135.2 3.1 %add_convert_fusion.1 = bf16[2,768,768]{2,1,0:T(8,128)(2,1)S(1)} fusion(bf16[2,768,768]{2,1,0:T(8,128)(2,1)} %collective-permute-done.15, bf16[2,768,768]{2,1,0:T(8,128)(2,1)} %far_0_1.1.refs_8_), kind=kLoop, calls=%fused_computation.1 | loop fusion | flops 4718592 | bytes 7077888 | tf_op jit(solution)/shard_map/convert_element_type | solution.py:535
  138.3 2.7 %collective-permute-start.16 = (bf16[2,768,768]{2,1,0:T(8,128)(2,1)S(1)}, bf16[2,768,768]{2,1,0:T(8,128)(2,1)}, u32[]{:S(2)}, u32[]{:S(2)}) collective-permute-start(bf16[2,768,768]{2,1,0:T(8,128)(2,1)S(1)} %add_convert_fusion.1), channel_id=1, source_target_pairs={{2,0},{6,4},{11,9},{15,13},{16,18},{20,22},{25,27},{29,31}} | collective-permute-start | bytes 7077896 | tf_op jit(solution)/shard_map/far_0_1_beside/ppermute | solution.py:439
  141.1 3.6 %collective-permute-start.22 = (bf16[768,768]{1,0:T(8,128)(2,1)S(1)}, bf16[768,768]{1,0:T(8,128)(2,1)S(1)}, u32[]{:S(2)}, u32[]{:S(2)}) collective-permute-start(bf16[768,768]{1,0:T(8,128)(2,1)S(1)} %copy-done.5), channel_id=1, source_target_pairs={{2,16},{3,24},{6,20},{7,28},{10,17},{11,25},{14,21},{15,29},{16,2}... | collective-permute-start | bytes 3538952 | tf_op jit(solution)/shard_map/near_0_direct/ppermute | solution.py:439
  145.4 0.7 collective-permute-start.21
  146.2 1.8 collective-permute-start.20
  148.0 1.3 collective-permute-start.23
  149.9 45.5 %collective-permute-done.22.refs_5_ = bf16[768,768]{1,0:T(8,128)(2,1)S(1)} collective-permute-done((bf16[768,768]{1,0:T(8,128)(2,1)S(1)}, bf16[768,768]{1,0:T(8,128)(2,1)S(1)}, u32[]{:S(2)}, u32[]{:S(2)}) %collective-permute-start.22) | collective-permute-done | bytes 1179680 | tf_op jit(solution)/shard_map/near_0_direct/ppermute | solution.py:439
  195.5 1.1 copy-done.1
  196.7 1.0 copy-done.2
  197.8 7.3 %shard_map.65 = f32[768,1536]{1,0:T(8,128)} custom-call(s32[2]{0:T(128)} %pad_add_fusion.slot, f32[768,768]{1,0:T(8,128)} %get-tuple-element.39.refs_6_.refs_0_, f32[768,768]{1,0:T(8,128)} %get-tuple-element.38.refs_8_.refs_1_, bf16[2,768,768]{2,1,0:T(8,128)(2,1)} %collective-permute-done.16.refs_2_, bf16[1,768,768]{2,1,0:T(8,128)(2,1)} %collective-permute-done.20.refs_3_, ...), custom_call_target="tpu_custom_call" | custom-call | bytes 13500000 | tf_op jit(solution)/shard_map/pallas_call | solution.py:385
  (45 shorter events, 4.4 us)
Async XLA Ops:
  1.4 5.5 %collective-permute-start = (f32[8,8]{1,0:T(8,128)S(1)}, f32[8,8]{1,0:T(8,128)S(1)}, u32[]{:S(2)}, u32[]{:S(2)}) collective-permute-start(f32[8,8]{1,0:T(8,128)S(1)} %pad_maximum_fusion.1), channel_id=1, source_target_pairs={{0,16},{1,17},{2,18},{3,19},{4,20},{5,21},{6,22},{7,23},{8,24},{9,... | collective-permute-start | bytes 776 | tf_op jit(solution)/shard_map/ppermute | solution.py:469
  5.5 6.9 %copy-start.4 = (s32[2,5]{1,0:T(2,128)}, s32[2,5]{1,0:T(2,128)S(1)}, u32[]{:S(2)}) copy-start(s32[2,5]{1,0:T(2,128)S(1)} %add_multiply_fusion.corner) | copy-start | bytes 124
  7.6 4.8 %collective-permute-start.1 = (f32[8,16]{1,0:T(8,128)S(1)}, f32[8,16]{1,0:T(8,128)S(1)}, u32[]{:S(2)}, u32[]{:S(2)}) collective-permute-start(f32[8,16]{1,0:T(8,128)S(1)} %pad_maximum_fusion.2), channel_id=1, source_target_pairs={{0,8},{1,9},{2,10},{3,11},{4,12},{5,13},{6,14},{7,15},{8,0},{9,1},... | collective-permute-start | bytes 1544 | tf_op jit(solution)/shard_map/ppermute | solution.py:469
  12.5 3.6 %collective-permute-start.2 = (f32[8,32]{1,0:T(8,128)S(1)}, f32[8,32]{1,0:T(8,128)S(1)}, u32[]{:S(2)}, u32[]{:S(2)}) collective-permute-start(f32[8,32]{1,0:T(8,128)S(1)} %pad_maximum_fusion.3), channel_id=1, source_target_pairs={{0,4},{1,5},{2,6},{3,7},{4,0},{5,1},{6,2},{7,3},{8,12},{9,13},{10,... | collective-permute-start | bytes 3080 | tf_op jit(solution)/shard_map/ppermute | solution.py:469
  16.2 3.6 %collective-permute-start.3 = (f32[8,64]{1,0:T(8,128)S(1)}, f32[8,64]{1,0:T(8,128)S(1)}, u32[]{:S(2)}, u32[]{:S(2)}) collective-permute-start(f32[8,64]{1,0:T(8,128)S(1)} %pad_maximum_fusion.4), channel_id=1, source_target_pairs={{0,2},{1,3},{2,0},{3,1},{4,6},{5,7},{6,4},{7,5},{8,10},{9,11},{10,... | collective-permute-start | bytes 6152 | tf_op jit(solution)/shard_map/ppermute | solution.py:469
  16.7 26.0 %collective-permute-start.6 = (bf16[768,768]{1,0:T(8,128)(2,1)}, bf16[768,768]{1,0:T(8,128)(2,1)}, u32[]{:S(2)}, u32[]{:S(2)}) collective-permute-start(bf16[768,768]{1,0:T(8,128)(2,1)} %get-tuple-element.31.refs_0_.refs_2_), channel_id=1, source_target_pairs={{0,8},{1,9},{2,10},{3,11},{4,12},{5,13},{6,14},{7,15},{8,0},{9,1},... | collective-permute-start | bytes 3538952 | tf_op jit(solution)/shard_map/raw_a_across_rows_2/ppermute | solution.py:439
  17.1 27.7 %collective-permute-start.5 = (bf16[768,768]{1,0:T(8,128)(2,1)}, bf16[768,768]{1,0:T(8,128)(2,1)}, u32[]{:S(2)}, u32[]{:S(2)}) collective-permute-start(bf16[768,768]{1,0:T(8,128)(2,1)} %get-tuple-element.29.refs_1_), channel_id=1, source_target_pairs={{0,4},{1,5},{2,6},{3,7},{4,0},{5,1},{6,2},{7,3},{8,12},{9,13},{10,... | collective-permute-start | bytes 3538952 | tf_op jit(solution)/shard_map/raw_a_across_rows_1/ppermute | solution.py:439
  19.9 31.1 %collective-permute-start.7 = (bf16[768,768]{1,0:T(8,128)(2,1)}, bf16[768,768]{1,0:T(8,128)(2,1)}, u32[]{:S(2)}, u32[]{:S(2)}) collective-permute-start(bf16[768,768]{1,0:T(8,128)(2,1)} %get-tuple-element.31.refs_0_.refs_2_), channel_id=1, source_target_pairs={{0,2},{1,3},{4,6},{5,7},{8,10},{9,11},{12,14},{13,15},{18,16},{19,... | collective-permute-start | bytes 3538952 | tf_op jit(solution)/shard_map/raw_a_beside/ppermute | solution.py:439
  21.1 1.2 collective-permute-start.4
  35.9 36.3 %collective-permute-start.10 = (bf16[768,768]{1,0:T(8,128)(2,1)}, bf16[768,768]{1,0:T(8,128)(2,1)}, u32[]{:S(2)}, u32[]{:S(2)}) collective-permute-start(bf16[768,768]{1,0:T(8,128)(2,1)} %get-tuple-element.36.refs_1_.refs_3_.refs_0_), channel_id=1, source_target_pairs={{0,2},{1,3},{4,6},{5,7},{8,10},{9,11},{12,14},{13,15},{18,16},{19,... | collective-permute-start | bytes 3538952 | tf_op jit(solution)/shard_map/density_b_beside/ppermute | solution.py:439
  37.2 37.4 %collective-permute-start.11 = (bf16[768,768]{1,0:T(8,128)(2,1)}, bf16[768,768]{1,0:T(8,128)(2,1)}, u32[]{:S(2)}, u32[]{:S(2)}) collective-permute-start(bf16[768,768]{1,0:T(8,128)(2,1)} %get-tuple-element.28.refs_4_.refs_0_.refs_2_), channel_id=1, source_target_pairs={{0,4},{1,5},{2,6},{3,7},{4,0},{5,1},{6,2},{7,3},{8,12},{9,13},{10,... | collective-permute-start | bytes 3538952 | tf_op jit(solution)/shard_map/density_b_across_rows_1/ppermute | solution.py:439
  51.0 23.6 %collective-permute-start.12 = (bf16[768,768]{1,0:T(8,128)(2,1)}, bf16[768,768]{1,0:T(8,128)(2,1)}, u32[]{:S(2)}, u32[]{:S(2)}) collective-permute-start(bf16[768,768]{1,0:T(8,128)(2,1)} %get-tuple-element.36.refs_1_.refs_3_.refs_0_), channel_id=1, source_target_pairs={{0,8},{1,9},{2,10},{3,11},{4,12},{5,13},{6,14},{7,15},{8,0},{9,1},... | collective-permute-start | bytes 3538952 | tf_op jit(solution)/shard_map/density_b_across_rows_2/ppermute | solution.py:439
  61.6 31.8 %collective-permute-start.14 = (bf16[768,768]{1,0:T(8,128)(2,1)}, bf16[768,768]{1,0:T(8,128)(2,1)}, u32[]{:S(2)}, u32[]{:S(2)}) collective-permute-start(bf16[768,768]{1,0:T(8,128)(2,1)} %get-tuple-element.33.refs_2_), channel_id=1, source_target_pairs={{0,4},{1,5},{2,6},{3,7},{4,0},{5,1},{6,2},{7,3},{8,12},{9,13},{10,... | collective-permute-start | bytes 3538952 | tf_op jit(solution)/shard_map/forward_b_across_rows_1/ppermute | solution.py:439
  64.4 29.0 %collective-permute-start.9 = (bf16[768,768]{1,0:T(8,128)(2,1)}, bf16[768,768]{1,0:T(8,128)(2,1)}, u32[]{:S(2)}, u32[]{:S(2)}) collective-permute-start(bf16[768,768]{1,0:T(8,128)(2,1)} %get-tuple-element.34.refs_4_), channel_id=1, source_target_pairs={{0,1},{1,0},{2,3},{3,2},{4,5},{5,4},{6,7},{7,6},{8,9},{9,8},{10,11... | collective-permute-start | bytes 3538952 | tf_op jit(solution)/shard_map/wide_a_across_cores/ppermute | solution.py:439
  74.6 18.9 %collective-permute-start.13 = (bf16[768,768]{1,0:T(8,128)(2,1)}, bf16[768,768]{1,0:T(8,128)(2,1)}, u32[]{:S(2)}, u32[]{:S(2)}) collective-permute-start(bf16[768,768]{1,0:T(8,128)(2,1)} %broadcast_select_fusion.refs_6_), channel_id=1, source_target_pairs={{0,1},{1,0},{2,3},{3,2},{4,5},{5,4},{6,7},{7,6},{8,9},{9,8},{10,11... | collective-permute-start | bytes 3538952 | tf_op jit(solution)/shard_map/wide_b_across_cores/ppermute | solution.py:439
  74.6 40.7 %collective-permute-start.8 = (bf16[768,768]{1,0:T(8,128)(2,1)}, bf16[768,768]{1,0:T(8,128)(2,1)}, u32[]{:S(2)}, u32[]{:S(2)}) collective-permute-start(bf16[768,768]{1,0:T(8,128)(2,1)} %get-tuple-element.32.refs_4_.refs_6_.refs_1_), channel_id=1, source_target_pairs={{0,8},{1,9},{2,10},{3,11},{4,12},{5,13},{6,14},{7,15},{8,0},{9,1},... | collective-permute-start | bytes 3538952 | tf_op jit(solution)/shard_map/forward_a_across_rows_2/ppermute | solution.py:439
  83.9 51.3 %collective-permute-start.15 = (bf16[2,768,768]{2,1,0:T(8,128)(2,1)}, bf16[2,768,768]{2,1,0:T(8,128)(2,1)}, u32[]{:S(2)}, u32[]{:S(2)}) collective-permute-start(bf16[2,768,768]{2,1,0:T(8,128)(2,1)} %far_0_1.1.refs_8_), channel_id=1, source_target_pairs={{3,2},{7,6},{10,11},{14,15},{17,16},{21,20},{24,25},{28,29}} | collective-permute-start | bytes 7077896 | tf_op jit(solution)/shard_map/far_0_1_across_cores/ppermute | solution.py:439
  103.8 30.0 %collective-permute-start.17 = (bf16[512,768]{1,0:T(8,128)(2,1)}, bf16[512,768]{1,0:T(8,128)(2,1)}, u32[]{:S(2)}, u32[]{:S(2)}) collective-permute-start(bf16[512,768]{1,0:T(8,128)(2,1)} %slice.12), channel_id=1, source_target_pairs={{2,0},{3,1},{6,4},{7,5},{10,8},{11,9},{14,12},{15,13},{16,18},{17,... | collective-permute-start | bytes 2359304 | tf_op jit(solution)/shard_map/near_1_beside/ppermute | solution.py:439
  109.8 23.9 %collective-permute-start.18 = (bf16[256,768]{1,0:T(8,128)(2,1)S(1)}, bf16[256,768]{1,0:T(8,128)(2,1)}, u32[]{:S(2)}, u32[]{:S(2)}) collective-permute-start(bf16[256,768]{1,0:T(8,128)(2,1)S(1)} %slice.13), channel_id=1, source_target_pairs={{2,20},{3,28},{6,16},{7,24},{10,21},{11,29},{14,17},{15,25},{16,6}... | collective-permute-start | bytes 1179656 | tf_op jit(solution)/shard_map/near_1_direct/ppermute | solution.py:439
  131.3 9.8 %copy-start.5 = (bf16[768,768]{1,0:T(8,128)(2,1)S(1)}, bf16[768,768]{1,0:T(8,128)(2,1)}, u32[]{:S(2)}) copy-start(bf16[768,768]{1,0:T(8,128)(2,1)} %get-tuple-element.42) | copy-start | bytes 3538948
  133.8 10.9 %collective-permute-start.19 = (bf16[2,768,768]{2,1,0:T(8,128)(2,1)}, bf16[2,768,768]{2,1,0:T(8,128)(2,1)S(1)}, u32[]{:S(2)}, u32[]{:S(2)}) collective-permute-start(bf16[2,768,768]{2,1,0:T(8,128)(2,1)} %far_2_3.1), channel_id=1, source_target_pairs={{2,3},{6,7},{11,10},{15,14},{16,17},{20,21},{25,24},{29,28}} | collective-permute-start | bytes 7077896 | tf_op jit(solution)/shard_map/far_2_3_across_cores/ppermute | solution.py:439
  135.2 9.5 %copy-start = (bf16[2,768,768]{2,1,0:T(8,128)(2,1)S(1)}, bf16[2,768,768]{2,1,0:T(8,128)(2,1)}, u32[]{:S(2)}) copy-start(bf16[2,768,768]{2,1,0:T(8,128)(2,1)} %far_2_3.1) | copy-start | bytes 7077892
  138.3 57.1 %collective-permute-start.16 = (bf16[2,768,768]{2,1,0:T(8,128)(2,1)S(1)}, bf16[2,768,768]{2,1,0:T(8,128)(2,1)}, u32[]{:S(2)}, u32[]{:S(2)}) collective-permute-start(bf16[2,768,768]{2,1,0:T(8,128)(2,1)S(1)} %add_convert_fusion.1), channel_id=1, source_target_pairs={{2,0},{6,4},{11,9},{15,13},{16,18},{20,22},{25,27},{29,31}} | collective-permute-start | bytes 7077896 | tf_op jit(solution)/shard_map/far_0_1_beside/ppermute | solution.py:439
  141.1 54.4 %collective-permute-start.22 = (bf16[768,768]{1,0:T(8,128)(2,1)S(1)}, bf16[768,768]{1,0:T(8,128)(2,1)S(1)}, u32[]{:S(2)}, u32[]{:S(2)}) collective-permute-start(bf16[768,768]{1,0:T(8,128)(2,1)S(1)} %copy-done.5), channel_id=1, source_target_pairs={{2,16},{3,24},{6,20},{7,28},{10,17},{11,25},{14,21},{15,29},{16,2}... | collective-permute-start | bytes 3538952 | tf_op jit(solution)/shard_map/near_0_direct/ppermute | solution.py:439
  145.4 51.1 %collective-permute-start.21 = (bf16[1,768,768]{2,1,0:T(8,128)(2,1)S(1)}, bf16[1,768,768]{2,1,0:T(8,128)(2,1)S(1)}, u32[]{:S(2)}, u32[]{:S(2)}) collective-permute-start(bf16[1,768,768]{2,1,0:T(8,128)(2,1)S(1)} %get-tuple-element.43), channel_id=1, source_target_pairs={{3,1},{7,5},{10,8},{14,12},{17,19},{21,23},{24,26},{28,30}} | collective-permute-start | bytes 3538952 | tf_op jit(solution)/shard_map/far_2_3_beside_1/ppermute | solution.py:439
  146.2 51.6 %collective-permute-start.20 = (bf16[1,768,768]{2,1,0:T(8,128)(2,1)S(1)}, bf16[1,768,768]{2,1,0:T(8,128)(2,1)}, u32[]{:S(2)}, u32[]{:S(2)}) collective-permute-start(bf16[1,768,768]{2,1,0:T(8,128)(2,1)S(1)} %get-tuple-element.44), channel_id=1, source_target_pairs={{3,1},{7,5},{10,8},{14,12},{17,19},{21,23},{24,26},{28,30}} | collective-permute-start | bytes 3538952 | tf_op jit(solution)/shard_map/far_2_3_beside_0/ppermute | solution.py:439
  148.0 47.5 %collective-permute-start.23 = (bf16[512,768]{1,0:T(8,128)(2,1)}, bf16[512,768]{1,0:T(8,128)(2,1)S(1)}, u32[]{:S(2)}, u32[]{:S(2)}) collective-permute-start(bf16[512,768]{1,0:T(8,128)(2,1)} %collective-permute-done.17), channel_id=1, source_target_pairs={{0,20},{1,28},{4,16},{5,24},{8,21},{9,29},{12,17},{13,25},{18,6},{... | collective-permute-start | bytes 2359304 | tf_op jit(solution)/shard_map/near_1_ahead/ppermute | solution.py:439
  195.5 1.1 copy-start.1
  195.5 1.3 copy-start.3
  196.7 1.0 copy-start.2

commit v6 on v5

--- a/solution.py
+++ b/solution.py
@@ -242,8 +242,7 @@
     seed = refs.pop(0) if seeded else None
     refs = refs[unread:]
     total = refs.pop(0)
-    rounded = refs.pop(0) if last else None
-    tall_in, wide_in, sems = refs
+    *rounded, tall_in, wide_in, sems = refs
     waits = []
     for n in range(count):
         for s in range(sources):
@@ -265,8 +264,11 @@
         for copy in waits[n]:
             copy.wait()
         add_product(total, wide_in.at[n], tall_in.at[n], False, n == 0 and not seeded)
-    if last:
-        rounded[...] = total[...].astype(jnp.bfloat16)
+    at = 0
+    for piece in rounded:
+        rows = piece.shape[0]
+        piece[...] = total[at : at + rows, :].astype(jnp.bfloat16)
+        at += rows
 
 
 def near_share(source, tall, sides, wide, seed, last, sooner):
@@ -280,7 +282,7 @@
     operands += sooner
     shapes = [jax.ShapeDtypeStruct(cell, jnp.float32)]
     if last:
-        shapes.append(jax.ShapeDtypeStruct(cell, jnp.bfloat16))
+        shapes += [jax.ShapeDtypeStruct((rows, cell[1]), jnp.bfloat16) for rows in last]
     return pl.pallas_call(
         functools.partial(near_kernel, sides, sources, seed is not None, last, len(sooner)),
         out_shape=shapes,
@@ -502,15 +504,17 @@
 
     tall = {mask: [None, None] for mask in range(half_rows)}
     def near_part(q):
+        straight = CUTS[q] * side // 6
+        pieces = [rows for rows in (straight, side - straight) if rows]
         what = f"near_{q}"
         place = after((row_in // 2) ^ col_in, *waits(what + "_source"))
         source = jnp.stack([place ^ (m // 2) for m in range(half_rows)]).astype(jnp.int32)
         sides = tuple(m % 2 for m in range(half_rows))
         with jax.named_scope(what):
-            got = near_share(source, [tall[m][q] for m in tall], sides, wide, None, True, [*done[-1:], *waits(what)])
+            got = near_share(source, [tall[m][q] for m in tall], sides, wide, None, pieces, [*done[-1:], *waits(what)])
         done.append(got[0])
         made[what] = got[1]
-        return got
+        return got[0], got[1:]
 
     def far_product(masks):
         what = "far_" + "_".join(map(str, masks))
@@ -560,14 +564,14 @@
     def opposite(h, i, y, k, turn):
         return (1 - h, k * 2 + (i + turn) % 2, h, i // 2)
 
-    def exchange(value, turn, cut):
+    def exchange(pieces_out, turn, cut):
         across = lambda h, i, y, k: opposite(h, i, y, k, turn) if h != y else None
         onward = lambda h, i, y, k: opposite(h, i, 1 - y, k, turn) if h == y else None
         pieces = []
         if cut > 0:
-            pieces.append(send(value[:cut], across, f"near_{turn}_direct"))
+            pieces.append(send(pieces_out[0], across, f"near_{turn}_direct"))
         if cut < side:
-            ahead = to_beside(value[cut:], False, f"near_{turn}_beside")
+            ahead = to_beside(pieces_out[-1], False, f"near_{turn}_beside")
             pieces.append(send(ahead, onward, f"near_{turn}_ahead"))
         return pieces
 

time: 206 us -> 203 us (0.985)
  local copies, waits for them, and re-layouts: 9.52 us -> 6.43 us
    slice x2 -> x0, local copies, waits for them, and re-layouts: 3.1 us -> none  [the longest x1 2.08 us: exchange(): ahead = to_beside(value[cut:], False, f'near_{turn}_beside')]
  transfers between devices with their start and end apart: 24 -> 24, of which waited for: 10 -> 10; matrix products, arithmetic and copies ran while one was open for 8% -> 6% of each run, Pallas kernels for 27% -> 28%
where the time goes in v6:
time: 203 us; the launch traced here: 202 us
  waiting for transfers between devices  80.6 us (40%)
  Pallas kernels  63.6 us (31%)
  starting transfers between devices  38.3 us (19%)
  other arithmetic  11 us (5%)
  local copies, waits for them, and re-layouts  6.43 us (3%)
    ppermute x19, waiting for transfers between devices, send(): made[what] = lax.ppermute(after(value, *waits(what)), AXES, moves(where))  76.2 us
    ppermute x19, starting transfers between devices, send(): made[what] = lax.ppermute(after(value, *waits(what)), AXES, moves(where))  32 us
    pallas_call x2, Pallas kernels, densities(): pl.pallas_call(functools.partial(density_kernel, chunks, sources, len(soo...  21 us
    pallas_call x2, Pallas kernels, near_share(): pl.pallas_call(functools.partial(near_kernel, sides, sources, seed is not...  16.3 us
    pallas_call x2, Pallas kernels, far_share(): pl.pallas_call(functools.partial(far_kernel, count, len(sooner)), out_sha...  16.2 us
    pallas_call x1, Pallas kernels, final_sum(): pl.pallas_call(functools.partial(final_kernel, [len(share) for share in f...  7.35 us
    ppermute x5, starting transfers between devices, double(): arrived = lax.ppermute(value, AXES, [(d, d ^ bit) for d in range(devices)])  6.23 us
    ppermute x5, waiting for transfers between devices, double(): arrived = lax.ppermute(value, AXES, [(d, d ^ bit) for d in range(devices)])  4.43 us
  transfers between devices with their start and end apart: 24, of which 10 were waited for; matrix products, arithmetic and copies ran while one was open for 6% of the time, Pallas kernels for 28%

profile of v6, /device:TPU:4, one launch (start us, length us, event | category | flops | bytes accessed | tf_op | source)
XLA Modules:
  0.0 201.7 jit_solution(5827072406739556075)
XLA Ops:
  0.0 0.7 convert_element_type.27
  0.7 0.7 pad_maximum_fusion.1
  1.4 2.6 %collective-permute-start = (f32[8,8]{1,0:T(8,128)S(1)}, f32[8,8]{1,0:T(8,128)S(1)}, u32[]{:S(2)}, u32[]{:S(2)}) collective-permute-start(f32[8,8]{1,0:T(8,128)S(1)} %pad_maximum_fusion.1), channel_id=1, source_target_pairs={{0,16},{1,17},{2,18},{3,19},{4,20},{5,21},{6,22},{7,23},{8,24},{9,... | collective-permute-start | bytes 776 | tf_op jit(solution)/shard_map/ppermute | solution.py:471
  5.5 0.7 pad_maximum_fusion.6.scale
  6.9 0.8 pad_maximum_fusion.2
  7.6 1.6 collective-permute-start.1
  9.2 3.2 %constant_dynamic-slice_fusion = (bf16[768,768]{1,0:T(8,128)(2,1)}, bf16[768,768]{1,0:T(8,128)(2,1)}) fusion(bf16[768,1536]{1,0:T(8,128)(2,1)} %param.9, s32[]{:T(128)S(6)} %select_n.49, s32[]{:T(128)S(6)} %select_n.48), kind=kLoop, calls=%fused_computation.16 | loop fusion | bytes 4718600 | tf_op jit(solution)/shard_map/dynamic_slice | solution.py:450
  12.5 1.5 collective-permute-start.2
  14.0 2.1 %collective-permute-done.2 = f32[8,32]{1,0:T(8,128)S(1)} collective-permute-done((f32[8,32]{1,0:T(8,128)S(1)}, f32[8,32]{1,0:T(8,128)S(1)}, u32[]{:S(2)}, u32[]{:S(2)}) %collective-permute-start.2) | collective-permute-done | bytes 1056 | tf_op jit(solution)/shard_map/ppermute | solution.py:471
  17.1 1.5 collective-permute-start.5
  18.6 1.2 collective-permute-done.3
  19.9 1.3 collective-permute-start.7
  21.2 1.2 collective-permute-done.4
  22.4 0.7 pad_maximum_fusion.edges
  23.1 2.8 %shard_map.64 = (bf16[256,144]{1,0:T(8,128)(2,1)}, s32[1,5,128]{2,1,0:T(8,128)}) custom-call(f32[8,256]{1,0:T(8,128)} %pad_maximum_fusion.edges, f32[8,128]{1,0:T(8,128)} %pad.5.corner), custom_call_target="tpu_custom_call" | custom-call | bytes 4500000 | tf_op jit(solution)/shard_map/pallas_call | solution.py:96
  25.9 10.1 %density_0.1 = (bf16[768,768]{1,0:T(8,128)(2,1)}, bf16[768,768]{1,0:T(8,128)(2,1)}) custom-call(s32[1,5,128]{2,1,0:T(8,128)} %get-tuple-element.27.hits, f32[3]{0:T(128)} %pad_maximum_fusion.6.scale, s32[2,5]{1,0:T(2,128)} %copy-done.5, bf16[256,144]{1,0:T(8,128)(2,1)} %get-tuple-element.28.coefficient, bf16[144,16384]{1,0:T(8,128)(2,1)} %weight.3, ...), custom_call_target="tpu_custom_call" | custom-call | bytes 16500000 | tf_op jit(solution)/shard_map/density_0/pallas_call | solution.py:208
  35.9 1.3 collective-permute-start.10
  37.2 2.2 %collective-permute-start.11 = (bf16[768,768]{1,0:T(8,128)(2,1)}, bf16[768,768]{1,0:T(8,128)(2,1)}, u32[]{:S(2)}, u32[]{:S(2)}) collective-permute-start(bf16[768,768]{1,0:T(8,128)(2,1)} %get-tuple-element.29.refs_4_.refs_0_.refs_2_), channel_id=1, source_target_pairs={{0,4},{1,5},{2,6},{3,7},{4,0},{5,1},{6,2},{7,3},{8,12},{9,13},{10,... | collective-permute-start | bytes 3538952 | tf_op jit(solution)/shard_map/density_b_across_rows_1/ppermute | solution.py:441
  39.5 3.3 %collective-permute-done.6.refs_1_ = bf16[768,768]{1,0:T(8,128)(2,1)} collective-permute-done((bf16[768,768]{1,0:T(8,128)(2,1)}, bf16[768,768]{1,0:T(8,128)(2,1)}, u32[]{:S(2)}, u32[]{:S(2)}) %collective-permute-start.6) | collective-permute-done | bytes 1179680 | tf_op jit(solution)/shard_map/raw_a_across_rows_2/ppermute | solution.py:441
  42.7 2.7 %collective-permute-done.5.refs_0_ = bf16[768,768]{1,0:T(8,128)(2,1)} collective-permute-done((bf16[768,768]{1,0:T(8,128)(2,1)}, bf16[768,768]{1,0:T(8,128)(2,1)}, u32[]{:S(2)}, u32[]{:S(2)}) %collective-permute-start.5) | collective-permute-done | bytes 1179680 | tf_op jit(solution)/shard_map/raw_a_across_rows_1/ppermute | solution.py:441
  45.4 5.6 %collective-permute-done.7.refs_3_ = bf16[768,768]{1,0:T(8,128)(2,1)} collective-permute-done((bf16[768,768]{1,0:T(8,128)(2,1)}, bf16[768,768]{1,0:T(8,128)(2,1)}, u32[]{:S(2)}, u32[]{:S(2)}) %collective-permute-start.7) | collective-permute-done | bytes 1179680 | tf_op jit(solution)/shard_map/raw_a_beside/ppermute | solution.py:441
  51.4 11.0 %density_2.1 = (bf16[768,768]{1,0:T(8,128)(2,1)}, bf16[768,768]{1,0:T(8,128)(2,1)}, bf16[768,768]{1,0:T(8,128)(2,1)}) custom-call(s32[1,5,128]{2,1,0:T(8,128)} %get-tuple-element.27.hits, f32[3]{0:T(128)} %pad_maximum_fusion.6.scale, s32[2,5]{1,0:T(2,128)} %copy-done.5, bf16[256,144]{1,0:T(8,128)(2,1)} %get-tuple-element.28.coefficient, ...), custom_call_target="tpu_custom_call" | custom-call | bytes 20250000 | tf_op jit(solution)/shard_map/density_2/pallas_call | solution.py:208
  62.4 1.5 collective-permute-start.14
  63.9 8.2 %collective-permute-done.10 = bf16[768,768]{1,0:T(8,128)(2,1)} collective-permute-done((bf16[768,768]{1,0:T(8,128)(2,1)}, bf16[768,768]{1,0:T(8,128)(2,1)}, u32[]{:S(2)}, u32[]{:S(2)}) %collective-permute-start.10) | collective-permute-done | bytes 1179680 | tf_op jit(solution)/shard_map/density_b_beside/ppermute | solution.py:441
  72.2 2.4 %broadcast_select_fusion.refs_6_ = bf16[768,768]{1,0:T(8,128)(2,1)} fusion(bf16[768,768]{1,0:T(8,128)(2,1)} %get-tuple-element.37.refs_1_.refs_3_.refs_0_, bf16[768,768]{1,0:T(8,128)(2,1)} %collective-permute-done.10, pred[]{:T(512)S(6)} %eq.8), kind=kLoop, calls=%fused_computation.2 | loop fusion | flops 589824 | bytes 3538945 | tf_op jit(solution)/shard_map/jit(_where)/select_n | solution.py:553
  74.6 0.8 collective-permute-start.8
  75.4 8.4 %far_0_1.1.refs_8_ = bf16[2,768,768]{2,1,0:T(8,128)(2,1)} custom-call(bf16[768,768]{1,0:T(8,128)(2,1)} %get-tuple-element.29.refs_4_.refs_0_.refs_2_, bf16[768,768]{1,0:T(8,128)(2,1)} %get-tuple-element.37.refs_1_.refs_3_.refs_0_, bf16[768,768]{1,0:T(8,128)(2,1)} %get-tuple-element.29.refs_4_.refs_0_.refs_2_, ...), custom_call_target="tpu_custom_call" | custom-call | bytes 13500000 | tf_op jit(solution)/shard_map/far_0_1/pallas_call | solution.py:322
  83.9 1.3 collective-permute-start.15
  85.2 0.6 pad_add_fusion.1.source
  85.8 7.7 %collective-permute-done.14.refs_3_.refs_5_ = bf16[768,768]{1,0:T(8,128)(2,1)} collective-permute-done((bf16[768,768]{1,0:T(8,128)(2,1)}, bf16[768,768]{1,0:T(8,128)(2,1)}, u32[]{:S(2)}, u32[]{:S(2)}) %collective-permute-start.14) | collective-permute-done | bytes 1179680 | tf_op jit(solution)/shard_map/forward_b_across_rows_1/ppermute | solution.py:441
  93.5 8.1 %near_1.1 = (f32[768,768]{1,0:T(8,128)}, bf16[256,768]{1,0:T(8,128)(2,1)}, bf16[512,768]{1,0:T(8,128)(2,1)}) custom-call(s32[4]{0:T(128)} %pad_add_fusion.1.source, bf16[768,768]{1,0:T(8,128)(2,1)} %get-tuple-element.37.refs_1_.refs_3_.refs_0_, bf16[768,768]{1,0:T(8,128)(2,1)} %collective-permute-done.11.refs_5_.refs_1_, ...), custom_call_target="tpu_custom_call" | custom-call | bytes 18000000 | tf_op jit(solution)/shard_map/near_1/pallas_call | solution.py:286
  101.5 5.2 %collective-permute-start.17 = (bf16[512,768]{1,0:T(8,128)(2,1)}, bf16[512,768]{1,0:T(8,128)(2,1)}, u32[]{:S(2)}, u32[]{:S(2)}) collective-permute-start(bf16[512,768]{1,0:T(8,128)(2,1)} %get-tuple-element.41), channel_id=1, source_target_pairs={{2,0},{3,1},{6,4},{7,5},{10,8},{11,9},{14,12},{15,13},{16,18},{17,... | collective-permute-start | bytes 2359304 | tf_op jit(solution)/shard_map/near_1_beside/ppermute | solution.py:441
  106.7 4.9 %collective-permute-start.18 = (bf16[256,768]{1,0:T(8,128)(2,1)}, bf16[256,768]{1,0:T(8,128)(2,1)S(1)}, u32[]{:S(2)}, u32[]{:S(2)}) collective-permute-start(bf16[256,768]{1,0:T(8,128)(2,1)} %get-tuple-element.42), channel_id=1, source_target_pairs={{2,20},{3,28},{6,16},{7,24},{10,21},{11,29},{14,17},{15,25},{16,6}... | collective-permute-start | bytes 1179656 | tf_op jit(solution)/shard_map/near_1_direct/ppermute | solution.py:441
  111.6 8.2 %near_0.1 = (f32[768,768]{1,0:T(8,128)}, bf16[768,768]{1,0:T(8,128)(2,1)}) custom-call(s32[4]{0:T(128)} %pad_add_fusion.1.source, bf16[768,768]{1,0:T(8,128)(2,1)} %get-tuple-element.29.refs_4_.refs_0_.refs_2_, bf16[768,768]{1,0:T(8,128)(2,1)} %get-tuple-element.33.refs_4_.refs_6_.refs_1_, bf16[768,768]{1,0:T(8,128)(2,1)} %get-tuple-element.34.refs_2_, ...), custom_call_target="tpu_custom_call" | custom-call | bytes 18000000 | tf_op jit(solution)/shard_map/near_0/pallas_call | solution.py:286
  119.9 7.7 %far_2_3.1 = bf16[2,768,768]{2,1,0:T(8,128)(2,1)} custom-call(bf16[768,768]{1,0:T(8,128)(2,1)} %get-tuple-element.29.refs_4_.refs_0_.refs_2_, bf16[768,768]{1,0:T(8,128)(2,1)} %get-tuple-element.37.refs_1_.refs_3_.refs_0_, bf16[768,768]{1,0:T(8,128)(2,1)} %get-tuple-element.34.refs_2_, bf16[768,768]{1,0:T(8,128)(2,1)} %collective-permute-done.12.refs_2_.refs_3_, ...), custom_call_target="tpu_custom_call" | custom-call | bytes 13500000 | tf_op jit(solution)/shard_map/far_2_3/pallas_call | solution.py:322
  127.6 2.8 %collective-permute-done.18.refs_6_ = bf16[256,768]{1,0:T(8,128)(2,1)S(1)} collective-permute-done((bf16[256,768]{1,0:T(8,128)(2,1)}, bf16[256,768]{1,0:T(8,128)(2,1)S(1)}, u32[]{:S(2)}, u32[]{:S(2)}) %collective-permute-start.18) | collective-permute-done | bytes 393248 | tf_op jit(solution)/shard_map/near_1_direct/ppermute | solution.py:441
  130.4 1.4 collective-permute-start.19
  131.9 3.1 %add_convert_fusion.1 = bf16[2,768,768]{2,1,0:T(8,128)(2,1)S(1)} fusion(bf16[2,768,768]{2,1,0:T(8,128)(2,1)} %collective-permute-done.15, bf16[2,768,768]{2,1,0:T(8,128)(2,1)} %far_0_1.1.refs_8_), kind=kLoop, calls=%fused_computation.1 | loop fusion | flops 4718592 | bytes 7077888 | tf_op jit(solution)/shard_map/convert_element_type | solution.py:539
  135.0 2.8 %collective-permute-start.16 = (bf16[2,768,768]{2,1,0:T(8,128)(2,1)S(1)}, bf16[2,768,768]{2,1,0:T(8,128)(2,1)}, u32[]{:S(2)}, u32[]{:S(2)}) collective-permute-start(bf16[2,768,768]{2,1,0:T(8,128)(2,1)S(1)} %add_convert_fusion.1), channel_id=1, source_target_pairs={{2,0},{6,4},{11,9},{15,13},{16,18},{20,22},{25,27},{29,31}} | collective-permute-start | bytes 7077896 | tf_op jit(solution)/shard_map/far_0_1_beside/ppermute | solution.py:441
  137.7 3.1 %collective-permute-start.22 = (bf16[768,768]{1,0:T(8,128)(2,1)S(1)}, bf16[768,768]{1,0:T(8,128)(2,1)S(1)}, u32[]{:S(2)}, u32[]{:S(2)}) collective-permute-start(bf16[768,768]{1,0:T(8,128)(2,1)S(1)} %copy-done.6), channel_id=1, source_target_pairs={{2,16},{3,24},{6,20},{7,28},{10,17},{11,25},{14,21},{15,29},{16,2}... | collective-permute-start | bytes 3538952 | tf_op jit(solution)/shard_map/near_0_direct/ppermute | solution.py:441
  141.6 0.7 collective-permute-start.21
  142.3 1.8 collective-permute-start.20
  144.1 1.3 collective-permute-start.23
  145.4 0.6 pad_add_fusion.slot
  146.0 45.9 %collective-permute-done.22.refs_5_ = bf16[768,768]{1,0:T(8,128)(2,1)S(1)} collective-permute-done((bf16[768,768]{1,0:T(8,128)(2,1)S(1)}, bf16[768,768]{1,0:T(8,128)(2,1)S(1)}, u32[]{:S(2)}, u32[]{:S(2)}) %collective-permute-start.22) | collective-permute-done | bytes 1179680 | tf_op jit(solution)/shard_map/near_0_direct/ppermute | solution.py:441
  191.9 1.1 copy-done.1
  193.2 1.0 copy-done.2
  194.2 7.3 %shard_map.65 = f32[768,1536]{1,0:T(8,128)} custom-call(s32[2]{0:T(128)} %pad_add_fusion.slot, f32[768,768]{1,0:T(8,128)} %get-tuple-element.40.refs_6_.refs_0_, f32[768,768]{1,0:T(8,128)} %get-tuple-element.39.refs_8_.refs_1_, bf16[2,768,768]{2,1,0:T(8,128)(2,1)} %collective-permute-done.16.refs_2_, bf16[1,768,768]{2,1,0:T(8,128)(2,1)} %collective-permute-done.20.refs_3_, ...), custom_call_target="tpu_custom_call" | custom-call | bytes 13500000 | tf_op jit(solution)/shard_map/pallas_call | solution.py:387
  (45 shorter events, 3.5 us)
Async XLA Ops:
  1.4 5.5 %collective-permute-start = (f32[8,8]{1,0:T(8,128)S(1)}, f32[8,8]{1,0:T(8,128)S(1)}, u32[]{:S(2)}, u32[]{:S(2)}) collective-permute-start(f32[8,8]{1,0:T(8,128)S(1)} %pad_maximum_fusion.1), channel_id=1, source_target_pairs={{0,16},{1,17},{2,18},{3,19},{4,20},{5,21},{6,22},{7,23},{8,24},{9,... | collective-permute-start | bytes 776 | tf_op jit(solution)/shard_map/ppermute | solution.py:471
  5.5 6.9 %copy-start.5 = (s32[2,5]{1,0:T(2,128)}, s32[2,5]{1,0:T(2,128)S(1)}, u32[]{:S(2)}) copy-start(s32[2,5]{1,0:T(2,128)S(1)} %add_multiply_fusion.corner) | copy-start | bytes 124
  7.6 4.8 %collective-permute-start.1 = (f32[8,16]{1,0:T(8,128)S(1)}, f32[8,16]{1,0:T(8,128)S(1)}, u32[]{:S(2)}, u32[]{:S(2)}) collective-permute-start(f32[8,16]{1,0:T(8,128)S(1)} %pad_maximum_fusion.2), channel_id=1, source_target_pairs={{0,8},{1,9},{2,10},{3,11},{4,12},{5,13},{6,14},{7,15},{8,0},{9,1},... | collective-permute-start | bytes 1544 | tf_op jit(solution)/shard_map/ppermute | solution.py:471
  12.5 3.6 %collective-permute-start.2 = (f32[8,32]{1,0:T(8,128)S(1)}, f32[8,32]{1,0:T(8,128)S(1)}, u32[]{:S(2)}, u32[]{:S(2)}) collective-permute-start(f32[8,32]{1,0:T(8,128)S(1)} %pad_maximum_fusion.3), channel_id=1, source_target_pairs={{0,4},{1,5},{2,6},{3,7},{4,0},{5,1},{6,2},{7,3},{8,12},{9,13},{10,... | collective-permute-start | bytes 3080 | tf_op jit(solution)/shard_map/ppermute | solution.py:471
  16.2 3.6 %collective-permute-start.3 = (f32[8,64]{1,0:T(8,128)S(1)}, f32[8,64]{1,0:T(8,128)S(1)}, u32[]{:S(2)}, u32[]{:S(2)}) collective-permute-start(f32[8,64]{1,0:T(8,128)S(1)} %pad_maximum_fusion.4), channel_id=1, source_target_pairs={{0,2},{1,3},{2,0},{3,1},{4,6},{5,7},{6,4},{7,5},{8,10},{9,11},{10,... | collective-permute-start | bytes 6152 | tf_op jit(solution)/shard_map/ppermute | solution.py:471
  16.7 26.0 %collective-permute-start.6 = (bf16[768,768]{1,0:T(8,128)(2,1)}, bf16[768,768]{1,0:T(8,128)(2,1)}, u32[]{:S(2)}, u32[]{:S(2)}) collective-permute-start(bf16[768,768]{1,0:T(8,128)(2,1)} %get-tuple-element.32.refs_0_.refs_2_), channel_id=1, source_target_pairs={{0,8},{1,9},{2,10},{3,11},{4,12},{5,13},{6,14},{7,15},{8,0},{9,1},... | collective-permute-start | bytes 3538952 | tf_op jit(solution)/shard_map/raw_a_across_rows_2/ppermute | solution.py:441
  17.1 28.3 %collective-permute-start.5 = (bf16[768,768]{1,0:T(8,128)(2,1)}, bf16[768,768]{1,0:T(8,128)(2,1)}, u32[]{:S(2)}, u32[]{:S(2)}) collective-permute-start(bf16[768,768]{1,0:T(8,128)(2,1)} %get-tuple-element.30.refs_1_), channel_id=1, source_target_pairs={{0,4},{1,5},{2,6},{3,7},{4,0},{5,1},{6,2},{7,3},{8,12},{9,13},{10,... | collective-permute-start | bytes 3538952 | tf_op jit(solution)/shard_map/raw_a_across_rows_1/ppermute | solution.py:441
  19.9 31.1 %collective-permute-start.7 = (bf16[768,768]{1,0:T(8,128)(2,1)}, bf16[768,768]{1,0:T(8,128)(2,1)}, u32[]{:S(2)}, u32[]{:S(2)}) collective-permute-start(bf16[768,768]{1,0:T(8,128)(2,1)} %get-tuple-element.32.refs_0_.refs_2_), channel_id=1, source_target_pairs={{0,2},{1,3},{4,6},{5,7},{8,10},{9,11},{12,14},{13,15},{18,16},{19,... | collective-permute-start | bytes 3538952 | tf_op jit(solution)/shard_map/raw_a_beside/ppermute | solution.py:441
  21.2 1.2 collective-permute-start.4
  35.9 36.3 %collective-permute-start.10 = (bf16[768,768]{1,0:T(8,128)(2,1)}, bf16[768,768]{1,0:T(8,128)(2,1)}, u32[]{:S(2)}, u32[]{:S(2)}) collective-permute-start(bf16[768,768]{1,0:T(8,128)(2,1)} %get-tuple-element.37.refs_1_.refs_3_.refs_0_), channel_id=1, source_target_pairs={{0,2},{1,3},{4,6},{5,7},{8,10},{9,11},{12,14},{13,15},{18,16},{19,... | collective-permute-start | bytes 3538952 | tf_op jit(solution)/shard_map/density_b_beside/ppermute | solution.py:441
  37.2 37.4 %collective-permute-start.11 = (bf16[768,768]{1,0:T(8,128)(2,1)}, bf16[768,768]{1,0:T(8,128)(2,1)}, u32[]{:S(2)}, u32[]{:S(2)}) collective-permute-start(bf16[768,768]{1,0:T(8,128)(2,1)} %get-tuple-element.29.refs_4_.refs_0_.refs_2_), channel_id=1, source_target_pairs={{0,4},{1,5},{2,6},{3,7},{4,0},{5,1},{6,2},{7,3},{8,12},{9,13},{10,... | collective-permute-start | bytes 3538952 | tf_op jit(solution)/shard_map/density_b_across_rows_1/ppermute | solution.py:441
  51.0 23.6 %collective-permute-start.12 = (bf16[768,768]{1,0:T(8,128)(2,1)}, bf16[768,768]{1,0:T(8,128)(2,1)}, u32[]{:S(2)}, u32[]{:S(2)}) collective-permute-start(bf16[768,768]{1,0:T(8,128)(2,1)} %get-tuple-element.37.refs_1_.refs_3_.refs_0_), channel_id=1, source_target_pairs={{0,8},{1,9},{2,10},{3,11},{4,12},{5,13},{6,14},{7,15},{8,0},{9,1},... | collective-permute-start | bytes 3538952 | tf_op jit(solution)/shard_map/density_b_across_rows_2/ppermute | solution.py:441
  62.4 31.1 %collective-permute-start.14 = (bf16[768,768]{1,0:T(8,128)(2,1)}, bf16[768,768]{1,0:T(8,128)(2,1)}, u32[]{:S(2)}, u32[]{:S(2)}) collective-permute-start(bf16[768,768]{1,0:T(8,128)(2,1)} %get-tuple-element.34.refs_2_), channel_id=1, source_target_pairs={{0,4},{1,5},{2,6},{3,7},{4,0},{5,1},{6,2},{7,3},{8,12},{9,13},{10,... | collective-permute-start | bytes 3538952 | tf_op jit(solution)/shard_map/forward_b_across_rows_1/ppermute | solution.py:441
  63.9 29.5 %collective-permute-start.9 = (bf16[768,768]{1,0:T(8,128)(2,1)}, bf16[768,768]{1,0:T(8,128)(2,1)}, u32[]{:S(2)}, u32[]{:S(2)}) collective-permute-start(bf16[768,768]{1,0:T(8,128)(2,1)} %get-tuple-element.35.refs_4_), channel_id=1, source_target_pairs={{0,1},{1,0},{2,3},{3,2},{4,5},{5,4},{6,7},{7,6},{8,9},{9,8},{10,11... | collective-permute-start | bytes 3538952 | tf_op jit(solution)/shard_map/wide_a_across_cores/ppermute | solution.py:441
  74.6 18.9 %collective-permute-start.13 = (bf16[768,768]{1,0:T(8,128)(2,1)}, bf16[768,768]{1,0:T(8,128)(2,1)}, u32[]{:S(2)}, u32[]{:S(2)}) collective-permute-start(bf16[768,768]{1,0:T(8,128)(2,1)} %broadcast_select_fusion.refs_6_), channel_id=1, source_target_pairs={{0,1},{1,0},{2,3},{3,2},{4,5},{5,4},{6,7},{7,6},{8,9},{9,8},{10,11... | collective-permute-start | bytes 3538952 | tf_op jit(solution)/shard_map/wide_b_across_cores/ppermute | solution.py:441
  74.6 37.0 %collective-permute-start.8 = (bf16[768,768]{1,0:T(8,128)(2,1)}, bf16[768,768]{1,0:T(8,128)(2,1)}, u32[]{:S(2)}, u32[]{:S(2)}) collective-permute-start(bf16[768,768]{1,0:T(8,128)(2,1)} %get-tuple-element.33.refs_4_.refs_6_.refs_1_), channel_id=1, source_target_pairs={{0,8},{1,9},{2,10},{3,11},{4,12},{5,13},{6,14},{7,15},{8,0},{9,1},... | collective-permute-start | bytes 3538952 | tf_op jit(solution)/shard_map/forward_a_across_rows_2/ppermute | solution.py:441
  83.9 48.0 %collective-permute-start.15 = (bf16[2,768,768]{2,1,0:T(8,128)(2,1)}, bf16[2,768,768]{2,1,0:T(8,128)(2,1)}, u32[]{:S(2)}, u32[]{:S(2)}) collective-permute-start(bf16[2,768,768]{2,1,0:T(8,128)(2,1)} %far_0_1.1.refs_8_), channel_id=1, source_target_pairs={{3,2},{7,6},{10,11},{14,15},{17,16},{21,20},{24,25},{28,29}} | collective-permute-start | bytes 7077896 | tf_op jit(solution)/shard_map/far_0_1_across_cores/ppermute | solution.py:441
  101.5 28.9 %collective-permute-start.17 = (bf16[512,768]{1,0:T(8,128)(2,1)}, bf16[512,768]{1,0:T(8,128)(2,1)}, u32[]{:S(2)}, u32[]{:S(2)}) collective-permute-start(bf16[512,768]{1,0:T(8,128)(2,1)} %get-tuple-element.41), channel_id=1, source_target_pairs={{2,0},{3,1},{6,4},{7,5},{10,8},{11,9},{14,12},{15,13},{16,18},{17,... | collective-permute-start | bytes 2359304 | tf_op jit(solution)/shard_map/near_1_beside/ppermute | solution.py:441
  106.7 23.7 %collective-permute-start.18 = (bf16[256,768]{1,0:T(8,128)(2,1)}, bf16[256,768]{1,0:T(8,128)(2,1)S(1)}, u32[]{:S(2)}, u32[]{:S(2)}) collective-permute-start(bf16[256,768]{1,0:T(8,128)(2,1)} %get-tuple-element.42), channel_id=1, source_target_pairs={{2,20},{3,28},{6,16},{7,24},{10,21},{11,29},{14,17},{15,25},{16,6}... | collective-permute-start | bytes 1179656 | tf_op jit(solution)/shard_map/near_1_direct/ppermute | solution.py:441
  127.6 10.1 %copy-start.6 = (bf16[768,768]{1,0:T(8,128)(2,1)S(1)}, bf16[768,768]{1,0:T(8,128)(2,1)}, u32[]{:S(2)}) copy-start(bf16[768,768]{1,0:T(8,128)(2,1)} %get-tuple-element.44) | copy-start | bytes 3538948
  130.4 4.5 %copy-start.4 = (bf16[256,768]{1,0:T(8,128)(2,1)}, bf16[256,768]{1,0:T(8,128)(2,1)S(1)}, u32[]{:S(2)}) copy-start(bf16[256,768]{1,0:T(8,128)(2,1)S(1)} %collective-permute-done.18.refs_6_) | copy-start | bytes 1179652
  130.4 10.4 %collective-permute-start.19 = (bf16[2,768,768]{2,1,0:T(8,128)(2,1)}, bf16[2,768,768]{2,1,0:T(8,128)(2,1)S(1)}, u32[]{:S(2)}, u32[]{:S(2)}) collective-permute-start(bf16[2,768,768]{2,1,0:T(8,128)(2,1)} %far_2_3.1), channel_id=1, source_target_pairs={{2,3},{6,7},{11,10},{15,14},{16,17},{20,21},{25,24},{29,28}} | collective-permute-start | bytes 7077896 | tf_op jit(solution)/shard_map/far_2_3_across_cores/ppermute | solution.py:441
  131.9 9.0 %copy-start = (bf16[2,768,768]{2,1,0:T(8,128)(2,1)S(1)}, bf16[2,768,768]{2,1,0:T(8,128)(2,1)}, u32[]{:S(2)}) copy-start(bf16[2,768,768]{2,1,0:T(8,128)(2,1)} %far_2_3.1) | copy-start | bytes 7077892
  135.0 56.9 %collective-permute-start.16 = (bf16[2,768,768]{2,1,0:T(8,128)(2,1)S(1)}, bf16[2,768,768]{2,1,0:T(8,128)(2,1)}, u32[]{:S(2)}, u32[]{:S(2)}) collective-permute-start(bf16[2,768,768]{2,1,0:T(8,128)(2,1)S(1)} %add_convert_fusion.1), channel_id=1, source_target_pairs={{2,0},{6,4},{11,9},{15,13},{16,18},{20,22},{25,27},{29,31}} | collective-permute-start | bytes 7077896 | tf_op jit(solution)/shard_map/far_0_1_beside/ppermute | solution.py:441
  137.7 54.2 %collective-permute-start.22 = (bf16[768,768]{1,0:T(8,128)(2,1)S(1)}, bf16[768,768]{1,0:T(8,128)(2,1)S(1)}, u32[]{:S(2)}, u32[]{:S(2)}) collective-permute-start(bf16[768,768]{1,0:T(8,128)(2,1)S(1)} %copy-done.6), channel_id=1, source_target_pairs={{2,16},{3,24},{6,20},{7,28},{10,17},{11,25},{14,21},{15,29},{16,2}... | collective-permute-start | bytes 3538952 | tf_op jit(solution)/shard_map/near_0_direct/ppermute | solution.py:441
  141.6 51.4 %collective-permute-start.21 = (bf16[1,768,768]{2,1,0:T(8,128)(2,1)S(1)}, bf16[1,768,768]{2,1,0:T(8,128)(2,1)S(1)}, u32[]{:S(2)}, u32[]{:S(2)}) collective-permute-start(bf16[1,768,768]{2,1,0:T(8,128)(2,1)S(1)} %get-tuple-element.45), channel_id=1, source_target_pairs={{3,1},{7,5},{10,8},{14,12},{17,19},{21,23},{24,26},{28,30}} | collective-permute-start | bytes 3538952 | tf_op jit(solution)/shard_map/far_2_3_beside_1/ppermute | solution.py:441
  142.3 51.9 %collective-permute-start.20 = (bf16[1,768,768]{2,1,0:T(8,128)(2,1)S(1)}, bf16[1,768,768]{2,1,0:T(8,128)(2,1)}, u32[]{:S(2)}, u32[]{:S(2)}) collective-permute-start(bf16[1,768,768]{2,1,0:T(8,128)(2,1)S(1)} %get-tuple-element.46), channel_id=1, source_target_pairs={{3,1},{7,5},{10,8},{14,12},{17,19},{21,23},{24,26},{28,30}} | collective-permute-start | bytes 3538952 | tf_op jit(solution)/shard_map/far_2_3_beside_0/ppermute | solution.py:441
  144.1 47.8 %collective-permute-start.23 = (bf16[512,768]{1,0:T(8,128)(2,1)}, bf16[512,768]{1,0:T(8,128)(2,1)S(1)}, u32[]{:S(2)}, u32[]{:S(2)}) collective-permute-start(bf16[512,768]{1,0:T(8,128)(2,1)} %collective-permute-done.17), channel_id=1, source_target_pairs={{0,20},{1,28},{4,16},{5,24},{8,21},{9,29},{12,17},{13,25},{18,6},{... | collective-permute-start | bytes 2359304 | tf_op jit(solution)/shard_map/near_1_ahead/ppermute | solution.py:441
  191.9 1.1 copy-start.1
  191.9 1.3 copy-start.3
  193.2 1.0 copy-start.2
